TPU v7x, 32 devices: a whole 2x2x4 slice. The times are simulated.
32 devices in a mesh: depth: 4 (over y, core), slab: 8 (over z, x).
Axes of the slice: x: 2, y: 2, z: 4, core: 2. Of those that a mesh axis runs over, the one named last changes fastest.
Arguments:
- slabs: float32 [4, 8, 4, 256, 256], P('depth', 'slab'), as said below
- incident: float32 [4, 2048, 256], P('depth', 'slab'), may hold values from -6 to 6
Outputs:
- down_field: float32 [4, 2048, 256], P('depth', 'slab')
- reflected: float32 [4, 2048, 256], P('depth', 'slab')
Inputs may be any that keep to these rules, and one draw needn't show every extreme that they name: Reflection blocks have spectral norm below one half; transmission blocks have spectral norm below 2, and every star product of consecutive slabs within a group has reflection blocks of norm below one.
All inputs are finite; a program needn't handle non-finite values.
Results may differ from a plain program's by a relative error of at most 0.0003.
Values sent between devices are 32-bit elements; how exact they have to be, the bound alone decides.
No kernel may reach another device: no remote copies, remote signals or barrier semaphores. Data moves between devices by JAX's collectives and lax.ppermute only.
A program may use at most 64 MiB of HBM per device.

v0:
```python
import functools

import jax
import jax.numpy as jnp
from jax import lax
from jax.experimental import pallas as pl
from jax.experimental.pallas import tpu as pltpu
from jax.sharding import PartitionSpec as P

AXES = ("depth", "slab")


def split(value):
    high = value.astype(jnp.bfloat16)
    return high, (value - high.astype(jnp.float32)).astype(jnp.bfloat16)


def product(left, right):
    left_high, left_low = split(left)
    right_high, right_low = split(right)
    dot = functools.partial(jnp.dot, preferred_element_type=jnp.float32)
    return dot(left_high, right_high) + (dot(left_high, right_low) + dot(left_low, right_high))


def inverse(coupling, power, total):
    order = coupling.shape[0]
    row = lax.broadcasted_iota(jnp.int32, (order, order), 0)
    column = lax.broadcasted_iota(jnp.int32, (order, order), 1)
    result = coupling + jnp.where(row == column, 1.0, 0.0)
    for _ in range(2):
        coupling = product(coupling, coupling)
        result = result + product(result, coupling)
    power[...] = coupling
    total[...] = result

    def more(state):
        turn, size = state
        return jnp.logical_and(turn < 40, size > 2.0**-24)

    def step(state):
        turn, _ = state
        squared = product(power[...], power[...])
        total[...] += product(total[...], squared)
        power[...] = squared
        return turn + 1, jnp.sum(squared * squared)

    lax.while_loop(more, step, (0, jnp.sum(coupling * coupling)))
    return total[...]


def call(body, flags, blocks, outs, scratch=True):
    order = blocks[0].shape[-1]
    square = jax.ShapeDtypeStruct((order, order), jnp.float32)
    vmem = pl.BlockSpec(memory_space=pltpu.VMEM)
    results = pl.pallas_call(
        body,
        out_shape=[square] * outs,
        in_specs=[pl.BlockSpec(memory_space=pltpu.SMEM)] + [vmem] * len(blocks),
        out_specs=[vmem] * outs,
        scratch_shapes=[pltpu.VMEM((order, order), jnp.float32)] * 2 if scratch else [],
        compiler_params=pltpu.CompilerParams(vmem_limit_bytes=32 * 2**20),
    )(flags, *blocks)
    return list(results)


def first_step(flags, own, c0, out0, down, back, up, power, total):
    turned = 2 * flags[0]
    refl, trans, behind, upward = own[turned], own[1 + turned], own[2 - turned], own[3 - turned]
    solver = inverse(product(behind, c0[...]), power, total)
    down[...] = product(solver, trans)
    back[...] = product(solver, behind)
    bounce = product(upward, c0[...])
    up[...] = upward + product(bounce, back[...])
    out0[...] = refl + product(bounce, down[...])


def second_step(flags, down, back, c1, out1, through):
    out1[...] = product(c1[...], down[...])
    through[...] = product(c1[...], back[...])


def third_step(flags, up, through, c2, out2, rest):
    out2[...] = product(up[...], c2[...])
    rest[...] = product(through[...], c2[...])


def real_blocks(turned, blocks):
    return [jnp.where(turned, blocks[3 - i][...], blocks[i][...]) for i in range(4)]


def lower_run(flags, o0, o1, o2, o3, refl_b, trans_b, refl, trans, power, total):
    refl_a, trans_a, up_a, back_a = real_blocks(flags[0] == 1, (o0, o1, o2, o3))
    solver = inverse(product(back_a, refl_b[...]), power, total)
    down = product(solver, trans_a)
    refl[...] = refl_a + product(product(up_a, refl_b[...]), down)
    trans[...] = product(trans_b[...], down)


def star_into(upper, lower, refl, trans, up, back, power, total):
    refl_a, trans_a, up_a, back_a = upper
    refl_b, trans_b, up_b, back_b = lower
    solver = inverse(product(back_a, refl_b), power, total)
    down = product(solver, trans_a)
    bounce = product(up_a, refl_b)
    turned_up = product(solver, product(back_a, up_b))
    back[...] = back_b + product(trans_b, turned_up)
    trans[...] = product(trans_b, down)
    up[...] = product(up_a, up_b) + product(bounce, turned_up)
    refl[...] = refl_a + product(bounce, down)


def upper_run(flags, o0, o1, o2, o3, c0, c1, c2, c3, *outs):
    upper = real_blocks(flags[1] == 1, (c0, c1, c2, c3))
    lower = real_blocks(flags[0] == 1, (o0, o1, o2, o3))
    star_into(upper, lower, *outs)


def any_run(flags, o0, o1, o2, o3, c0, c1, c2, c3, *outs):
    own = real_blocks(flags[0] == 1, (o0, o1, o2, o3))
    came = real_blocks(flags[1] == 1, (c0, c1, c2, c3))
    below = flags[2] == 1
    upper = [jnp.where(below, c, o) for o, c in zip(own, came)]
    lower = [jnp.where(below, o, c) for o, c in zip(own, came)]
    star_into(upper, lower, *outs)


def whole_run(flags, refl_a, trans_a, up_a, back_a, refl_b, trans_b, refl, trans, power, total):
    solver = inverse(product(back_a[...], refl_b[...]), power, total)
    down = product(solver, trans_a[...])
    trans[...] = product(trans_b[...], down)
    refl[...] = refl_a[...] + product(product(up_a[...], refl_b[...]), down)


def times_transpose(rows, matrix):
    return lax.dot_general(
        rows, matrix, (((1,), (1,)), ((), ())), precision=lax.Precision.HIGH, preferred_element_type=jnp.float32
    )


def filled(useful, groups, count):
    def mate(device):
        return (device[0] ^ 1, device[1])

    devices = [(g, s) for g in range(groups) for s in range(count)]
    pairs = dict(useful)
    if groups % 2 == 0:
        targets = set(pairs.values())
        for device in devices:
            if device not in pairs and mate(device) not in targets:
                pairs[device] = mate(device)
        spare = set(devices) - set(pairs.values())
        for source, target in useful.items():
            if mate(target) not in pairs and mate(source) in spare:
                pairs[mate(target)] = mate(source)
                spare.discard(mate(source))
    return sorted((a[0] * count + a[1], b[0] * count + b[1]) for a, b in pairs.items())


def shards(slabs, incident):
    groups, count = lax.axis_size("depth"), lax.axis_size("slab")
    group, place = lax.axis_index("depth"), lax.axis_index("slab")
    levels = count.bit_length() - 1
    parity = group % 2

    def send(block, useful):
        return lax.ppermute(block, AXES, filled(useful, groups, count))

    def turn(g, k):
        return g % 2 if k < count // 2 - 1 else 0

    def home(g, k):
        return (g, 2 * k + turn(g, k))

    def guest(g, k):
        return (g, 2 * k + 1 - turn(g, k))

    pair = place // 2
    turned = jnp.where(pair == count // 2 - 1, 0, parity)
    owners = [range(count // 2)]
    merges = []
    while len(owners[-1]) > 1:
        now, kept = owners[-1], []
        merges.append([])
        for k in range(0, len(now), 2):
            below = len(now) > 2 and k // 2 % 2 == 0
            merges[-1].append((now[k], now[k + 1], True) if below else (now[k + 1], now[k], False))
            kept.append(merges[-1][-1][1])
        owners.append(kept)

    def routes(level, reverse=False, wanted=lambda merge: True):
        found = {}
        for merge in merges[level - 1]:
            source, target, _ = merge
            if wanted(merge):
                for g in range(groups):
                    a, b = home(g, source), home(g, target)
                    found[b if reverse else a] = a if reverse else b
        return found

    def is_one(pairs):
        return functools.reduce(jnp.logical_or, [pair == k for k in pairs], False)

    def flags(*values):
        return jnp.stack([jnp.asarray(v).astype(jnp.int32) for v in values])

    own = slabs[0, 0]
    spread = {guest(g, k): home(g, k) for g in range(groups) for k in range(count // 2)}
    came = []
    for index in (0, 1, 3, 2):
        chosen = lax.dynamic_index_in_dim(own, index + 2 * turned * (1 if index < 2 else -1), keepdims=False)
        came.append(send(chosen, spread))
    first = flags(turned)
    split_level = levels - 2
    onward = routes(1)
    onward_late = routes(1, wanted=lambda m: m[2]) if split_level == 1 else onward
    out0, down, back, up = call(first_step, first, [own, came[0]], 4)
    sent = [send(out0, onward)]
    out1, through = call(second_step, first, [down, back, came[1]], 2, False)
    sent.append(send(out1, onward))
    out2, rest = call(third_step, first, [up, through, came[2]], 2, False)
    sent.append(send(out2, onward_late))
    out3 = came[3] + rest
    sent.append(send(out3, onward_late))
    state = [out0, out1, out2, out3]
    own_turned, came_turned = turned, is_one([m[1] for m in merges[0] if m[0] < count // 2 - 1]) * parity

    for level in range(1, levels - 1):
        if level > 1:
            own_turned, came_turned = 0, 0
            late = routes(level, wanted=lambda m: m[2]) if level == split_level else routes(level)
            sent = [send(block, routes(level) if i < 2 else late) for i, block in enumerate(state)]
        if level < split_level:
            below = is_one([m[1] for m in merges[level - 1] if m[2]])
            state = call(any_run, flags(own_turned, came_turned, below), state + sent, 4)
        else:
            last = call(lower_run, flags(own_turned), state + sent[:2], 2)
            state = call(upper_run, flags(own_turned, came_turned), state + sent, 4)

    top = routes(levels - 1)
    arrived = [send(block, top) for block in last]
    refl, trans = call(whole_run, flags(0), state + arrived, 2)

    def spread_out(block):
        for level in range(levels - 1, 0, -1):
            fresh = is_one([m[0] for m in merges[level - 1]])
            block = jnp.where(fresh, send(block, routes(level, reverse=True)), block)
        at_home = place == 2 * pair + turned
        return jnp.where(at_home, block, send(block, {b: a for a, b in spread.items()}))

    trans = spread_out(trans)
    refl = spread_out(refl)

    injected = incident[0]
    field = injected
    for g in range(groups - 1):
        leaving = times_transpose(field, trans)
        arriving = send(leaving, {(g, s): (g + 1, s) for s in range(count)})
        field = jnp.where(group == g + 1, injected + arriving, field)
    bounced = times_transpose(field, refl)
    return (field[None], bounced[None])


def solution(mesh):
    placed = (P("depth", "slab", None, None, None), P("depth", "slab", None))
    return jax.shard_map(
        shards,
        mesh=mesh,
        in_specs=placed,
        out_specs=(P("depth", "slab", None), P("depth", "slab", None)),
        check_vma=False,
    )
```

profile of v0, /device:TPU:25, one launch (start us, length us, event | category | flops | bytes accessed | tf_op | source)
XLA Modules:
  0.0 78.7 jit_solution(14974103529941847871)
XLA Ops:
  0.7 0.0 copy-start
  0.7 1.4 %dynamic-slice_bitcast_fusion = (f32[256,256]{1,0:T(8,128)S(1)}, f32[256,256]{1,0:T(8,128)S(1)}, f32[256,256]{1,0:T(8,128)S(1)}, f32[256,256]{1,0:T(8,128)S(1)}) fusion(f32[1,1,4,256,256]{4,3,2,1,0:T(8,128)} %param.2, s32[]{:T(128)S(6)} %select_n.90, s32[]{:T(128)S(6)} %select_n.88, s32[]{:T(128)S(6)} %select_n.87, s32[]{:T(128)S(6)} %select_n.89), kind=kLoop, calls=%fused_computation.9 | loop fusion | bytes 2097168 | tf_op jit(solution)/shard_map/jit(dynamic_index_in_dim)/squeeze | solution.py:210
  2.1 1.3 %collective-permute-start = (f32[256,256]{1,0:T(8,128)S(1)}, f32[256,256]{1,0:T(8,128)S(1)}, u32[]{:S(2)}, u32[]{:S(2)}) collective-permute-start(f32[256,256]{1,0:T(8,128)S(1)} %get-tuple-element.38), channel_id=1, source_target_pairs={{0,8},{1,0},{2,10},{3,2},{4,12},{5,4},{6,7},{7,6},{8,9},{9,1},{10,... | collective-permute-start | bytes 786440 | tf_op jit(solution)/shard_map/ppermute | solution.py:166
  3.3 0.3 collective-permute-start.1
  3.6 1.2 %collective-permute-start.2 = (f32[256,256]{1,0:T(8,128)S(1)}, f32[256,256]{1,0:T(8,128)S(1)}, u32[]{:S(2)}, u32[]{:S(2)}) collective-permute-start(f32[256,256]{1,0:T(8,128)S(1)} %get-tuple-element.39), channel_id=1, source_target_pairs={{0,8},{1,0},{2,10},{3,2},{4,12},{5,4},{6,7},{7,6},{8,9},{9,1},{10,... | collective-permute-start | bytes 786440 | tf_op jit(solution)/shard_map/ppermute | solution.py:166
  4.8 0.3 collective-permute-start.3
  5.0 4.2 %collective-permute-done.c0 = f32[256,256]{1,0:T(8,128)S(1)} collective-permute-done((f32[256,256]{1,0:T(8,128)S(1)}, f32[256,256]{1,0:T(8,128)S(1)}, u32[]{:S(2)}, u32[]{:S(2)}) %collective-permute-start) | collective-permute-done | bytes 262176 | tf_op jit(solution)/shard_map/ppermute | solution.py:166
  9.3 0.0 copy-done
  9.3 2.1 %shard_map.41 = (f32[256,256]{1,0:T(8,128)S(1)}, f32[256,256]{1,0:T(8,128)S(1)}, f32[256,256]{1,0:T(8,128)S(1)}, f32[256,256]{1,0:T(8,128)S(1)}) custom-call(s32[1]{0:T(128)} %bitcast.1.flags, f32[4,256,256]{2,1,0:T(8,128)S(1)} %bitcast.37, f32[256,256]{1,0:T(8,128)S(1)} %collective-permute-done.c0), custom_call_target="tpu_custom_call" | custom-call | tf_op jit(solution)/shard_map/pallas_call | solution.py:55
  11.4 0.1 collective-permute-start.4
  11.5 3.4 %collective-permute-done.1.c1 = f32[256,256]{1,0:T(8,128)S(1)} collective-permute-done((f32[256,256]{1,0:T(8,128)S(1)}, f32[256,256]{1,0:T(8,128)S(1)}, u32[]{:S(2)}, u32[]{:S(2)}) %collective-permute-start.1) | collective-permute-done | bytes 262176 | tf_op jit(solution)/shard_map/ppermute | solution.py:166
  14.9 0.4 shard_map.42
  15.3 0.1 collective-permute-start.5
  15.4 10.8 %collective-permute-done.2.c2 = f32[256,256]{1,0:T(8,128)S(1)} collective-permute-done((f32[256,256]{1,0:T(8,128)S(1)}, f32[256,256]{1,0:T(8,128)S(1)}, u32[]{:S(2)}, u32[]{:S(2)}) %collective-permute-start.2) | collective-permute-done | bytes 262176 | tf_op jit(solution)/shard_map/ppermute | solution.py:166
  26.1 0.4 shard_map.43
  26.5 2.7 %collective-permute-start.6 = (f32[256,256]{1,0:T(8,128)S(1)}, f32[256,256]{1,0:T(8,128)S(1)}, u32[]{:S(2)}, u32[]{:S(2)}) collective-permute-start(f32[256,256]{1,0:T(8,128)S(1)} %get-tuple-element.24.o2), channel_id=1, source_target_pairs={{0,2},{1,9},{2,10},{3,1},{4,12},{5,13},{6,14},{7,15},{8,0},{9,11},... | collective-permute-start | bytes 786440 | tf_op jit(solution)/shard_map/ppermute | solution.py:166
  29.2 2.5 %collective-permute-done.3 = f32[256,256]{1,0:T(8,128)S(1)} collective-permute-done((f32[256,256]{1,0:T(8,128)S(1)}, f32[256,256]{1,0:T(8,128)S(1)}, u32[]{:S(2)}, u32[]{:S(2)}) %collective-permute-start.3) | collective-permute-done | bytes 262176 | tf_op jit(solution)/shard_map/ppermute | solution.py:166
  31.8 1.6 %collective-permute-start.7 = (f32[256,256]{1,0:T(8,128)S(1)}, f32[256,256]{1,0:T(8,128)S(1)}, u32[]{:S(2)}, u32[]{:S(2)}) collective-permute-start(f32[256,256]{1,0:T(8,128)S(1)} %add.58.o3), channel_id=1, source_target_pairs={{0,2},{1,9},{2,10},{3,1},{4,12},{5,13},{6,14},{7,15},{8,0},{9,11},... | collective-permute-start | bytes 786440 | tf_op jit(solution)/shard_map/ppermute | solution.py:166
  33.4 0.0 collective-permute-done.4.c0.refl_b
  33.4 0.0 collective-permute-done.5.c1.trans_b
  33.4 2.0 %shard_map.45 = (f32[256,256]{1,0:T(8,128)S(1)}, f32[256,256]{1,0:T(8,128)S(1)}) custom-call(s32[1]{0:T(128)} %bitcast.1.flags, f32[256,256]{1,0:T(8,128)S(1)} %get-tuple-element.18.o0, f32[256,256]{1,0:T(8,128)S(1)} %get-tuple-element.21.o1, f32[256,256]{1,0:T(8,128)S(1)} %get-tuple-element.24.o2, f32[256,256]{1,0:T(8,128)S(1)} %add.58.o3, ...), custom_call_target="tpu_custom_call" | custom-call | tf_op jit(solution)/shard_map/pallas_call | solution.py:55
  35.4 0.1 collective-permute-start.8
  35.5 0.5 collective-permute-start.9
  36.0 0.1 pad_add_fusion.flags
  36.1 0.0 collective-permute-done.6.c2
  36.1 0.0 collective-permute-done.7.c3
  36.1 3.4 %shard_map.44 = (f32[256,256]{1,0:T(8,128)S(1)}, f32[256,256]{1,0:T(8,128)S(1)}, f32[256,256]{1,0:T(8,128)S(1)}, f32[256,256]{1,0:T(8,128)S(1)}) custom-call(s32[2]{0:T(128)S(1)} %pad_add_fusion.flags, f32[256,256]{1,0:T(8,128)S(1)} %get-tuple-element.18.o0, f32[256,256]{1,0:T(8,128)S(1)} %get-tuple-element.21.o1, f32[256,256]{1,0:T(8,128)S(1)} %get-tuple-element.24.o2, ...), custom_call_target="tpu_custom_call" | custom-call | tf_op jit(solution)/shard_map/pallas_call | solution.py:55
  39.5 0.0 collective-permute-done.8.refl_b
  39.5 0.0 collective-permute-done.9.trans_b
  39.5 2.1 %shard_map.46 = (f32[256,256]{1,0:T(8,128)S(1)}, f32[256,256]{1,0:T(8,128)S(1)}) custom-call(s32[1]{0:T(128)} %constant.57.clone.1.flags, f32[256,256]{1,0:T(8,128)S(1)} %get-tuple-element.26.refl_a, f32[256,256]{1,0:T(8,128)S(1)} %get-tuple-element.27.trans_a, f32[256,256]{1,0:T(8,128)S(1)} %get-tuple-element.28.up_a, ...), custom_call_target="tpu_custom_call" | custom-call | tf_op jit(solution)/shard_map/pallas_call | solution.py:55
  41.7 0.1 collective-permute-start.10
  41.8 1.5 %collective-permute-done.10 = f32[256,256]{1,0:T(8,128)S(1)} collective-permute-done((f32[256,256]{1,0:T(8,128)S(1)}, f32[256,256]{1,0:T(8,128)S(1)}, u32[]{:S(2)}, u32[]{:S(2)}) %collective-permute-start.10) | collective-permute-done | bytes 262176 | tf_op jit(solution)/shard_map/ppermute | solution.py:166
  43.3 0.1 collective-permute-start.11
  43.4 6.1 %collective-permute-done.11 = f32[256,256]{1,0:T(8,128)S(1)} collective-permute-done((f32[256,256]{1,0:T(8,128)S(1)}, f32[256,256]{1,0:T(8,128)S(1)}, u32[]{:S(2)}, u32[]{:S(2)}) %collective-permute-start.11) | collective-permute-done | bytes 262176 | tf_op jit(solution)/shard_map/ppermute | solution.py:166
  49.5 0.1 collective-permute-start.12
  49.6 0.0 copy-start.1
  49.6 7.4 %collective-permute-done.12 = f32[256,256]{1,0:T(8,128)S(1)} collective-permute-done((f32[256,256]{1,0:T(8,128)S(1)}, f32[256,256]{1,0:T(8,128)S(1)}, u32[]{:S(2)}, u32[]{:S(2)}) %collective-permute-start.12) | collective-permute-done | bytes 262176 | tf_op jit(solution)/shard_map/ppermute | solution.py:166
  57.1 0.0 copy-done.1
  57.1 0.3 convolution_bitcast_fusion.1
  57.5 1.3 %collective-permute-start.13 = (f32[256,256]{0,1:T(8,128)S(1)}, f32[256,256]{0,1:T(8,128)S(1)}, u32[]{:S(2)}, u32[]{:S(2)}) collective-permute-start(f32[256,256]{0,1:T(8,128)S(1)} %convolution_bitcast_fusion.1), channel_id=1, source_target_pairs={{0,8},{1,9},{2,10},{3,11},{4,12},{5,13},{6,14},{7,15},{8,0},{9,1},... | collective-permute-start | bytes 786440 | tf_op jit(solution)/shard_map/ppermute | solution.py:166
  58.8 0.1 copy.4
  58.9 0.1 collective-permute-start.16
  59.0 1.0 %collective-permute-done.13 = f32[256,256]{0,1:T(8,128)S(1)} collective-permute-done((f32[256,256]{0,1:T(8,128)S(1)}, f32[256,256]{0,1:T(8,128)S(1)}, u32[]{:S(2)}, u32[]{:S(2)}) %collective-permute-start.13) | collective-permute-done | bytes 262176 | tf_op jit(solution)/shard_map/ppermute | solution.py:166
  59.9 0.3 fusion.5
  60.2 1.6 %collective-permute-start.14 = (f32[256,256]{0,1:T(8,128)S(1)}, f32[256,256]{0,1:T(8,128)S(1)}, u32[]{:S(2)}, u32[]{:S(2)}) collective-permute-start(f32[256,256]{0,1:T(8,128)S(1)} %fusion.5), channel_id=1, source_target_pairs={{0,8},{1,9},{2,10},{3,11},{4,12},{5,13},{6,14},{7,15},{8,16},{9,17... | collective-permute-start | bytes 786440 | tf_op jit(solution)/shard_map/ppermute | solution.py:166
  61.8 0.0 collective-permute-done.16
  61.9 0.1 collective-permute-start.17
  61.9 3.2 %collective-permute-done.14 = f32[256,256]{0,1:T(8,128)S(1)} collective-permute-done((f32[256,256]{0,1:T(8,128)S(1)}, f32[256,256]{0,1:T(8,128)S(1)}, u32[]{:S(2)}, u32[]{:S(2)}) %collective-permute-start.14) | collective-permute-done | bytes 262176 | tf_op jit(solution)/shard_map/ppermute | solution.py:166
  65.1 0.3 fusion.6
  65.4 1.4 %collective-permute-start.15 = (f32[256,256]{0,1:T(8,128)S(1)}, f32[256,256]{0,1:T(8,128)S(1)}, u32[]{:S(2)}, u32[]{:S(2)}) collective-permute-start(f32[256,256]{0,1:T(8,128)S(1)} %fusion.6), channel_id=1, source_target_pairs={{0,8},{1,9},{2,10},{3,11},{4,12},{5,13},{6,14},{7,15},{8,0},{9,1},... | collective-permute-start | bytes 786440 | tf_op jit(solution)/shard_map/ppermute | solution.py:166
  66.8 2.7 %collective-permute-done.17 = f32[256,256]{1,0:T(8,128)S(1)} collective-permute-done((f32[256,256]{1,0:T(8,128)S(1)}, f32[256,256]{1,0:T(8,128)S(1)}, u32[]{:S(2)}, u32[]{:S(2)}) %collective-permute-start.17) | collective-permute-done | bytes 262176 | tf_op jit(solution)/shard_map/ppermute | solution.py:166
  69.5 0.1 collective-permute-start.18
  69.6 0.0 collective-permute-done.15
  69.6 0.1 fusion.1
  69.7 0.8 %copy.7 = f32[1,256,256]{2,1,0:T(8,128)} copy(f32[1,256,256]{1,2,0:T(8,128)S(1)} %bitcast.38) | data formatting | bytes 524288
  70.5 7.1 %collective-permute-done.18 = f32[256,256]{1,0:T(8,128)S(1)} collective-permute-done((f32[256,256]{1,0:T(8,128)S(1)}, f32[256,256]{1,0:T(8,128)S(1)}, u32[]{:S(2)}, u32[]{:S(2)}) %collective-permute-start.18) | collective-permute-done | bytes 262176 | tf_op jit(solution)/shard_map/ppermute | solution.py:166
  77.6 1.1 %convolution_bitcast_fusion = f32[1,256,256]{2,1,0:T(8,128)} fusion(f32[256,256]{0,1:T(8,128)S(1)} %fusion.1, f32[256,256]{1,0:T(8,128)S(1)} %broadcast_select_fusion.2, f32[256,256]{1,0:T(8,128)S(1)} %collective-permute-done.18, pred[]{:T(512)S(6)} %eq.35), kind=kOutput, calls=%fused_computation | convolution fusion | flops 100728832 | bytes 1048577 | tf_op jit(solution)/shard_map/dot_general | solution.py:135
  (6 shorter events, 0.2 us)
Async XLA Ops:
  0.7 8.6 %copy-start = (f32[1,1,4,256,256]{4,3,2,1,0:T(8,128)S(1)}, f32[1,1,4,256,256]{4,3,2,1,0:T(8,128)}, u32[]{:S(2)}) copy-start(f32[1,1,4,256,256]{4,3,2,1,0:T(8,128)} %param.2) | copy-start | bytes 3145732
  2.1 7.2 %collective-permute-start = (f32[256,256]{1,0:T(8,128)S(1)}, f32[256,256]{1,0:T(8,128)S(1)}, u32[]{:S(2)}, u32[]{:S(2)}) collective-permute-start(f32[256,256]{1,0:T(8,128)S(1)} %get-tuple-element.38), channel_id=1, source_target_pairs={{0,8},{1,0},{2,10},{3,2},{4,12},{5,4},{6,7},{7,6},{8,9},{9,1},{10,... | collective-permute-start | bytes 786440 | tf_op jit(solution)/shard_map/ppermute | solution.py:166
  3.3 11.6 %collective-permute-start.1 = (f32[256,256]{1,0:T(8,128)S(1)}, f32[256,256]{1,0:T(8,128)S(1)}, u32[]{:S(2)}, u32[]{:S(2)}) collective-permute-start(f32[256,256]{1,0:T(8,128)S(1)} %get-tuple-element.37), channel_id=1, source_target_pairs={{0,8},{1,0},{2,10},{3,2},{4,12},{5,4},{6,7},{7,6},{8,9},{9,1},{10,... | collective-permute-start | bytes 786440 | tf_op jit(solution)/shard_map/ppermute | solution.py:166
  3.6 22.6 %collective-permute-start.2 = (f32[256,256]{1,0:T(8,128)S(1)}, f32[256,256]{1,0:T(8,128)S(1)}, u32[]{:S(2)}, u32[]{:S(2)}) collective-permute-start(f32[256,256]{1,0:T(8,128)S(1)} %get-tuple-element.39), channel_id=1, source_target_pairs={{0,8},{1,0},{2,10},{3,2},{4,12},{5,4},{6,7},{7,6},{8,9},{9,1},{10,... | collective-permute-start | bytes 786440 | tf_op jit(solution)/shard_map/ppermute | solution.py:166
  4.8 27.0 %collective-permute-start.3 = (f32[256,256]{1,0:T(8,128)S(1)}, f32[256,256]{1,0:T(8,128)S(1)}, u32[]{:S(2)}, u32[]{:S(2)}) collective-permute-start(f32[256,256]{1,0:T(8,128)S(1)} %get-tuple-element.36), channel_id=1, source_target_pairs={{0,8},{1,0},{2,10},{3,2},{4,12},{5,4},{6,7},{7,6},{8,9},{9,1},{10,... | collective-permute-start | bytes 786440 | tf_op jit(solution)/shard_map/ppermute | solution.py:166
  11.4 22.0 %collective-permute-start.4 = (f32[256,256]{1,0:T(8,128)S(1)}, f32[256,256]{1,0:T(8,128)S(1)}, u32[]{:S(2)}, u32[]{:S(2)}) collective-permute-start(f32[256,256]{1,0:T(8,128)S(1)} %get-tuple-element.18.o0), channel_id=1, source_target_pairs={{0,2},{1,9},{2,10},{3,1},{4,12},{5,6},{6,4},{7,15},{8,0},{9,11},{1... | collective-permute-start | bytes 786440 | tf_op jit(solution)/shard_map/ppermute | solution.py:166
  15.3 18.1 %collective-permute-start.5 = (f32[256,256]{1,0:T(8,128)S(1)}, f32[256,256]{1,0:T(8,128)S(1)}, u32[]{:S(2)}, u32[]{:S(2)}) collective-permute-start(f32[256,256]{1,0:T(8,128)S(1)} %get-tuple-element.21.o1), channel_id=1, source_target_pairs={{0,2},{1,9},{2,10},{3,1},{4,12},{5,6},{6,4},{7,15},{8,0},{9,11},{1... | collective-permute-start | bytes 786440 | tf_op jit(solution)/shard_map/ppermute | solution.py:166
  26.5 9.6 %collective-permute-start.6 = (f32[256,256]{1,0:T(8,128)S(1)}, f32[256,256]{1,0:T(8,128)S(1)}, u32[]{:S(2)}, u32[]{:S(2)}) collective-permute-start(f32[256,256]{1,0:T(8,128)S(1)} %get-tuple-element.24.o2), channel_id=1, source_target_pairs={{0,2},{1,9},{2,10},{3,1},{4,12},{5,13},{6,14},{7,15},{8,0},{9,11},... | collective-permute-start | bytes 786440 | tf_op jit(solution)/shard_map/ppermute | solution.py:166
  31.8 4.3 %collective-permute-start.7 = (f32[256,256]{1,0:T(8,128)S(1)}, f32[256,256]{1,0:T(8,128)S(1)}, u32[]{:S(2)}, u32[]{:S(2)}) collective-permute-start(f32[256,256]{1,0:T(8,128)S(1)} %add.58.o3), channel_id=1, source_target_pairs={{0,2},{1,9},{2,10},{3,1},{4,12},{5,13},{6,14},{7,15},{8,0},{9,11},... | collective-permute-start | bytes 786440 | tf_op jit(solution)/shard_map/ppermute | solution.py:166
  35.4 4.1 %collective-permute-start.8 = (f32[256,256]{1,0:T(8,128)S(1)}, f32[256,256]{1,0:T(8,128)S(1)}, u32[]{:S(2)}, u32[]{:S(2)}) collective-permute-start(f32[256,256]{1,0:T(8,128)S(1)} %get-tuple-element.30), channel_id=1, source_target_pairs={{0,8},{1,9},{2,10},{3,5},{4,2},{5,13},{6,14},{7,15},{8,0},{9,1},{1... | collective-permute-start | bytes 786440 | tf_op jit(solution)/shard_map/ppermute | solution.py:166
  35.5 4.0 %collective-permute-start.9 = (f32[256,256]{1,0:T(8,128)S(1)}, f32[256,256]{1,0:T(8,128)S(1)}, u32[]{:S(2)}, u32[]{:S(2)}) collective-permute-start(f32[256,256]{1,0:T(8,128)S(1)} %get-tuple-element.31), channel_id=1, source_target_pairs={{0,8},{1,9},{2,10},{3,5},{4,2},{5,13},{6,14},{7,15},{8,0},{9,1},{1... | collective-permute-start | bytes 786440 | tf_op jit(solution)/shard_map/ppermute | solution.py:166
  41.7 1.6 %collective-permute-start.10 = (f32[256,256]{1,0:T(8,128)S(1)}, f32[256,256]{1,0:T(8,128)S(1)}, u32[]{:S(2)}, u32[]{:S(2)}) collective-permute-start(f32[256,256]{1,0:T(8,128)S(1)} %get-tuple-element.32), channel_id=1, source_target_pairs={{0,8},{1,9},{2,4},{3,11},{4,12},{5,3},{6,14},{7,15},{8,0},{9,1},{1... | collective-permute-start | bytes 786440 | tf_op jit(solution)/shard_map/ppermute | solution.py:166
  43.3 6.2 %collective-permute-start.11 = (f32[256,256]{1,0:T(8,128)S(1)}, f32[256,256]{1,0:T(8,128)S(1)}, u32[]{:S(2)}, u32[]{:S(2)}) collective-permute-start(f32[256,256]{1,0:T(8,128)S(1)} %broadcast_select_fusion.1), channel_id=1, source_target_pairs={{0,8},{1,3},{2,0},{3,11},{4,6},{5,13},{6,5},{7,15},{8,10},{9,1},{1... | collective-permute-start | bytes 786440 | tf_op jit(solution)/shard_map/ppermute | solution.py:166
  49.5 7.5 %collective-permute-start.12 = (f32[256,256]{1,0:T(8,128)S(1)}, f32[256,256]{1,0:T(8,128)S(1)}, u32[]{:S(2)}, u32[]{:S(2)}) collective-permute-start(f32[256,256]{1,0:T(8,128)S(1)} %broadcast_select_fusion.3), channel_id=1, source_target_pairs={{0,1},{1,9},{2,3},{3,11},{4,5},{5,13},{6,7},{7,6},{8,0},{9,8},{10,... | collective-permute-start | bytes 786440 | tf_op jit(solution)/shard_map/ppermute | solution.py:166
  49.6 7.5 %copy-start.1 = (f32[1,256,256]{2,1,0:T(8,128)S(1)}, f32[1,256,256]{2,1,0:T(8,128)}, u32[]{:S(2)}) copy-start(f32[1,256,256]{2,1,0:T(8,128)} %param.3) | copy-start | bytes 786436
  57.5 2.5 %collective-permute-start.13 = (f32[256,256]{0,1:T(8,128)S(1)}, f32[256,256]{0,1:T(8,128)S(1)}, u32[]{:S(2)}, u32[]{:S(2)}) collective-permute-start(f32[256,256]{0,1:T(8,128)S(1)} %convolution_bitcast_fusion.1), channel_id=1, source_target_pairs={{0,8},{1,9},{2,10},{3,11},{4,12},{5,13},{6,14},{7,15},{8,0},{9,1},... | collective-permute-start | bytes 786440 | tf_op jit(solution)/shard_map/ppermute | solution.py:166
  58.9 2.9 %collective-permute-start.16 = (f32[256,256]{1,0:T(8,128)S(1)}, f32[256,256]{1,0:T(8,128)S(1)}, u32[]{:S(2)}, u32[]{:S(2)}) collective-permute-start(f32[256,256]{1,0:T(8,128)S(1)} %get-tuple-element.33), channel_id=1, source_target_pairs={{0,8},{1,9},{2,4},{3,11},{4,12},{5,3},{6,14},{7,15},{8,0},{9,1},{1... | collective-permute-start | bytes 786440 | tf_op jit(solution)/shard_map/ppermute | solution.py:166
  60.2 4.9 %collective-permute-start.14 = (f32[256,256]{0,1:T(8,128)S(1)}, f32[256,256]{0,1:T(8,128)S(1)}, u32[]{:S(2)}, u32[]{:S(2)}) collective-permute-start(f32[256,256]{0,1:T(8,128)S(1)} %fusion.5), channel_id=1, source_target_pairs={{0,8},{1,9},{2,10},{3,11},{4,12},{5,13},{6,14},{7,15},{8,16},{9,17... | collective-permute-start | bytes 786440 | tf_op jit(solution)/shard_map/ppermute | solution.py:166
  61.9 7.7 %collective-permute-start.17 = (f32[256,256]{1,0:T(8,128)S(1)}, f32[256,256]{1,0:T(8,128)S(1)}, u32[]{:S(2)}, u32[]{:S(2)}) collective-permute-start(f32[256,256]{1,0:T(8,128)S(1)} %broadcast_select_fusion), channel_id=1, source_target_pairs={{0,8},{1,3},{2,0},{3,11},{4,6},{5,13},{6,5},{7,15},{8,10},{9,1},{1... | collective-permute-start | bytes 786440 | tf_op jit(solution)/shard_map/ppermute | solution.py:166
  65.4 4.2 %collective-permute-start.15 = (f32[256,256]{0,1:T(8,128)S(1)}, f32[256,256]{0,1:T(8,128)S(1)}, u32[]{:S(2)}, u32[]{:S(2)}) collective-permute-start(f32[256,256]{0,1:T(8,128)S(1)} %fusion.6), channel_id=1, source_target_pairs={{0,8},{1,9},{2,10},{3,11},{4,12},{5,13},{6,14},{7,15},{8,0},{9,1},... | collective-permute-start | bytes 786440 | tf_op jit(solution)/shard_map/ppermute | solution.py:166
  69.5 8.1 %collective-permute-start.18 = (f32[256,256]{1,0:T(8,128)S(1)}, f32[256,256]{1,0:T(8,128)S(1)}, u32[]{:S(2)}, u32[]{:S(2)}) collective-permute-start(f32[256,256]{1,0:T(8,128)S(1)} %broadcast_select_fusion.2), channel_id=1, source_target_pairs={{0,1},{1,9},{2,3},{3,11},{4,5},{5,13},{6,7},{7,6},{8,0},{9,8},{10,... | collective-permute-start | bytes 786440 | tf_op jit(solution)/shard_map/ppermute | solution.py:166
where the time goes:
time: 78.9 us; the launch traced here: 78.7 us
  waiting for transfers between devices  49.9 us (63%)
  starting transfers between devices  12.7 us (16%)
  Pallas kernels  10.5 us (13%)
  local copies, waits for them, and re-layouts  2.33 us (3%)
  matrix products  2 us (3%)
  between operations  0.94 us (1%)
    ppermute x19, waiting for transfers between devices, send(): return lax.ppermute(block, AXES, filled(useful, groups, count))  49.9 us
    ppermute x19, starting transfers between devices, send(): return lax.ppermute(block, AXES, filled(useful, groups, count))  12.7 us
    pallas_call x6, Pallas kernels, call(): pl.pallas_call(body, out_shape=[square] * outs, in_specs=[pl.BlockSpec(me...  10.5 us
    dot_general x4, matrix products, times_transpose(): lax.dot_general(rows, matrix, (((1,), (1,)), ((), ())), precision=lax.Pre...  2 us
  transfers between devices with their start and end apart: 19, of which 11 were waited for; matrix products, arithmetic and copies ran while one was open for 2% of the time, Pallas kernels for 11%

commit v1 on v0

--- a/solution.py
+++ b/solution.py
@@ -88,12 +88,15 @@
     return [jnp.where(turned, blocks[3 - i][...], blocks[i][...]) for i in range(4)]
 
 
-def lower_run(flags, o0, o1, o2, o3, refl_b, trans_b, refl, trans, power, total):
+def lower_run(flags, o0, o1, o2, o3, refl_b, refl, down, power, total):
     refl_a, trans_a, up_a, back_a = real_blocks(flags[0] == 1, (o0, o1, o2, o3))
     solver = inverse(product(back_a, refl_b[...]), power, total)
-    down = product(solver, trans_a)
-    refl[...] = refl_a + product(product(up_a, refl_b[...]), down)
-    trans[...] = product(trans_b[...], down)
+    down[...] = product(solver, trans_a)
+    refl[...] = refl_a + product(product(up_a, refl_b[...]), down[...])
+
+
+def times(flags, left, right, out):
+    out[...] = product(left[...], right[...])
 
 
 def star_into(upper, lower, refl, trans, up, back, power, total):
@@ -124,11 +127,10 @@
     star_into(upper, lower, *outs)
 
 
-def whole_run(flags, refl_a, trans_a, up_a, back_a, refl_b, trans_b, refl, trans, power, total):
+def whole_run(flags, refl_a, trans_a, up_a, back_a, refl_b, refl, down, power, total):
     solver = inverse(product(back_a[...], refl_b[...]), power, total)
-    down = product(solver, trans_a[...])
-    trans[...] = product(trans_b[...], down)
-    refl[...] = refl_a[...] + product(product(up_a[...], refl_b[...]), down)
+    down[...] = product(solver, trans_a[...])
+    refl[...] = refl_a[...] + product(product(up_a[...], refl_b[...]), down[...])
 
 
 def times_transpose(rows, matrix):
@@ -205,10 +207,13 @@
 
     own = slabs[0, 0]
     spread = {guest(g, k): home(g, k) for g in range(groups) for k in range(count // 2)}
-    came = []
-    for index in (0, 1, 3, 2):
-        chosen = lax.dynamic_index_in_dim(own, index + 2 * turned * (1 if index < 2 else -1), keepdims=False)
-        came.append(send(chosen, spread))
+    spread_late = {guest(g, k): home(g, k) for g in range(groups) for k in range(count // 2 - 1)}
+    came, rest_of_own = [], own
+    for index, wanted in ((0, spread), (1, spread), (3, spread_late), (2, spread_late)):
+        chosen = lax.dynamic_index_in_dim(rest_of_own, index + 2 * turned * (1 if index < 2 else -1), keepdims=False)
+        if not came:
+            chosen, rest_of_own = lax.optimization_barrier((chosen, own))
+        came.append(send(chosen, wanted))
     first = flags(turned)
     split_level = levels - 2
     onward = routes(1)
@@ -233,27 +238,33 @@
             below = is_one([m[1] for m in merges[level - 1] if m[2]])
             state = call(any_run, flags(own_turned, came_turned, below), state + sent, 4)
         else:
-            last = call(lower_run, flags(own_turned), state + sent[:2], 2)
+            top = routes(levels - 1)
+            low_refl, low_down = call(lower_run, flags(own_turned), state + sent[:1], 2)
+            arrived = [send(low_refl, top)]
+            (low_trans,) = call(times, flags(0), [sent[1], low_down], 1, False)
+            arrived.append(send(low_trans, top))
             state = call(upper_run, flags(own_turned, came_turned), state + sent, 4)
 
-    top = routes(levels - 1)
-    arrived = [send(block, top) for block in last]
-    refl, trans = call(whole_run, flags(0), state + arrived, 2)
-
-    def spread_out(block):
-        for level in range(levels - 1, 0, -1):
-            fresh = is_one([m[0] for m in merges[level - 1]])
-            block = jnp.where(fresh, send(block, routes(level, reverse=True)), block)
-        at_home = place == 2 * pair + turned
-        return jnp.where(at_home, block, send(block, {b: a for a, b in spread.items()}))
-
-    trans = spread_out(trans)
-    refl = spread_out(refl)
+    refl, down = call(whole_run, flags(0), state + arrived[:1], 2)
+    (trans,) = call(times, flags(0), [arrived[1], down], 1, False)
+
+    at_home = place == 2 * pair + turned
+    hops = []
+    for level in range(levels - 1, 0, -1):
+        hops.append((is_one([m[0] for m in merges[level - 1]]), routes(level, reverse=True)))
+    hops.append((jnp.logical_not(at_home), {b: a for a, b in spread.items()}))
+    for i, (fresh, route) in enumerate(hops):
+        trans = jnp.where(fresh, send(trans, route), trans)
+        if i > 0:
+            trans, _ = lax.optimization_barrier((trans, refl))
+        refl = jnp.where(fresh, send(refl, route), refl)
 
     injected = incident[0]
     field = injected
     for g in range(groups - 1):
         leaving = times_transpose(field, trans)
+        if g == 1:
+            leaving, _ = lax.optimization_barrier((leaving, refl))
         arriving = send(leaving, {(g, s): (g + 1, s) for s in range(count)})
         field = jnp.where(group == g + 1, injected + arriving, field)
     bounced = times_transpose(field, refl)

time: 78.9 us -> 65.9 us (0.84)
  waiting for transfers between devices: 49.9 us -> 19.8 us
  starting transfers between devices: 12.7 us -> 27.5 us
  local copies, waits for them, and re-layouts: 2.33 us -> 4.03 us
    ppermute x19, waiting for transfers between devices: 49.9 us -> 19.8 us  [send(): return lax.ppermute(block, AXES, filled(useful, groups, count))]
    ppermute x19, starting transfers between devices: 12.7 us -> 27.5 us  [send(): return lax.ppermute(block, AXES, filled(useful, groups, count))]
    squeeze x1 -> x2, local copies, waits for them, and re-layouts: 1.35 us -> 2.22 us  [shards(): lax.dynamic_index_in_dim(rest_of_own, index + 2 * turned * (1 if index <...]
    pallas_call x6 -> x8, Pallas kernels: 10.5 us -> 10.9 us  [call(): pl.pallas_call(body, out_shape=[square] * outs, in_specs=[pl.BlockSpec(me...]
  transfers between devices with their start and end apart: 19 -> 19, of which waited for: 11 -> 10; matrix products, arithmetic and copies ran while one was open for 2% -> 3% of each run, Pallas kernels for 11% -> 16%
where the time goes in v1:
time: 65.9 us; the launch traced here: 65.7 us
  starting transfers between devices  27.5 us (42%)
  waiting for transfers between devices  19.8 us (30%)
  Pallas kernels  10.9 us (17%)
  local copies, waits for them, and re-layouts  4.03 us (6%)
  matrix products  2.13 us (3%)
  between operations  0.92 us (1%)
    ppermute x19, starting transfers between devices, send(): return lax.ppermute(block, AXES, filled(useful, groups, count))  27.5 us
    ppermute x19, waiting for transfers between devices, send(): return lax.ppermute(block, AXES, filled(useful, groups, count))  19.8 us
    pallas_call x8, Pallas kernels, call(): pl.pallas_call(body, out_shape=[square] * outs, in_specs=[pl.BlockSpec(me...  10.9 us
    squeeze x2, local copies, waits for them, and re-layouts, shards(): lax.dynamic_index_in_dim(rest_of_own, index + 2 * turned * (1 if index <...  2.22 us
    dot_general x4, matrix products, times_transpose(): lax.dot_general(rows, matrix, (((1,), (1,)), ((), ())), precision=lax.Pre...  2.13 us
    unnamed x6, local copies, waits for them, and re-layouts  1.69 us
  transfers between devices with their start and end apart: 19, of which 10 were waited for; matrix products, arithmetic and copies ran while one was open for 3% of the time, Pallas kernels for 16%

profile of v1, /device:TPU:25, one launch (start us, length us, event | category | flops | bytes accessed | tf_op | source)
XLA Modules:
  0.0 65.7 jit_solution(956729406513795988)
XLA Ops:
  0.7 0.0 copy-start
  0.7 1.1 %dynamic-slice_bitcast_fusion.3 = f32[256,256]{1,0:T(8,128)S(1)} fusion(f32[1,1,4,256,256]{4,3,2,1,0:T(8,128)} %param.2, s32[]{:T(128)S(6)} %select_n.87), kind=kLoop, calls=%fused_computation.11 | loop fusion | bytes 524292 | tf_op jit(solution)/shard_map/jit(dynamic_index_in_dim)/squeeze | solution.py:213
  1.7 1.3 %collective-permute-start = (f32[256,256]{1,0:T(8,128)S(1)}, f32[256,256]{1,0:T(8,128)S(1)}, u32[]{:S(2)}, u32[]{:S(2)}) collective-permute-start(f32[256,256]{1,0:T(8,128)S(1)} %dynamic-slice_bitcast_fusion.3), channel_id=1, source_target_pairs={{0,8},{1,0},{2,10},{3,2},{4,12},{5,4},{6,7},{7,6},{8,9},{9,1},{10,... | collective-permute-start | bytes 786440 | tf_op jit(solution)/shard_map/ppermute | solution.py:168
  3.0 1.2 %dynamic-slice_bitcast_fusion = (f32[256,256]{1,0:T(8,128)S(1)}, f32[256,256]{1,0:T(8,128)S(1)}, f32[256,256]{1,0:T(8,128)S(1)}) fusion(f32[4,256,256]{2,1,0:T(8,128)} %bitcast.38, s32[]{:T(128)S(6)} %select_n.90, s32[]{:T(128)S(6)} %select_n.89, s32[]{:T(128)S(6)} %select_n.88), kind=kLoop, calls=%fused_computation.8 | loop fusion | bytes 1572876 | tf_op jit(solution)/shard_map/jit(dynamic_index_in_dim)/squeeze | solution.py:213
  4.2 0.3 collective-permute-start.1
  4.5 1.2 %collective-permute-start.3 = (f32[256,256]{1,0:T(8,128)S(1)}, f32[256,256]{1,0:T(8,128)S(1)}, u32[]{:S(2)}, u32[]{:S(2)}) collective-permute-start(f32[256,256]{1,0:T(8,128)S(1)} %get-tuple-element.47), channel_id=1, source_target_pairs={{0,8},{1,0},{2,10},{3,2},{4,12},{5,4},{6,14},{7,15},{8,9},{9,1},{1... | collective-permute-start | bytes 786440 | tf_op jit(solution)/shard_map/ppermute | solution.py:168
  5.7 0.0 collective-permute-start.4
  5.7 3.3 %collective-permute-done.c0 = f32[256,256]{1,0:T(8,128)S(1)} collective-permute-done((f32[256,256]{1,0:T(8,128)S(1)}, f32[256,256]{1,0:T(8,128)S(1)}, u32[]{:S(2)}, u32[]{:S(2)}) %collective-permute-start) | collective-permute-done | bytes 262176 | tf_op jit(solution)/shard_map/ppermute | solution.py:168
  9.0 0.0 copy-done
  9.0 2.1 %shard_map.41 = (f32[256,256]{1,0:T(8,128)S(1)}, f32[256,256]{1,0:T(8,128)S(1)}, f32[256,256]{1,0:T(8,128)S(1)}, f32[256,256]{1,0:T(8,128)S(1)}) custom-call(s32[1]{0:T(128)} %bitcast.1.flags, f32[4,256,256]{2,1,0:T(8,128)S(1)} %bitcast.39, f32[256,256]{1,0:T(8,128)S(1)} %collective-permute-done.c0), custom_call_target="tpu_custom_call" | custom-call | tf_op jit(solution)/shard_map/pallas_call | solution.py:55
  11.1 0.1 collective-permute-start.5
  11.1 3.4 %collective-permute-done.1.c1 = f32[256,256]{1,0:T(8,128)S(1)} collective-permute-done((f32[256,256]{1,0:T(8,128)S(1)}, f32[256,256]{1,0:T(8,128)S(1)}, u32[]{:S(2)}, u32[]{:S(2)}) %collective-permute-start.1) | collective-permute-done | bytes 262176 | tf_op jit(solution)/shard_map/ppermute | solution.py:168
  14.6 0.4 shard_map.42
  15.0 0.1 collective-permute-start.2
  15.0 0.0 collective-permute-done.3.c2
  15.1 0.4 shard_map.43
  15.4 0.0 collective-permute-done.4
  15.5 1.6 %collective-permute-start.8 = (f32[256,256]{1,0:T(8,128)S(1)}, f32[256,256]{1,0:T(8,128)S(1)}, u32[]{:S(2)}, u32[]{:S(2)}) collective-permute-start(f32[256,256]{1,0:T(8,128)S(1)} %add.57.o3), channel_id=1, source_target_pairs={{0,2},{1,9},{2,10},{3,1},{4,12},{5,13},{6,14},{7,15},{8,0},{9,11},... | collective-permute-start | bytes 786440 | tf_op jit(solution)/shard_map/ppermute | solution.py:168
  17.1 0.1 collective-permute-start.7
  17.1 0.0 collective-permute-done.5.refl_b.c0
  17.1 2.0 %shard_map.44 = (f32[256,256]{1,0:T(8,128)S(1)}, f32[256,256]{1,0:T(8,128)S(1)}) custom-call(s32[1]{0:T(128)} %bitcast.1.flags, f32[256,256]{1,0:T(8,128)S(1)} %get-tuple-element.28.o0, f32[256,256]{1,0:T(8,128)S(1)} %get-tuple-element.27.o1, f32[256,256]{1,0:T(8,128)S(1)} %get-tuple-element.31.o2, f32[256,256]{1,0:T(8,128)S(1)} %add.57.o3, ...), custom_call_target="tpu_custom_call" | custom-call | tf_op jit(solution)/shard_map/pallas_call | solution.py:55
  19.2 4.0 %collective-permute-start.9 = (f32[256,256]{1,0:T(8,128)S(1)}, f32[256,256]{1,0:T(8,128)S(1)}, u32[]{:S(2)}, u32[]{:S(2)}) collective-permute-start(f32[256,256]{1,0:T(8,128)S(1)} %get-tuple-element.38), channel_id=1, source_target_pairs={{0,8},{1,9},{2,10},{3,5},{4,2},{5,13},{6,14},{7,15},{8,0},{9,1},{1... | collective-permute-start | bytes 786440 | tf_op jit(solution)/shard_map/ppermute | solution.py:168
  23.2 0.0 collective-permute-done.2.left.c1
  23.2 0.3 shard_map.45
  23.5 0.8 %collective-permute-start.6 = (f32[256,256]{1,0:T(8,128)S(1)}, f32[256,256]{1,0:T(8,128)S(1)}, u32[]{:S(2)}, u32[]{:S(2)}) collective-permute-start(f32[256,256]{1,0:T(8,128)S(1)} %shard_map.45), channel_id=1, source_target_pairs={{0,8},{1,9},{2,10},{3,5},{4,2},{5,13},{6,14},{7,15},{8,0},{9,1},{1... | collective-permute-start | bytes 786440 | tf_op jit(solution)/shard_map/ppermute | solution.py:168
  24.2 0.1 pad_add_fusion.flags
  24.3 0.0 collective-permute-done.8.c3
  24.3 0.0 collective-permute-done.7.c2
  24.3 3.4 %shard_map.46 = (f32[256,256]{1,0:T(8,128)S(1)}, f32[256,256]{1,0:T(8,128)S(1)}, f32[256,256]{1,0:T(8,128)S(1)}, f32[256,256]{1,0:T(8,128)S(1)}) custom-call(s32[2]{0:T(128)S(1)} %pad_add_fusion.flags, f32[256,256]{1,0:T(8,128)S(1)} %get-tuple-element.28.o0, f32[256,256]{1,0:T(8,128)S(1)} %get-tuple-element.27.o1, f32[256,256]{1,0:T(8,128)S(1)} %get-tuple-element.31.o2, ...), custom_call_target="tpu_custom_call" | custom-call | tf_op jit(solution)/shard_map/pallas_call | solution.py:55
  27.8 0.0 collective-permute-done.9.refl_b
  27.8 2.0 %shard_map.47 = (f32[256,256]{1,0:T(8,128)S(1)}, f32[256,256]{1,0:T(8,128)S(1)}) custom-call(s32[1]{0:T(128)} %constant.54.clone.1.flags, f32[256,256]{1,0:T(8,128)S(1)} %get-tuple-element.34.refl_a, f32[256,256]{1,0:T(8,128)S(1)} %get-tuple-element.35.trans_a, f32[256,256]{1,0:T(8,128)S(1)} %get-tuple-element.36.up_a, ...), custom_call_target="tpu_custom_call" | custom-call | tf_op jit(solution)/shard_map/pallas_call | solution.py:55
  29.8 0.0 collective-permute-done.6.left
  29.8 0.3 shard_map.48
  30.1 0.1 collective-permute-start.10
  30.2 0.5 collective-permute-start.12
  30.7 1.0 %collective-permute-done.10 = f32[256,256]{1,0:T(8,128)S(1)} collective-permute-done((f32[256,256]{1,0:T(8,128)S(1)}, f32[256,256]{1,0:T(8,128)S(1)}, u32[]{:S(2)}, u32[]{:S(2)}) %collective-permute-start.10) | collective-permute-done | bytes 262176 | tf_op jit(solution)/shard_map/ppermute | solution.py:168
  31.7 3.5 %collective-permute-start.11 = (f32[256,256]{1,0:T(8,128)S(1)}, f32[256,256]{1,0:T(8,128)S(1)}, u32[]{:S(2)}, u32[]{:S(2)}) collective-permute-start(f32[256,256]{1,0:T(8,128)S(1)} %broadcast_select_fusion.1), channel_id=1, source_target_pairs={{0,8},{1,3},{2,0},{3,11},{4,6},{5,13},{6,5},{7,15},{8,10},{9,1},{1... | collective-permute-start | bytes 786440 | tf_op jit(solution)/shard_map/ppermute | solution.py:168
  35.2 0.0 collective-permute-done.12
  35.2 3.1 %collective-permute-start.14 = (f32[256,256]{1,0:T(8,128)S(1)}, f32[256,256]{1,0:T(8,128)S(1)}, u32[]{:S(2)}, u32[]{:S(2)}) collective-permute-start(f32[256,256]{1,0:T(8,128)S(1)} %broadcast_select_fusion), channel_id=1, source_target_pairs={{0,8},{1,3},{2,0},{3,11},{4,6},{5,13},{6,5},{7,15},{8,10},{9,1},{1... | collective-permute-start | bytes 786440 | tf_op jit(solution)/shard_map/ppermute | solution.py:168
  38.4 1.0 %collective-permute-done.11 = f32[256,256]{1,0:T(8,128)S(1)} collective-permute-done((f32[256,256]{1,0:T(8,128)S(1)}, f32[256,256]{1,0:T(8,128)S(1)}, u32[]{:S(2)}, u32[]{:S(2)}) %collective-permute-start.11) | collective-permute-done | bytes 262176 | tf_op jit(solution)/shard_map/ppermute | solution.py:168
  39.4 0.1 collective-permute-start.13
  39.5 5.5 %collective-permute-done.14 = f32[256,256]{1,0:T(8,128)S(1)} collective-permute-done((f32[256,256]{1,0:T(8,128)S(1)}, f32[256,256]{1,0:T(8,128)S(1)}, u32[]{:S(2)}, u32[]{:S(2)}) %collective-permute-start.14) | collective-permute-done | bytes 262176 | tf_op jit(solution)/shard_map/ppermute | solution.py:168
  45.0 0.0 copy-start.1
  45.0 0.1 collective-permute-start.16
  45.1 0.1 collective-permute-done.13
  45.3 0.7 %copy-done.1 = f32[1,256,256]{2,1,0:T(8,128)S(1)} copy-done((f32[1,256,256]{2,1,0:T(8,128)S(1)}, f32[1,256,256]{2,1,0:T(8,128)}, u32[]{:S(2)}) %copy-start.1) | copy-done | bytes 262168
  46.0 0.3 convolution_bitcast_fusion.1
  46.3 6.2 %collective-permute-start.15 = (f32[256,256]{0,1:T(8,128)S(1)}, f32[256,256]{0,1:T(8,128)S(1)}, u32[]{:S(2)}, u32[]{:S(2)}) collective-permute-start(f32[256,256]{0,1:T(8,128)S(1)} %convolution_bitcast_fusion.1), channel_id=1, source_target_pairs={{0,8},{1,9},{2,10},{3,11},{4,12},{5,13},{6,14},{7,15},{8,0},{9,1},... | collective-permute-start | bytes 786440 | tf_op jit(solution)/shard_map/ppermute | solution.py:168
  52.6 0.1 copy.4
  52.7 0.7 %collective-permute-done.16 = f32[256,256]{1,0:T(8,128)S(1)} collective-permute-done((f32[256,256]{1,0:T(8,128)S(1)}, f32[256,256]{1,0:T(8,128)S(1)}, u32[]{:S(2)}, u32[]{:S(2)}) %collective-permute-start.16) | collective-permute-done | bytes 262176 | tf_op jit(solution)/shard_map/ppermute | solution.py:168
  53.4 0.3 collective-permute-done.15
  53.7 0.4 fusion.3
  54.1 0.1 copy.5
  54.3 3.3 %collective-permute-start.17 = (f32[256,256]{0,1:T(8,128)S(1)}, f32[256,256]{0,1:T(8,128)S(1)}, u32[]{:S(2)}, u32[]{:S(2)}) collective-permute-start(f32[256,256]{0,1:T(8,128)S(1)} %copy.5), channel_id=1, source_target_pairs={{0,8},{1,9},{2,10},{3,11},{4,12},{5,13},{6,14},{7,15},{8,16},{9,17... | collective-permute-start | bytes 786440 | tf_op jit(solution)/shard_map/ppermute | solution.py:168
  57.5 3.3 %collective-permute-done.17 = f32[256,256]{0,1:T(8,128)S(1)} collective-permute-done((f32[256,256]{0,1:T(8,128)S(1)}, f32[256,256]{0,1:T(8,128)S(1)}, u32[]{:S(2)}, u32[]{:S(2)}) %collective-permute-start.17) | collective-permute-done | bytes 262176 | tf_op jit(solution)/shard_map/ppermute | solution.py:168
  60.8 0.3 fusion.4
  61.1 1.4 %collective-permute-start.18 = (f32[256,256]{0,1:T(8,128)S(1)}, f32[256,256]{0,1:T(8,128)S(1)}, u32[]{:S(2)}, u32[]{:S(2)}) collective-permute-start(f32[256,256]{0,1:T(8,128)S(1)} %fusion.4), channel_id=1, source_target_pairs={{0,8},{1,9},{2,10},{3,11},{4,12},{5,13},{6,14},{7,15},{8,0},{9,1},... | collective-permute-start | bytes 786440 | tf_op jit(solution)/shard_map/ppermute | solution.py:168
  62.6 1.2 %collective-permute-done.18 = f32[256,256]{0,1:T(8,128)S(1)} collective-permute-done((f32[256,256]{0,1:T(8,128)S(1)}, f32[256,256]{0,1:T(8,128)S(1)}, u32[]{:S(2)}, u32[]{:S(2)}) %collective-permute-start.18) | collective-permute-done | bytes 262176 | tf_op jit(solution)/shard_map/ppermute | solution.py:168
  63.7 0.1 fusion.1
  63.8 1.1 %convolution_bitcast_fusion = f32[1,256,256]{2,1,0:T(8,128)} fusion(f32[256,256]{0,1:T(8,128)S(1)} %fusion.1, f32[256,256]{1,0:T(8,128)S(1)} %broadcast_select_fusion.4), kind=kOutput, calls=%fused_computation | convolution fusion | flops 100663296 | bytes 786432 | tf_op jit(solution)/shard_map/dot_general | solution.py:137
  64.9 0.8 %copy.7 = f32[1,256,256]{2,1,0:T(8,128)} copy(f32[1,256,256]{1,2,0:T(8,128)S(1)} %bitcast.40) | data formatting | bytes 524288
  (7 shorter events, 0.2 us)
Async XLA Ops:
  0.7 8.3 %copy-start = (f32[1,1,4,256,256]{4,3,2,1,0:T(8,128)S(1)}, f32[1,1,4,256,256]{4,3,2,1,0:T(8,128)}, u32[]{:S(2)}) copy-start(f32[1,1,4,256,256]{4,3,2,1,0:T(8,128)} %param.2) | copy-start | bytes 3145732
  1.7 7.2 %collective-permute-start = (f32[256,256]{1,0:T(8,128)S(1)}, f32[256,256]{1,0:T(8,128)S(1)}, u32[]{:S(2)}, u32[]{:S(2)}) collective-permute-start(f32[256,256]{1,0:T(8,128)S(1)} %dynamic-slice_bitcast_fusion.3), channel_id=1, source_target_pairs={{0,8},{1,0},{2,10},{3,2},{4,12},{5,4},{6,7},{7,6},{8,9},{9,1},{10,... | collective-permute-start | bytes 786440 | tf_op jit(solution)/shard_map/ppermute | solution.py:168
  4.2 10.4 %collective-permute-start.1 = (f32[256,256]{1,0:T(8,128)S(1)}, f32[256,256]{1,0:T(8,128)S(1)}, u32[]{:S(2)}, u32[]{:S(2)}) collective-permute-start(f32[256,256]{1,0:T(8,128)S(1)} %get-tuple-element.48), channel_id=1, source_target_pairs={{0,8},{1,0},{2,10},{3,2},{4,12},{5,4},{6,7},{7,6},{8,9},{9,1},{10,... | collective-permute-start | bytes 786440 | tf_op jit(solution)/shard_map/ppermute | solution.py:168
  4.5 10.6 %collective-permute-start.3 = (f32[256,256]{1,0:T(8,128)S(1)}, f32[256,256]{1,0:T(8,128)S(1)}, u32[]{:S(2)}, u32[]{:S(2)}) collective-permute-start(f32[256,256]{1,0:T(8,128)S(1)} %get-tuple-element.47), channel_id=1, source_target_pairs={{0,8},{1,0},{2,10},{3,2},{4,12},{5,4},{6,14},{7,15},{8,9},{9,1},{1... | collective-permute-start | bytes 786440 | tf_op jit(solution)/shard_map/ppermute | solution.py:168
  5.7 9.7 %collective-permute-start.4 = (f32[256,256]{1,0:T(8,128)S(1)}, f32[256,256]{1,0:T(8,128)S(1)}, u32[]{:S(2)}, u32[]{:S(2)}) collective-permute-start(f32[256,256]{1,0:T(8,128)S(1)} %get-tuple-element.46), channel_id=1, source_target_pairs={{0,8},{1,0},{2,10},{3,2},{4,12},{5,4},{6,14},{7,15},{8,9},{9,1},{1... | collective-permute-start | bytes 786440 | tf_op jit(solution)/shard_map/ppermute | solution.py:168
  11.1 6.1 %collective-permute-start.5 = (f32[256,256]{1,0:T(8,128)S(1)}, f32[256,256]{1,0:T(8,128)S(1)}, u32[]{:S(2)}, u32[]{:S(2)}) collective-permute-start(f32[256,256]{1,0:T(8,128)S(1)} %get-tuple-element.28.o0), channel_id=1, source_target_pairs={{0,2},{1,9},{2,10},{3,1},{4,12},{5,6},{6,4},{7,15},{8,0},{9,11},{1... | collective-permute-start | bytes 786440 | tf_op jit(solution)/shard_map/ppermute | solution.py:168
  15.0 8.2 %collective-permute-start.2 = (f32[256,256]{1,0:T(8,128)S(1)}, f32[256,256]{1,0:T(8,128)S(1)}, u32[]{:S(2)}, u32[]{:S(2)}) collective-permute-start(f32[256,256]{1,0:T(8,128)S(1)} %get-tuple-element.27.o1), channel_id=1, source_target_pairs={{0,2},{1,9},{2,10},{3,1},{4,12},{5,6},{6,4},{7,15},{8,0},{9,11},{1... | collective-permute-start | bytes 786440 | tf_op jit(solution)/shard_map/ppermute | solution.py:168
  15.5 8.8 %collective-permute-start.8 = (f32[256,256]{1,0:T(8,128)S(1)}, f32[256,256]{1,0:T(8,128)S(1)}, u32[]{:S(2)}, u32[]{:S(2)}) collective-permute-start(f32[256,256]{1,0:T(8,128)S(1)} %add.57.o3), channel_id=1, source_target_pairs={{0,2},{1,9},{2,10},{3,1},{4,12},{5,13},{6,14},{7,15},{8,0},{9,11},... | collective-permute-start | bytes 786440 | tf_op jit(solution)/shard_map/ppermute | solution.py:168
  17.1 7.2 %collective-permute-start.7 = (f32[256,256]{1,0:T(8,128)S(1)}, f32[256,256]{1,0:T(8,128)S(1)}, u32[]{:S(2)}, u32[]{:S(2)}) collective-permute-start(f32[256,256]{1,0:T(8,128)S(1)} %get-tuple-element.31.o2), channel_id=1, source_target_pairs={{0,2},{1,9},{2,10},{3,1},{4,12},{5,13},{6,14},{7,15},{8,0},{9,11},... | collective-permute-start | bytes 786440 | tf_op jit(solution)/shard_map/ppermute | solution.py:168
  19.2 8.6 %collective-permute-start.9 = (f32[256,256]{1,0:T(8,128)S(1)}, f32[256,256]{1,0:T(8,128)S(1)}, u32[]{:S(2)}, u32[]{:S(2)}) collective-permute-start(f32[256,256]{1,0:T(8,128)S(1)} %get-tuple-element.38), channel_id=1, source_target_pairs={{0,8},{1,9},{2,10},{3,5},{4,2},{5,13},{6,14},{7,15},{8,0},{9,1},{1... | collective-permute-start | bytes 786440 | tf_op jit(solution)/shard_map/ppermute | solution.py:168
  23.5 6.3 %collective-permute-start.6 = (f32[256,256]{1,0:T(8,128)S(1)}, f32[256,256]{1,0:T(8,128)S(1)}, u32[]{:S(2)}, u32[]{:S(2)}) collective-permute-start(f32[256,256]{1,0:T(8,128)S(1)} %shard_map.45), channel_id=1, source_target_pairs={{0,8},{1,9},{2,10},{3,5},{4,2},{5,13},{6,14},{7,15},{8,0},{9,1},{1... | collective-permute-start | bytes 786440 | tf_op jit(solution)/shard_map/ppermute | solution.py:168
  30.1 1.6 %collective-permute-start.10 = (f32[256,256]{1,0:T(8,128)S(1)}, f32[256,256]{1,0:T(8,128)S(1)}, u32[]{:S(2)}, u32[]{:S(2)}) collective-permute-start(f32[256,256]{1,0:T(8,128)S(1)} %shard_map.48), channel_id=1, source_target_pairs={{0,8},{1,9},{2,4},{3,11},{4,12},{5,3},{6,14},{7,15},{8,0},{9,1},{1... | collective-permute-start | bytes 786440 | tf_op jit(solution)/shard_map/ppermute | solution.py:168
  30.2 5.0 %collective-permute-start.12 = (f32[256,256]{1,0:T(8,128)S(1)}, f32[256,256]{1,0:T(8,128)S(1)}, u32[]{:S(2)}, u32[]{:S(2)}) collective-permute-start(f32[256,256]{1,0:T(8,128)S(1)} %get-tuple-element.40), channel_id=1, source_target_pairs={{0,8},{1,9},{2,4},{3,11},{4,12},{5,3},{6,14},{7,15},{8,0},{9,1},{1... | collective-permute-start | bytes 786440 | tf_op jit(solution)/shard_map/ppermute | solution.py:168
  31.7 7.6 %collective-permute-start.11 = (f32[256,256]{1,0:T(8,128)S(1)}, f32[256,256]{1,0:T(8,128)S(1)}, u32[]{:S(2)}, u32[]{:S(2)}) collective-permute-start(f32[256,256]{1,0:T(8,128)S(1)} %broadcast_select_fusion.1), channel_id=1, source_target_pairs={{0,8},{1,3},{2,0},{3,11},{4,6},{5,13},{6,5},{7,15},{8,10},{9,1},{1... | collective-permute-start | bytes 786440 | tf_op jit(solution)/shard_map/ppermute | solution.py:168
  35.2 9.7 %collective-permute-start.14 = (f32[256,256]{1,0:T(8,128)S(1)}, f32[256,256]{1,0:T(8,128)S(1)}, u32[]{:S(2)}, u32[]{:S(2)}) collective-permute-start(f32[256,256]{1,0:T(8,128)S(1)} %broadcast_select_fusion), channel_id=1, source_target_pairs={{0,8},{1,3},{2,0},{3,11},{4,6},{5,13},{6,5},{7,15},{8,10},{9,1},{1... | collective-permute-start | bytes 786440 | tf_op jit(solution)/shard_map/ppermute | solution.py:168
  39.4 5.8 %collective-permute-start.13 = (f32[256,256]{1,0:T(8,128)S(1)}, f32[256,256]{1,0:T(8,128)S(1)}, u32[]{:S(2)}, u32[]{:S(2)}) collective-permute-start(f32[256,256]{1,0:T(8,128)S(1)} %broadcast_select_fusion.3), channel_id=1, source_target_pairs={{0,1},{1,9},{2,3},{3,11},{4,5},{5,13},{6,7},{7,6},{8,0},{9,8},{10,... | collective-permute-start | bytes 786440 | tf_op jit(solution)/shard_map/ppermute | solution.py:168
  45.0 1.0 %copy-start.1 = (f32[1,256,256]{2,1,0:T(8,128)S(1)}, f32[1,256,256]{2,1,0:T(8,128)}, u32[]{:S(2)}) copy-start(f32[1,256,256]{2,1,0:T(8,128)} %param.3) | copy-start | bytes 786436
  45.0 8.4 %collective-permute-start.16 = (f32[256,256]{1,0:T(8,128)S(1)}, f32[256,256]{1,0:T(8,128)S(1)}, u32[]{:S(2)}, u32[]{:S(2)}) collective-permute-start(f32[256,256]{1,0:T(8,128)S(1)} %broadcast_select_fusion.2), channel_id=1, source_target_pairs={{0,1},{1,9},{2,3},{3,11},{4,5},{5,13},{6,7},{7,6},{8,0},{9,8},{10,... | collective-permute-start | bytes 786440 | tf_op jit(solution)/shard_map/ppermute | solution.py:168
  46.3 7.4 %collective-permute-start.15 = (f32[256,256]{0,1:T(8,128)S(1)}, f32[256,256]{0,1:T(8,128)S(1)}, u32[]{:S(2)}, u32[]{:S(2)}) collective-permute-start(f32[256,256]{0,1:T(8,128)S(1)} %convolution_bitcast_fusion.1), channel_id=1, source_target_pairs={{0,8},{1,9},{2,10},{3,11},{4,12},{5,13},{6,14},{7,15},{8,0},{9,1},... | collective-permute-start | bytes 786440 | tf_op jit(solution)/shard_map/ppermute | solution.py:168
  54.3 6.6 %collective-permute-start.17 = (f32[256,256]{0,1:T(8,128)S(1)}, f32[256,256]{0,1:T(8,128)S(1)}, u32[]{:S(2)}, u32[]{:S(2)}) collective-permute-start(f32[256,256]{0,1:T(8,128)S(1)} %copy.5), channel_id=1, source_target_pairs={{0,8},{1,9},{2,10},{3,11},{4,12},{5,13},{6,14},{7,15},{8,16},{9,17... | collective-permute-start | bytes 786440 | tf_op jit(solution)/shard_map/ppermute | solution.py:168
  61.1 2.6 %collective-permute-start.18 = (f32[256,256]{0,1:T(8,128)S(1)}, f32[256,256]{0,1:T(8,128)S(1)}, u32[]{:S(2)}, u32[]{:S(2)}) collective-permute-start(f32[256,256]{0,1:T(8,128)S(1)} %fusion.4), channel_id=1, source_target_pairs={{0,8},{1,9},{2,10},{3,11},{4,12},{5,13},{6,14},{7,15},{8,0},{9,1},... | collective-permute-start | bytes 786440 | tf_op jit(solution)/shard_map/ppermute | solution.py:168

commit v2 on v0

v2 whole, which is shorter than its diff:
```python
import functools

import jax
import jax.numpy as jnp
from jax import lax
from jax.experimental import pallas as pl
from jax.experimental.pallas import tpu as pltpu
from jax.sharding import PartitionSpec as P

AXES = ("depth", "slab")


def split(value):
    high = value.astype(jnp.bfloat16)
    return high, (value - high.astype(jnp.float32)).astype(jnp.bfloat16)


def product(left, right):
    left_high, left_low = split(left)
    right_high, right_low = split(right)
    dot = functools.partial(jnp.dot, preferred_element_type=jnp.float32)
    return dot(left_high, right_high) + (dot(left_high, right_low) + dot(left_low, right_high))


def inverse(coupling, power, total):
    order = coupling.shape[0]
    row = lax.broadcasted_iota(jnp.int32, (order, order), 0)
    column = lax.broadcasted_iota(jnp.int32, (order, order), 1)
    result = coupling + jnp.where(row == column, 1.0, 0.0)
    for _ in range(2):
        coupling = product(coupling, coupling)
        result = result + product(result, coupling)
    power[...] = coupling
    total[...] = result

    def more(state):
        turn, size = state
        return jnp.logical_and(turn < 40, size > 2.0**-24)

    def step(state):
        turn, _ = state
        squared = product(power[...], power[...])
        total[...] += product(total[...], squared)
        power[...] = squared
        return turn + 1, jnp.sum(squared * squared)

    lax.while_loop(more, step, (0, jnp.sum(coupling * coupling)))
    return total[...]


def call(body, blocks, outs, solves=False):
    order = blocks[0].shape[-1]
    square = jax.ShapeDtypeStruct((order, order), jnp.float32)
    vmem = pl.BlockSpec(memory_space=pltpu.VMEM)
    results = pl.pallas_call(
        body,
        out_shape=[square] * outs,
        in_specs=[vmem] * len(blocks),
        out_specs=[vmem] * outs,
        scratch_shapes=[pltpu.VMEM((order, order), jnp.float32)] * 2 if solves else [],
        compiler_params=pltpu.CompilerParams(vmem_limit_bytes=12 * 2**20),
    )(*blocks)
    return list(results)


def first_step(marks, own, c0, out0, down, back, up, power, total):
    turned = 2 * marks()[0]
    refl, trans, behind, upward = own[turned], own[1 + turned], own[2 - turned], own[3 - turned]
    solver = inverse(product(behind, c0[...]), power, total)
    down[...] = product(solver, trans)
    back[...] = product(solver, behind)
    bounce = product(upward, c0[...])
    up[...] = upward + product(bounce, back[...])
    out0[...] = refl + product(bounce, down[...])


def second_step(marks, down, back, up, c1, out1, kept):
    turned = marks()[0] == 1
    out1[...] = product(jnp.where(turned, up[...], c1[...]), jnp.where(turned, c1[...], down[...]))
    kept[...] = product(jnp.where(turned, back[...], c1[...]), jnp.where(turned, c1[...], back[...]))


def third_step(marks, down, up, kept, c2, out2, rest):
    turned = marks()[0] == 1
    out2[...] = product(jnp.where(turned, c2[...], up[...]), jnp.where(turned, down[...], c2[...]))
    rest[...] = product(jnp.where(turned, c2[...], kept[...]), jnp.where(turned, kept[...], c2[...]))


def ordered(turned, first, last):
    return jnp.where(turned, last[...], first[...]), jnp.where(turned, first[...], last[...])


def lower_run(marks, o0, o1, o2, o3, refl_b, refl, down, power, total):
    mark = marks()
    refl_a, back_a = ordered(mark[0] == 1, o0, o3)
    solver = inverse(product(back_a, refl_b[...]), power, total)
    down[...] = product(solver, o1[...])
    refl[...] = refl_a + product(product(o2[...], refl_b[...]), down[...])


def upper_run(marks, o0, o1, o2, o3, c0, c1, c3, back, trans, solver, power, total):
    mark = marks()
    refl_b, back_b = ordered(mark[0] == 1, o0, o3)
    _, back_a = ordered(mark[1] == 1, c0, c3)
    solver[...] = inverse(product(back_a, refl_b), power, total)
    through = product(o1[...], solver[...])
    back[...] = back_b + product(through, product(back_a, o2[...]))
    trans[...] = product(through, c1[...])


def whole_down(back_a, trans_a, refl_b, down, power, total):
    down[...] = product(inverse(product(back_a[...], refl_b[...]), power, total), trans_a[...])


def whole_refl(marks, o0, o2, o3, c0, c1, c2, c3, solver, low_refl, down, refl):
    mark = marks()
    refl_b, _ = ordered(mark[0] == 1, o0, o3)
    refl_a, back_a = ordered(mark[1] == 1, c0, c3)
    first = refl_a + product(c2[...], product(refl_b, product(solver[...], c1[...])))
    turned_up = product(solver[...], product(back_a, o2[...]))
    up = product(c2[...], o2[...] + product(refl_b, turned_up))
    refl[...] = first + product(up, product(low_refl[...], down[...]))


def any_run(marks, o0, o1, o2, o3, c0, c1, c2, c3, refl, trans, up, back, power, total):
    mark = marks()
    refl_own, back_own = ordered(mark[0] == 1, o0, o3)
    refl_came, back_came = ordered(mark[1] == 1, c0, c3)
    own, came = (refl_own, o1[...], o2[...], back_own), (refl_came, c1[...], c2[...], back_came)
    below = mark[2] == 1
    refl_a, trans_a, up_a, back_a = [jnp.where(below, c, o) for o, c in zip(own, came)]
    refl_b, trans_b, up_b, back_b = [jnp.where(below, o, c) for o, c in zip(own, came)]
    solver = inverse(product(back_a, refl_b), power, total)
    down = product(solver, trans_a)
    bounce = product(up_a, refl_b)
    turned_up = product(solver, product(back_a, up_b))
    back[...] = back_b + product(trans_b, turned_up)
    trans[...] = product(trans_b, down)
    up[...] = product(up_a, up_b) + product(bounce, turned_up)
    refl[...] = refl_a + product(bounce, down)


def times(left, right, out):
    out[...] = product(left[...], right[...])


def times_transpose(rows, matrix):
    return lax.dot_general(
        rows, matrix, (((1,), (1,)), ((), ())), precision=lax.Precision.HIGH, preferred_element_type=jnp.float32
    )


def filled(useful, groups, count):
    def mate(device):
        return (device[0] ^ 1, device[1])

    pairs = dict(useful)
    targets = set(pairs.values())
    devices = [(g, s) for g in range(groups) for s in range(count)]
    for device in devices:
        if device not in pairs and mate(device) not in targets:
            pairs[device] = mate(device)
    spare = set(devices) - set(pairs.values())
    for source, target in useful.items():
        if mate(target) not in pairs and mate(source) in spare:
            pairs[mate(target)] = mate(source)
            spare.discard(mate(source))
    return pairs


def shards(slabs, incident):
    groups, count = lax.axis_size("depth"), lax.axis_size("slab")
    group, place = lax.axis_index("depth"), lax.axis_index("slab")
    levels = count.bit_length() - 1
    parity = group % 2
    pair, side = place // 2, place % 2
    pairs = count // 2

    def send(block, useful, fill=True):
        route = filled(useful, groups, count) if fill else useful
        route = sorted((a[0] * count + a[1], b[0] * count + b[1]) for a, b in route.items())
        return lax.ppermute(block, AXES, route)

    def turn(g, k):
        return g % 2 if k < pairs - 1 else 0

    def home(g, k):
        return (g, 2 * k + turn(g, k))

    def guest(g, k):
        return (g, 2 * k + 1 - turn(g, k))

    turned = jnp.where(pair == pairs - 1, 0, parity)
    owners = [list(range(pairs))]
    merges = []
    while len(owners[-1]) > 1:
        now, kept = owners[-1], []
        merges.append([])
        for k in range(0, len(now), 2):
            below = len(now) > 2 and k // 2 % 2 == 0
            merges[-1].append((now[k], now[k + 1], True) if below else (now[k + 1], now[k], False))
            kept.append(merges[-1][-1][1])
        owners.append(kept)

    def routes(level, late=False):
        return {
            home(g, source): home(g, target)
            for source, target, below in merges[level - 1]
            if below or not late
            for g in range(groups)
        }

    def is_one(some):
        return functools.reduce(jnp.logical_or, [pair == k for k in some], False)

    def marks(level):
        odd, at = lax.axis_index("depth") % 2, lax.axis_index("slab") // 2

        def among(some):
            return functools.reduce(jnp.maximum, [(at == k).astype(jnp.int32) for k in some], jnp.int32(0))

        below = among([m[1] for m in merges[max(level, 1) - 1] if m[2]])
        if level > 1:
            return jnp.int32(0), jnp.int32(0), below
        return (1 - among([pairs - 1])) * odd, among([m[1] for m in merges[0] if m[0] < pairs - 1]) * odd, below

    own = slabs[0, 0]
    injected = incident[0]
    spread = {guest(g, k): home(g, k) for g in range(groups) for k in range(pairs)}
    spread_late = {guest(g, k): home(g, k) for g in range(groups) for k in range(pairs - 1)}
    chosen = lax.dynamic_index_in_dim(own, 2 * turned, keepdims=False)
    chosen, after = lax.optimization_barrier((chosen, own))
    came = [send(chosen, spread), send(after[1], spread), send(after[3], spread_late)]
    came.append(send(lax.dynamic_index_in_dim(after, 2 - 2 * turned, keepdims=False), spread_late))
    first = functools.partial(marks, 1)
    split_level = levels - 2
    late = split_level == 1
    out0, down, back, up = call(functools.partial(first_step, first), [own, came[0]], 4, True)
    sent = [send(out0, routes(1))]
    out1, kept = call(functools.partial(second_step, first), [down, back, up, came[1]], 2)
    sent.append(send(out1, routes(1)))
    out2, rest = call(functools.partial(third_step, first), [down, up, kept, came[2]], 2)
    sent.append(send(out2, routes(1, late)))
    out3 = came[3] + rest
    sent.append(send(out3, routes(1, late)))
    state = [out0, out1, out2, out3]
    for level in range(1, split_level):
        state = call(functools.partial(any_run, functools.partial(marks, level)), state + sent, 4, True)
        late = level + 1 == split_level
        sent = [send(block, routes(level + 1, late and i > 1)) for i, block in enumerate(state)]

    top = routes(levels - 1)
    split_marks = functools.partial(marks, split_level)
    low_refl, low_down = call(functools.partial(lower_run, split_marks), state + sent[:1], 2, True)
    low_refl = send(low_refl, top)
    (low_trans,) = call(times, [sent[1], low_down], 1)
    low_trans = send(low_trans, top)
    back_a, trans_a, solver = call(functools.partial(upper_run, split_marks), state + [sent[0], sent[1], sent[3]], 3, True)
    back_a, _ = lax.optimization_barrier((back_a, sent[2]))
    (down,) = call(whole_down, [back_a, trans_a, low_refl], 1, True)
    (trans,) = call(times, [low_trans, down], 1)
    (refl,) = call(functools.partial(whole_refl, split_marks), [state[0], state[2], state[3]] + sent + [solver, low_refl, down], 1)

    def line(g, k):
        return (g, 2 * k + g % 2)

    def hand_out(block):
        level = levels - 1
        while level > 0:
            steps = []
            for far, near, _ in merges[level - 1]:
                if level > 1:
                    below = {m[1]: m[0] for m in merges[level - 2]}
                    steps.append([(near, below[far]), (near, far), (near, below[near])])
                else:
                    steps.append([(near, far)])
            got = block
            for step in zip(*steps):
                fresh = is_one([target for _, target in step])
                route = {line(g, a): line(g, b) for a, b in step for g in range(groups)}
                got = jnp.where(fresh, send(block, route, False), got)
            block = got
            level -= 2
        return block

    trans, _ = lax.optimization_barrier((hand_out(trans), refl))
    refl = hand_out(refl)

    across = {}
    for g in range(groups):
        for k in range(pairs):
            across[line(g, k)] = (g | 1, 2 * k + 1 - g % 2)
    swap = {(g, s): (g ^ 1, s) for g in range(groups) for s in range(count)}
    crossed = send(trans, across, False)
    trans_even = jnp.where(side == 1, crossed, send(trans, swap))
    trans_odd = jnp.where(side == 1, trans, crossed)
    even = send(injected, swap)
    opposite = {line(g, k): (g, line(g, k)[1] ^ 1) for g in range(groups) for k in range(pairs)}
    spread_refl = jnp.where(side == parity, refl, send(refl, opposite))
    handed = jnp.zeros_like(injected)
    for j in range(0, groups, 2):
        field_even = even + handed
        field_odd = injected + times_transpose(field_even, trans_even)
        if j + 2 < groups:
            leaving, _ = lax.optimization_barrier((times_transpose(field_odd, trans_odd), refl))
            arriving = send(leaving, {(j + 1, s): (j + 3, s) for s in range(count)})
            arriving, _ = lax.optimization_barrier((arriving, spread_refl))
            handed = jnp.where(group // 2 == j // 2 + 1, arriving, handed)
    field = jnp.where(parity == 1, field_odd, send(field_even, swap))
    bounced = times_transpose(field, spread_refl)
    return (field[None], bounced[None])


def solution(mesh):
    placed = (P("depth", "slab", None, None, None), P("depth", "slab", None))
    return jax.shard_map(
        shards,
        mesh=mesh,
        in_specs=placed,
        out_specs=(P("depth", "slab", None), P("depth", "slab", None)),
        check_vma=False,
    )
```

time: 78.9 us -> 58.9 us (0.75)
  waiting for transfers between devices: 49.9 us -> 11.2 us
  starting transfers between devices: 12.7 us -> 30.9 us
    ppermute x19 -> x22, waiting for transfers between devices: 49.9 us -> 11.2 us  [send(): return lax.ppermute(block, AXES, route)]
    ppermute x19 -> x22, starting transfers between devices: 12.7 us -> 30.9 us  [send(): return lax.ppermute(block, AXES, route)]
    unnamed x6, local copies, waits for them, and re-layouts: 0.97 us -> 0.02 us
    squeeze x1 -> x2, local copies, waits for them, and re-layouts: 1.35 us -> 2.22 us  [the longest x1 1.16 us: shards(): lax.dynamic_index_in_dim(after, 2 - 2 * turned, keepdims=False)]
    pallas_call x6 -> x9, Pallas kernels: 10.5 us -> 11.1 us  [call(): pl.pallas_call(body, out_shape=[square] * outs, in_specs=[vmem] * len(blo...]
  transfers between devices with their start and end apart: 19 -> 22, of which waited for: 11 -> 5; matrix products, arithmetic and copies ran while one was open for 2% -> 3% of each run, Pallas kernels for 11% -> 18%
where the time goes in v2:
time: 58.9 us; the launch traced here: 58.6 us
  starting transfers between devices  30.9 us (52%)
  waiting for transfers between devices  11.2 us (19%)
  Pallas kernels  11.1 us (19%)
  local copies, waits for them, and re-layouts  2.24 us (4%)
  matrix products  2.07 us (4%)
  between operations  0.97 us (2%)
    ppermute x22, starting transfers between devices, send(): return lax.ppermute(block, AXES, route)  30.9 us
    ppermute x22, waiting for transfers between devices, send(): return lax.ppermute(block, AXES, route)  11.2 us
    pallas_call x9, Pallas kernels, call(): pl.pallas_call(body, out_shape=[square] * outs, in_specs=[vmem] * len(blo...  11.1 us
    dot_general x4, matrix products, times_transpose(): lax.dot_general(rows, matrix, (((1,), (1,)), ((), ())), precision=lax.Pre...  2.07 us
  transfers between devices with their start and end apart: 22, of which 5 were waited for; matrix products, arithmetic and copies ran while one was open for 3% of the time, Pallas kernels for 18%

profile of v2, /device:TPU:25, one launch (start us, length us, event | category | flops | bytes accessed | tf_op | source)
XLA Modules:
  0.0 58.6 jit_solution(14264841209451832774)
XLA Ops:
  0.7 0.0 copy-start
  0.7 1.1 %dynamic-slice_bitcast_fusion.1 = f32[256,256]{1,0:T(8,128)S(1)} fusion(f32[1,1,4,256,256]{4,3,2,1,0:T(8,128)} %param.2, s32[]{:T(128)S(6)} %select_n.98), kind=kLoop, calls=%fused_computation.13 | loop fusion | bytes 524292 | tf_op jit(solution)/shard_map/jit(dynamic_index_in_dim)/squeeze | solution.py:231
  1.7 1.3 %collective-permute-start.1 = (f32[256,256]{1,0:T(8,128)S(1)}, f32[256,256]{1,0:T(8,128)S(1)}, u32[]{:S(2)}, u32[]{:S(2)}) collective-permute-start(f32[256,256]{1,0:T(8,128)S(1)} %dynamic-slice_bitcast_fusion.1), channel_id=1, source_target_pairs={{0,8},{1,0},{2,10},{3,2},{4,12},{5,4},{6,7},{7,6},{8,9},{9,1},{10,... | collective-permute-start | bytes 786440 | tf_op jit(solution)/shard_map/ppermute | solution.py:182
  3.0 1.2 %dynamic-slice_bitcast_fusion = (f32[256,256]{1,0:T(8,128)S(1)}, f32[256,256]{1,0:T(8,128)S(1)}, f32[256,256]{1,0:T(8,128)S(1)}) fusion(f32[4,256,256]{2,1,0:T(8,128)} %bitcast.24, s32[]{:T(128)S(6)} %select_n.99), kind=kLoop, calls=%fused_computation.10 | loop fusion | bytes 1572868 | tf_op jit(solution)/shard_map/jit(dynamic_index_in_dim)/squeeze | solution.py:234
  4.2 0.3 collective-permute-start.2
  4.5 1.2 %collective-permute-start.4 = (f32[256,256]{1,0:T(8,128)S(1)}, f32[256,256]{1,0:T(8,128)S(1)}, u32[]{:S(2)}, u32[]{:S(2)}) collective-permute-start(f32[256,256]{1,0:T(8,128)S(1)} %get-tuple-element.41), channel_id=1, source_target_pairs={{0,8},{1,0},{2,10},{3,2},{4,12},{5,4},{6,14},{7,15},{8,9},{9,1},{1... | collective-permute-start | bytes 786440 | tf_op jit(solution)/shard_map/ppermute | solution.py:182
  5.7 0.0 collective-permute-start.5
  5.7 3.3 %collective-permute-done.1.c0 = f32[256,256]{1,0:T(8,128)S(1)} collective-permute-done((f32[256,256]{1,0:T(8,128)S(1)}, f32[256,256]{1,0:T(8,128)S(1)}, u32[]{:S(2)}, u32[]{:S(2)}) %collective-permute-start.1) | collective-permute-done | bytes 262176 | tf_op jit(solution)/shard_map/ppermute | solution.py:182
  9.0 2.1 %shard_map.41 = (f32[256,256]{1,0:T(8,128)S(1)}, f32[256,256]{1,0:T(8,128)S(1)}, f32[256,256]{1,0:T(8,128)S(1)}, f32[256,256]{1,0:T(8,128)S(1)}) custom-call(f32[4,256,256]{2,1,0:T(8,128)S(1)} %bitcast.25, f32[256,256]{1,0:T(8,128)S(1)} %collective-permute-done.1.c0), custom_call_target="tpu_custom_call" | custom-call | tf_op jit(solution)/shard_map/pallas_call | solution.py:55
  11.1 0.1 collective-permute-start.6
  11.2 3.4 %collective-permute-done.2.c1 = f32[256,256]{1,0:T(8,128)S(1)} collective-permute-done((f32[256,256]{1,0:T(8,128)S(1)}, f32[256,256]{1,0:T(8,128)S(1)}, u32[]{:S(2)}, u32[]{:S(2)}) %collective-permute-start.2) | collective-permute-done | bytes 262176 | tf_op jit(solution)/shard_map/ppermute | solution.py:182
  14.6 0.4 shard_map.42
  15.0 0.1 collective-permute-start.3
  15.1 0.0 collective-permute-done.4.c2
  15.1 0.4 shard_map.43
  15.5 0.0 collective-permute-done.5
  15.6 1.6 %collective-permute-start.8 = (f32[256,256]{1,0:T(8,128)S(1)}, f32[256,256]{1,0:T(8,128)S(1)}, u32[]{:S(2)}, u32[]{:S(2)}) collective-permute-start(f32[256,256]{1,0:T(8,128)S(1)} %add.33.o3), channel_id=1, source_target_pairs={{0,2},{1,9},{2,10},{3,1},{4,12},{5,13},{6,14},{7,15},{8,0},{9,11},... | collective-permute-start | bytes 786440 | tf_op jit(solution)/shard_map/ppermute | solution.py:182
  17.2 0.1 collective-permute-start.9
  17.2 0.0 collective-permute-done.6.refl_b.c0
  17.2 2.0 %shard_map.44 = (f32[256,256]{1,0:T(8,128)S(1)}, f32[256,256]{1,0:T(8,128)S(1)}) custom-call(f32[256,256]{1,0:T(8,128)S(1)} %get-tuple-element.27.o0, f32[256,256]{1,0:T(8,128)S(1)} %get-tuple-element.26.o1, f32[256,256]{1,0:T(8,128)S(1)} %get-tuple-element.29.o2, f32[256,256]{1,0:T(8,128)S(1)} %add.33.o3, f32[256,256]{1,0:T(8,128)S(1)} %collective-permute-done.6.refl_b.c0), custom_call_target="tpu_custom_call" | custom-call | tf_op jit(solution)/shard_map/pallas_call | solution.py:55
  19.3 3.9 %collective-permute-start.10 = (f32[256,256]{1,0:T(8,128)S(1)}, f32[256,256]{1,0:T(8,128)S(1)}, u32[]{:S(2)}, u32[]{:S(2)}) collective-permute-start(f32[256,256]{1,0:T(8,128)S(1)} %get-tuple-element.35), channel_id=1, source_target_pairs={{0,8},{1,9},{2,10},{3,5},{4,2},{5,13},{6,14},{7,15},{8,0},{9,1},{1... | collective-permute-start | bytes 786440 | tf_op jit(solution)/shard_map/ppermute | solution.py:182
  23.2 0.0 collective-permute-done.3.left.c1
  23.2 0.3 shard_map.45
  23.5 0.8 %collective-permute-start.7 = (f32[256,256]{1,0:T(8,128)S(1)}, f32[256,256]{1,0:T(8,128)S(1)}, u32[]{:S(2)}, u32[]{:S(2)}) collective-permute-start(f32[256,256]{1,0:T(8,128)S(1)} %shard_map.45), channel_id=1, source_target_pairs={{0,8},{1,9},{2,10},{3,5},{4,2},{5,13},{6,14},{7,15},{8,0},{9,1},{1... | collective-permute-start | bytes 786440 | tf_op jit(solution)/shard_map/ppermute | solution.py:182
  24.3 0.0 collective-permute-done.8.c3
  24.3 2.0 %shard_map.46 = (f32[256,256]{1,0:T(8,128)S(1)}, f32[256,256]{1,0:T(8,128)S(1)}, f32[256,256]{1,0:T(8,128)S(1)}) custom-call(f32[256,256]{1,0:T(8,128)S(1)} %get-tuple-element.27.o0, f32[256,256]{1,0:T(8,128)S(1)} %get-tuple-element.26.o1, f32[256,256]{1,0:T(8,128)S(1)} %get-tuple-element.29.o2, f32[256,256]{1,0:T(8,128)S(1)} %add.33.o3, ...), custom_call_target="tpu_custom_call" | custom-call | tf_op jit(solution)/shard_map/pallas_call | solution.py:55
  26.3 0.0 collective-permute-done.9.c2
  26.3 0.0 collective-permute-done.10.refl_b.low_refl
  26.3 1.5 %shard_map.47.right.down = f32[256,256]{1,0:T(8,128)S(1)} custom-call(f32[256,256]{1,0:T(8,128)S(1)} %get-tuple-element.33.back_a, f32[256,256]{1,0:T(8,128)S(1)} %get-tuple-element.34.trans_a, f32[256,256]{1,0:T(8,128)S(1)} %collective-permute-done.10.refl_b.low_refl), custom_call_target="tpu_custom_call" | custom-call | tf_op jit(solution)/shard_map/pallas_call | solution.py:55
  27.8 0.0 collective-permute-done.7.left
  27.8 0.3 shard_map.48
  28.1 0.7 %collective-permute-start.11 = (f32[256,256]{1,0:T(8,128)S(1)}, f32[256,256]{1,0:T(8,128)S(1)}, u32[]{:S(2)}, u32[]{:S(2)}) collective-permute-start(f32[256,256]{1,0:T(8,128)S(1)} %shard_map.48), channel_id=1, source_target_pairs={{2,0},{11,9},{18,16},{27,25}} | collective-permute-start | bytes 786440 | tf_op jit(solution)/shard_map/ppermute | solution.py:182
  28.8 0.7 %collective-permute-start.12 = (f32[256,256]{1,0:T(8,128)S(1)}, f32[256,256]{1,0:T(8,128)S(1)}, u32[]{:S(2)}, u32[]{:S(2)}) collective-permute-start(f32[256,256]{1,0:T(8,128)S(1)} %shard_map.48), channel_id=1, source_target_pairs={{2,4},{11,13},{18,20},{27,29}} | collective-permute-start | bytes 786440 | tf_op jit(solution)/shard_map/ppermute | solution.py:182
  29.5 0.7 %collective-permute-start.13 = (f32[256,256]{1,0:T(8,128)S(1)}, f32[256,256]{1,0:T(8,128)S(1)}, u32[]{:S(2)}, u32[]{:S(2)}) collective-permute-start(f32[256,256]{1,0:T(8,128)S(1)} %shard_map.48), channel_id=1, source_target_pairs={{2,6},{11,15},{18,22},{27,31}} | collective-permute-start | bytes 786440 | tf_op jit(solution)/shard_map/ppermute | solution.py:182
  30.2 0.0 copy-start.1
  30.2 2.0 %shard_map.49 = f32[256,256]{1,0:T(8,128)S(1)} custom-call(f32[256,256]{1,0:T(8,128)S(1)} %get-tuple-element.27.o0, f32[256,256]{1,0:T(8,128)S(1)} %get-tuple-element.29.o2, f32[256,256]{1,0:T(8,128)S(1)} %add.33.o3, f32[256,256]{1,0:T(8,128)S(1)} %collective-permute-done.6.refl_b.c0, f32[256,256]{1,0:T(8,128)S(1)} %collective-permute-done.3.left.c1, ...), custom_call_target="tpu_custom_call" | custom-call | tf_op jit(solution)/shard_map/pallas_call | solution.py:55
  32.2 0.7 %collective-permute-start.16 = (f32[256,256]{1,0:T(8,128)S(1)}, f32[256,256]{1,0:T(8,128)S(1)}, u32[]{:S(2)}, u32[]{:S(2)}) collective-permute-start(f32[256,256]{1,0:T(8,128)S(1)} %shard_map.49), channel_id=1, source_target_pairs={{2,0},{11,9},{18,16},{27,25}} | collective-permute-start | bytes 786440 | tf_op jit(solution)/shard_map/ppermute | solution.py:182
  32.9 0.7 %collective-permute-start = (f32[256,256]{1,0:T(8,128)S(1)}, f32[256,256]{1,0:T(8,128)S(1)}, u32[]{:S(2)}, u32[]{:S(2)}) collective-permute-start(f32[256,256]{1,0:T(8,128)S(1)} %bitcast.26), channel_id=1, source_target_pairs={{0,8},{1,9},{2,10},{3,11},{4,12},{5,13},{6,14},{7,15},{8,0},{9,1},... | collective-permute-start | bytes 786440 | tf_op jit(solution)/shard_map/ppermute | solution.py:182
  33.6 0.0 collective-permute-done.11
  33.6 0.7 %collective-permute-start.17 = (f32[256,256]{1,0:T(8,128)S(1)}, f32[256,256]{1,0:T(8,128)S(1)}, u32[]{:S(2)}, u32[]{:S(2)}) collective-permute-start(f32[256,256]{1,0:T(8,128)S(1)} %shard_map.49), channel_id=1, source_target_pairs={{2,4},{11,13},{18,20},{27,29}} | collective-permute-start | bytes 786440 | tf_op jit(solution)/shard_map/ppermute | solution.py:182
  34.3 0.0 collective-permute-done.12
  34.3 0.7 %collective-permute-start.18 = (f32[256,256]{1,0:T(8,128)S(1)}, f32[256,256]{1,0:T(8,128)S(1)}, u32[]{:S(2)}, u32[]{:S(2)}) collective-permute-start(f32[256,256]{1,0:T(8,128)S(1)} %shard_map.49), channel_id=1, source_target_pairs={{2,6},{11,15},{18,22},{27,31}} | collective-permute-start | bytes 786440 | tf_op jit(solution)/shard_map/ppermute | solution.py:182
  35.0 0.0 collective-permute-done.13
  35.0 0.1 select_select_fusion.1
  35.1 1.3 %collective-permute-start.14 = (f32[256,256]{1,0:T(8,128)S(1)}, f32[256,256]{1,0:T(8,128)S(1)}, u32[]{:S(2)}, u32[]{:S(2)}) collective-permute-start(f32[256,256]{1,0:T(8,128)S(1)} %select_select_fusion.1), channel_id=1, source_target_pairs={{0,9},{2,11},{4,13},{6,15},{9,8},{11,10},{13,12},{15,14},{16,25},{... | collective-permute-start | bytes 786440 | tf_op jit(solution)/shard_map/ppermute | solution.py:182
  36.4 0.0 collective-permute-done.16
  36.4 7.7 %collective-permute-start.15 = (f32[256,256]{1,0:T(8,128)S(1)}, f32[256,256]{1,0:T(8,128)S(1)}, u32[]{:S(2)}, u32[]{:S(2)}) collective-permute-start(f32[256,256]{1,0:T(8,128)S(1)} %select_select_fusion.1), channel_id=1, source_target_pairs={{0,8},{1,9},{2,10},{3,11},{4,12},{5,13},{6,14},{7,15},{8,0},{9,1},... | collective-permute-start | bytes 786440 | tf_op jit(solution)/shard_map/ppermute | solution.py:182
  44.1 0.0 collective-permute-done.17
  44.1 0.0 collective-permute-done.18
  44.1 0.1 select_select_fusion
  44.2 4.6 %collective-permute-start.20 = (f32[256,256]{1,0:T(8,128)S(1)}, f32[256,256]{1,0:T(8,128)S(1)}, u32[]{:S(2)}, u32[]{:S(2)}) collective-permute-start(f32[256,256]{1,0:T(8,128)S(1)} %select_select_fusion), channel_id=1, source_target_pairs={{0,1},{1,9},{2,3},{3,11},{4,5},{5,13},{6,7},{7,15},{8,0},{9,8},{10... | collective-permute-start | bytes 786440 | tf_op jit(solution)/shard_map/ppermute | solution.py:182
  48.8 0.0 collective-permute-done
  48.8 0.0 collective-permute-done.14
  48.8 0.0 collective-permute-done.15
  48.8 0.3 fusion.1
  49.2 0.3 fusion.2
  49.5 1.3 %collective-permute-start.19 = (f32[256,256]{1,0:T(8,128)S(1)}, f32[256,256]{1,0:T(8,128)S(1)}, u32[]{:S(2)}, u32[]{:S(2)}) collective-permute-start(f32[256,256]{1,0:T(8,128)S(1)} %fusion.2), channel_id=1, source_target_pairs={{0,8},{1,9},{2,10},{3,11},{4,12},{5,13},{6,14},{7,15},{8,24},{9,25... | collective-permute-start | bytes 786440 | tf_op jit(solution)/shard_map/ppermute | solution.py:182
  50.8 0.3 collective-permute-done.20
  51.1 3.0 %collective-permute-done.19 = f32[256,256]{1,0:T(8,128)S(1)} collective-permute-done((f32[256,256]{1,0:T(8,128)S(1)}, f32[256,256]{1,0:T(8,128)S(1)}, u32[]{:S(2)}, u32[]{:S(2)}) %collective-permute-start.19) | collective-permute-done | bytes 262176 | tf_op jit(solution)/shard_map/ppermute | solution.py:182
  54.1 1.9 %collective-permute-start.21 = (f32[256,256]{1,0:T(8,128)S(1)}, f32[256,256]{1,0:T(8,128)S(1)}, u32[]{:S(2)}, u32[]{:S(2)}) collective-permute-start(f32[256,256]{1,0:T(8,128)S(1)} %select_add_fusion), channel_id=1, source_target_pairs={{0,8},{1,9},{2,10},{3,11},{4,12},{5,13},{6,14},{7,15},{8,0},{9,1},... | collective-permute-start | bytes 786440 | tf_op jit(solution)/shard_map/ppermute | solution.py:182
  56.1 1.2 %collective-permute-done.21 = f32[256,256]{1,0:T(8,128)S(1)} collective-permute-done((f32[256,256]{1,0:T(8,128)S(1)}, f32[256,256]{1,0:T(8,128)S(1)}, u32[]{:S(2)}, u32[]{:S(2)}) %collective-permute-start.21) | collective-permute-done | bytes 262176 | tf_op jit(solution)/shard_map/ppermute | solution.py:182
  57.2 0.3 fusion
  57.6 0.0 copy-start.2
  57.6 1.0 %convolution_bitcast_fusion = f32[1,256,256]{2,1,0:T(8,128)} fusion(f32[256,256]{1,0:T(8,128)S(1)} %fusion, f32[256,256]{1,0:T(8,128)S(1)} %broadcast_select_fusion), kind=kOutput, calls=%fused_computation | convolution fusion | flops 100663296 | bytes 786432 | tf_op jit(solution)/shard_map/dot_general | solution.py:148
  (6 shorter events, 0.1 us)
Async XLA Ops:
  0.7 8.3 %copy-start = (f32[1,1,4,256,256]{4,3,2,1,0:T(8,128)S(1)}, f32[1,1,4,256,256]{4,3,2,1,0:T(8,128)}, u32[]{:S(2)}) copy-start(f32[1,1,4,256,256]{4,3,2,1,0:T(8,128)} %param.2) | copy-start | bytes 3145732
  1.7 7.2 %collective-permute-start.1 = (f32[256,256]{1,0:T(8,128)S(1)}, f32[256,256]{1,0:T(8,128)S(1)}, u32[]{:S(2)}, u32[]{:S(2)}) collective-permute-start(f32[256,256]{1,0:T(8,128)S(1)} %dynamic-slice_bitcast_fusion.1), channel_id=1, source_target_pairs={{0,8},{1,0},{2,10},{3,2},{4,12},{5,4},{6,7},{7,6},{8,9},{9,1},{10,... | collective-permute-start | bytes 786440 | tf_op jit(solution)/shard_map/ppermute | solution.py:182
  4.2 10.4 %collective-permute-start.2 = (f32[256,256]{1,0:T(8,128)S(1)}, f32[256,256]{1,0:T(8,128)S(1)}, u32[]{:S(2)}, u32[]{:S(2)}) collective-permute-start(f32[256,256]{1,0:T(8,128)S(1)} %get-tuple-element.42), channel_id=1, source_target_pairs={{0,8},{1,0},{2,10},{3,2},{4,12},{5,4},{6,7},{7,6},{8,9},{9,1},{10,... | collective-permute-start | bytes 786440 | tf_op jit(solution)/shard_map/ppermute | solution.py:182
  4.5 10.6 %collective-permute-start.4 = (f32[256,256]{1,0:T(8,128)S(1)}, f32[256,256]{1,0:T(8,128)S(1)}, u32[]{:S(2)}, u32[]{:S(2)}) collective-permute-start(f32[256,256]{1,0:T(8,128)S(1)} %get-tuple-element.41), channel_id=1, source_target_pairs={{0,8},{1,0},{2,10},{3,2},{4,12},{5,4},{6,14},{7,15},{8,9},{9,1},{1... | collective-permute-start | bytes 786440 | tf_op jit(solution)/shard_map/ppermute | solution.py:182
  5.7 9.8 %collective-permute-start.5 = (f32[256,256]{1,0:T(8,128)S(1)}, f32[256,256]{1,0:T(8,128)S(1)}, u32[]{:S(2)}, u32[]{:S(2)}) collective-permute-start(f32[256,256]{1,0:T(8,128)S(1)} %get-tuple-element.40), channel_id=1, source_target_pairs={{0,8},{1,0},{2,10},{3,2},{4,12},{5,4},{6,14},{7,15},{8,9},{9,1},{1... | collective-permute-start | bytes 786440 | tf_op jit(solution)/shard_map/ppermute | solution.py:182
  11.1 6.2 %collective-permute-start.6 = (f32[256,256]{1,0:T(8,128)S(1)}, f32[256,256]{1,0:T(8,128)S(1)}, u32[]{:S(2)}, u32[]{:S(2)}) collective-permute-start(f32[256,256]{1,0:T(8,128)S(1)} %get-tuple-element.27.o0), channel_id=1, source_target_pairs={{0,2},{1,9},{2,10},{3,1},{4,12},{5,6},{6,4},{7,15},{8,0},{9,11},{1... | collective-permute-start | bytes 786440 | tf_op jit(solution)/shard_map/ppermute | solution.py:182
  15.0 8.2 %collective-permute-start.3 = (f32[256,256]{1,0:T(8,128)S(1)}, f32[256,256]{1,0:T(8,128)S(1)}, u32[]{:S(2)}, u32[]{:S(2)}) collective-permute-start(f32[256,256]{1,0:T(8,128)S(1)} %get-tuple-element.26.o1), channel_id=1, source_target_pairs={{0,2},{1,9},{2,10},{3,1},{4,12},{5,6},{6,4},{7,15},{8,0},{9,11},{1... | collective-permute-start | bytes 786440 | tf_op jit(solution)/shard_map/ppermute | solution.py:182
  15.6 8.7 %collective-permute-start.8 = (f32[256,256]{1,0:T(8,128)S(1)}, f32[256,256]{1,0:T(8,128)S(1)}, u32[]{:S(2)}, u32[]{:S(2)}) collective-permute-start(f32[256,256]{1,0:T(8,128)S(1)} %add.33.o3), channel_id=1, source_target_pairs={{0,2},{1,9},{2,10},{3,1},{4,12},{5,13},{6,14},{7,15},{8,0},{9,11},... | collective-permute-start | bytes 786440 | tf_op jit(solution)/shard_map/ppermute | solution.py:182
  17.2 9.1 %collective-permute-start.9 = (f32[256,256]{1,0:T(8,128)S(1)}, f32[256,256]{1,0:T(8,128)S(1)}, u32[]{:S(2)}, u32[]{:S(2)}) collective-permute-start(f32[256,256]{1,0:T(8,128)S(1)} %get-tuple-element.29.o2), channel_id=1, source_target_pairs={{0,2},{1,9},{2,10},{3,1},{4,12},{5,13},{6,14},{7,15},{8,0},{9,11},... | collective-permute-start | bytes 786440 | tf_op jit(solution)/shard_map/ppermute | solution.py:182
  19.3 7.0 %collective-permute-start.10 = (f32[256,256]{1,0:T(8,128)S(1)}, f32[256,256]{1,0:T(8,128)S(1)}, u32[]{:S(2)}, u32[]{:S(2)}) collective-permute-start(f32[256,256]{1,0:T(8,128)S(1)} %get-tuple-element.35), channel_id=1, source_target_pairs={{0,8},{1,9},{2,10},{3,5},{4,2},{5,13},{6,14},{7,15},{8,0},{9,1},{1... | collective-permute-start | bytes 786440 | tf_op jit(solution)/shard_map/ppermute | solution.py:182
  23.5 4.4 %collective-permute-start.7 = (f32[256,256]{1,0:T(8,128)S(1)}, f32[256,256]{1,0:T(8,128)S(1)}, u32[]{:S(2)}, u32[]{:S(2)}) collective-permute-start(f32[256,256]{1,0:T(8,128)S(1)} %shard_map.45), channel_id=1, source_target_pairs={{0,8},{1,9},{2,10},{3,5},{4,2},{5,13},{6,14},{7,15},{8,0},{9,1},{1... | collective-permute-start | bytes 786440 | tf_op jit(solution)/shard_map/ppermute | solution.py:182
  28.1 5.5 %collective-permute-start.11 = (f32[256,256]{1,0:T(8,128)S(1)}, f32[256,256]{1,0:T(8,128)S(1)}, u32[]{:S(2)}, u32[]{:S(2)}) collective-permute-start(f32[256,256]{1,0:T(8,128)S(1)} %shard_map.48), channel_id=1, source_target_pairs={{2,0},{11,9},{18,16},{27,25}} | collective-permute-start | bytes 786440 | tf_op jit(solution)/shard_map/ppermute | solution.py:182
  28.8 5.5 %collective-permute-start.12 = (f32[256,256]{1,0:T(8,128)S(1)}, f32[256,256]{1,0:T(8,128)S(1)}, u32[]{:S(2)}, u32[]{:S(2)}) collective-permute-start(f32[256,256]{1,0:T(8,128)S(1)} %shard_map.48), channel_id=1, source_target_pairs={{2,4},{11,13},{18,20},{27,29}} | collective-permute-start | bytes 786440 | tf_op jit(solution)/shard_map/ppermute | solution.py:182
  29.5 5.5 %collective-permute-start.13 = (f32[256,256]{1,0:T(8,128)S(1)}, f32[256,256]{1,0:T(8,128)S(1)}, u32[]{:S(2)}, u32[]{:S(2)}) collective-permute-start(f32[256,256]{1,0:T(8,128)S(1)} %shard_map.48), channel_id=1, source_target_pairs={{2,6},{11,15},{18,22},{27,31}} | collective-permute-start | bytes 786440 | tf_op jit(solution)/shard_map/ppermute | solution.py:182
  30.2 2.7 %copy-start.1 = (f32[1,256,256]{2,1,0:T(8,128)S(1)}, f32[1,256,256]{2,1,0:T(8,128)}, u32[]{:S(2)}) copy-start(f32[1,256,256]{2,1,0:T(8,128)} %param.3) | copy-start | bytes 786436
  32.2 4.2 %collective-permute-start.16 = (f32[256,256]{1,0:T(8,128)S(1)}, f32[256,256]{1,0:T(8,128)S(1)}, u32[]{:S(2)}, u32[]{:S(2)}) collective-permute-start(f32[256,256]{1,0:T(8,128)S(1)} %shard_map.49), channel_id=1, source_target_pairs={{2,0},{11,9},{18,16},{27,25}} | collective-permute-start | bytes 786440 | tf_op jit(solution)/shard_map/ppermute | solution.py:182
  32.9 15.9 %collective-permute-start = (f32[256,256]{1,0:T(8,128)S(1)}, f32[256,256]{1,0:T(8,128)S(1)}, u32[]{:S(2)}, u32[]{:S(2)}) collective-permute-start(f32[256,256]{1,0:T(8,128)S(1)} %bitcast.26), channel_id=1, source_target_pairs={{0,8},{1,9},{2,10},{3,11},{4,12},{5,13},{6,14},{7,15},{8,0},{9,1},... | collective-permute-start | bytes 786440 | tf_op jit(solution)/shard_map/ppermute | solution.py:182
  33.6 10.5 %collective-permute-start.17 = (f32[256,256]{1,0:T(8,128)S(1)}, f32[256,256]{1,0:T(8,128)S(1)}, u32[]{:S(2)}, u32[]{:S(2)}) collective-permute-start(f32[256,256]{1,0:T(8,128)S(1)} %shard_map.49), channel_id=1, source_target_pairs={{2,4},{11,13},{18,20},{27,29}} | collective-permute-start | bytes 786440 | tf_op jit(solution)/shard_map/ppermute | solution.py:182
  34.3 9.8 %collective-permute-start.18 = (f32[256,256]{1,0:T(8,128)S(1)}, f32[256,256]{1,0:T(8,128)S(1)}, u32[]{:S(2)}, u32[]{:S(2)}) collective-permute-start(f32[256,256]{1,0:T(8,128)S(1)} %shard_map.49), channel_id=1, source_target_pairs={{2,6},{11,15},{18,22},{27,31}} | collective-permute-start | bytes 786440 | tf_op jit(solution)/shard_map/ppermute | solution.py:182
  35.1 13.8 %collective-permute-start.14 = (f32[256,256]{1,0:T(8,128)S(1)}, f32[256,256]{1,0:T(8,128)S(1)}, u32[]{:S(2)}, u32[]{:S(2)}) collective-permute-start(f32[256,256]{1,0:T(8,128)S(1)} %select_select_fusion.1), channel_id=1, source_target_pairs={{0,9},{2,11},{4,13},{6,15},{9,8},{11,10},{13,12},{15,14},{16,25},{... | collective-permute-start | bytes 786440 | tf_op jit(solution)/shard_map/ppermute | solution.py:182
  36.4 12.4 %collective-permute-start.15 = (f32[256,256]{1,0:T(8,128)S(1)}, f32[256,256]{1,0:T(8,128)S(1)}, u32[]{:S(2)}, u32[]{:S(2)}) collective-permute-start(f32[256,256]{1,0:T(8,128)S(1)} %select_select_fusion.1), channel_id=1, source_target_pairs={{0,8},{1,9},{2,10},{3,11},{4,12},{5,13},{6,14},{7,15},{8,0},{9,1},... | collective-permute-start | bytes 786440 | tf_op jit(solution)/shard_map/ppermute | solution.py:182
  44.2 6.9 %collective-permute-start.20 = (f32[256,256]{1,0:T(8,128)S(1)}, f32[256,256]{1,0:T(8,128)S(1)}, u32[]{:S(2)}, u32[]{:S(2)}) collective-permute-start(f32[256,256]{1,0:T(8,128)S(1)} %select_select_fusion), channel_id=1, source_target_pairs={{0,1},{1,9},{2,3},{3,11},{4,5},{5,13},{6,7},{7,15},{8,0},{9,8},{10... | collective-permute-start | bytes 786440 | tf_op jit(solution)/shard_map/ppermute | solution.py:182
  49.5 4.6 %collective-permute-start.19 = (f32[256,256]{1,0:T(8,128)S(1)}, f32[256,256]{1,0:T(8,128)S(1)}, u32[]{:S(2)}, u32[]{:S(2)}) collective-permute-start(f32[256,256]{1,0:T(8,128)S(1)} %fusion.2), channel_id=1, source_target_pairs={{0,8},{1,9},{2,10},{3,11},{4,12},{5,13},{6,14},{7,15},{8,24},{9,25... | collective-permute-start | bytes 786440 | tf_op jit(solution)/shard_map/ppermute | solution.py:182
  54.1 3.1 %collective-permute-start.21 = (f32[256,256]{1,0:T(8,128)S(1)}, f32[256,256]{1,0:T(8,128)S(1)}, u32[]{:S(2)}, u32[]{:S(2)}) collective-permute-start(f32[256,256]{1,0:T(8,128)S(1)} %select_add_fusion), channel_id=1, source_target_pairs={{0,8},{1,9},{2,10},{3,11},{4,12},{5,13},{6,14},{7,15},{8,0},{9,1},... | collective-permute-start | bytes 786440 | tf_op jit(solution)/shard_map/ppermute | solution.py:182
  57.6 1.1 %copy-start.2 = (f32[256,256]{1,0:T(8,128)}, f32[256,256]{1,0:T(8,128)S(1)}, u32[]{:S(2)}) copy-start(f32[256,256]{1,0:T(8,128)S(1)} %fusion) | copy-start | bytes 786436

commit v3 on v2

--- a/solution.py
+++ b/solution.py
@@ -63,15 +63,19 @@
     return list(results)
 
 
-def first_step(marks, own, c0, out0, down, back, up, power, total):
+def first_step(marks, own, c0, out0, down, solver, bounce, power, total):
     turned = 2 * marks()[0]
     refl, trans, behind, upward = own[turned], own[1 + turned], own[2 - turned], own[3 - turned]
-    solver = inverse(product(behind, c0[...]), power, total)
-    down[...] = product(solver, trans)
-    back[...] = product(solver, behind)
-    bounce = product(upward, c0[...])
-    up[...] = upward + product(bounce, back[...])
-    out0[...] = refl + product(bounce, down[...])
+    solver[...] = inverse(product(behind, c0[...]), power, total)
+    down[...] = product(solver[...], trans)
+    bounce[...] = product(upward, c0[...])
+    out0[...] = refl + product(bounce[...], down[...])
+
+
+def first_rest(marks, own, solver, bounce, back, up):
+    turned = 2 * marks()[0]
+    back[...] = product(solver[...], own[2 - turned])
+    up[...] = own[3 - turned] + product(bounce[...], back[...])
 
 
 def second_step(marks, down, back, up, c1, out1, kept):
@@ -235,8 +239,9 @@
     first = functools.partial(marks, 1)
     split_level = levels - 2
     late = split_level == 1
-    out0, down, back, up = call(functools.partial(first_step, first), [own, came[0]], 4, True)
+    out0, down, solver, bounce = call(functools.partial(first_step, first), [own, came[0]], 4, True)
     sent = [send(out0, routes(1))]
+    back, up = call(functools.partial(first_rest, first), [own, solver, bounce], 2)
     out1, kept = call(functools.partial(second_step, first), [down, back, up, came[1]], 2)
     sent.append(send(out1, routes(1)))
     out2, rest = call(functools.partial(third_step, first), [down, up, kept, came[2]], 2)
@@ -264,7 +269,7 @@
     def line(g, k):
         return (g, 2 * k + g % 2)
 
-    def hand_out(block):
+    def hand_out(block, fill):
         level = levels - 1
         while level > 0:
             steps = []
@@ -278,13 +283,13 @@
             for step in zip(*steps):
                 fresh = is_one([target for _, target in step])
                 route = {line(g, a): line(g, b) for a, b in step for g in range(groups)}
-                got = jnp.where(fresh, send(block, route, False), got)
+                got = jnp.where(fresh, send(block, route, fill), got)
             block = got
             level -= 2
         return block
 
-    trans, _ = lax.optimization_barrier((hand_out(trans), refl))
-    refl = hand_out(refl)
+    trans, _ = lax.optimization_barrier((hand_out(trans, True), refl))
+    refl = hand_out(refl, False)
 
     across = {}
     for g in range(groups):

time: 58.9 us -> 57.7 us (0.980)
  starting transfers between devices: 30.9 us -> 29.2 us
  waiting for transfers between devices: 11.2 us -> 10.5 us
  Pallas kernels: 11.1 us -> 11.7 us
    ppermute x22, starting transfers between devices: 30.9 us -> 29.2 us  [send(): return lax.ppermute(block, AXES, route)]
    ppermute x22, waiting for transfers between devices: 11.2 us -> 10.5 us  [send(): return lax.ppermute(block, AXES, route)]
    pallas_call x9 -> x10, Pallas kernels: 11.1 us -> 11.7 us  [call(): pl.pallas_call(body, out_shape=[square] * outs, in_specs=[vmem] * len(blo...]
  transfers between devices with their start and end apart: 22 -> 22, of which waited for: 5 -> 5; matrix products, arithmetic and copies ran while one was open for 3% -> 4% of each run, Pallas kernels for 18% -> 20%
where the time goes in v3:
time: 57.7 us; the launch traced here: 56.9 us
  starting transfers between devices  29.2 us (51%)
  Pallas kernels  11.7 us (20%)
  waiting for transfers between devices  10.5 us (18%)
  local copies, waits for them, and re-layouts  2.23 us (4%)
  matrix products  2.07 us (4%)
  between operations  0.97 us (2%)
    ppermute x22, starting transfers between devices, send(): return lax.ppermute(block, AXES, route)  29.2 us
    pallas_call x10, Pallas kernels, call(): pl.pallas_call(body, out_shape=[square] * outs, in_specs=[vmem] * len(blo...  11.7 us
    ppermute x22, waiting for transfers between devices, send(): return lax.ppermute(block, AXES, route)  10.5 us
    dot_general x4, matrix products, times_transpose(): lax.dot_general(rows, matrix, (((1,), (1,)), ((), ())), precision=lax.Pre...  2.07 us
    squeeze x1, local copies, waits for them, and re-layouts, shards(): lax.dynamic_index_in_dim(after, 2 - 2 * turned, keepdims=False)  1.16 us
  transfers between devices with their start and end apart: 22, of which 5 were waited for; matrix products, arithmetic and copies ran while one was open for 4% of the time, Pallas kernels for 20%

profile of v3, /device:TPU:25, one launch (start us, length us, event | category | flops | bytes accessed | tf_op | source)
XLA Modules:
  0.0 56.9 jit_solution(18315565281293533832)
XLA Ops:
  0.7 0.0 copy-start
  0.7 1.1 %dynamic-slice_bitcast_fusion.1 = f32[256,256]{1,0:T(8,128)S(1)} fusion(f32[1,1,4,256,256]{4,3,2,1,0:T(8,128)} %param.2, s32[]{:T(128)S(6)} %select_n.98), kind=kLoop, calls=%fused_computation.13 | loop fusion | bytes 524292 | tf_op jit(solution)/shard_map/jit(dynamic_index_in_dim)/squeeze | solution.py:235
  1.7 1.3 %collective-permute-start.1 = (f32[256,256]{1,0:T(8,128)S(1)}, f32[256,256]{1,0:T(8,128)S(1)}, u32[]{:S(2)}, u32[]{:S(2)}) collective-permute-start(f32[256,256]{1,0:T(8,128)S(1)} %dynamic-slice_bitcast_fusion.1), channel_id=1, source_target_pairs={{0,8},{1,0},{2,10},{3,2},{4,12},{5,4},{6,7},{7,6},{8,9},{9,1},{10,... | collective-permute-start | bytes 786440 | tf_op jit(solution)/shard_map/ppermute | solution.py:186
  3.0 1.2 %dynamic-slice_bitcast_fusion = (f32[256,256]{1,0:T(8,128)S(1)}, f32[256,256]{1,0:T(8,128)S(1)}, f32[256,256]{1,0:T(8,128)S(1)}) fusion(f32[4,256,256]{2,1,0:T(8,128)} %bitcast.24, s32[]{:T(128)S(6)} %select_n.99), kind=kLoop, calls=%fused_computation.10 | loop fusion | bytes 1572868 | tf_op jit(solution)/shard_map/jit(dynamic_index_in_dim)/squeeze | solution.py:238
  4.2 0.3 collective-permute-start.2
  4.5 1.2 %collective-permute-start.4 = (f32[256,256]{1,0:T(8,128)S(1)}, f32[256,256]{1,0:T(8,128)S(1)}, u32[]{:S(2)}, u32[]{:S(2)}) collective-permute-start(f32[256,256]{1,0:T(8,128)S(1)} %get-tuple-element.45), channel_id=1, source_target_pairs={{0,8},{1,0},{2,10},{3,2},{4,12},{5,4},{6,14},{7,15},{8,9},{9,1},{1... | collective-permute-start | bytes 786440 | tf_op jit(solution)/shard_map/ppermute | solution.py:186
  5.7 0.0 collective-permute-start.5
  5.7 3.3 %collective-permute-done.1.c0 = f32[256,256]{1,0:T(8,128)S(1)} collective-permute-done((f32[256,256]{1,0:T(8,128)S(1)}, f32[256,256]{1,0:T(8,128)S(1)}, u32[]{:S(2)}, u32[]{:S(2)}) %collective-permute-start.1) | collective-permute-done | bytes 262176 | tf_op jit(solution)/shard_map/ppermute | solution.py:186
  9.0 2.1 %shard_map.41 = (f32[256,256]{1,0:T(8,128)S(1)}, f32[256,256]{1,0:T(8,128)S(1)}, f32[256,256]{1,0:T(8,128)S(1)}, f32[256,256]{1,0:T(8,128)S(1)}) custom-call(f32[4,256,256]{2,1,0:T(8,128)S(1)} %bitcast.25, f32[256,256]{1,0:T(8,128)S(1)} %collective-permute-done.1.c0), custom_call_target="tpu_custom_call" | custom-call | tf_op jit(solution)/shard_map/pallas_call | solution.py:55
  11.0 0.1 collective-permute-start.6
  11.1 0.7 %shard_map.42 = (f32[256,256]{1,0:T(8,128)S(1)}, f32[256,256]{1,0:T(8,128)S(1)}) custom-call(f32[4,256,256]{2,1,0:T(8,128)S(1)} %bitcast.26, f32[256,256]{1,0:T(8,128)S(1)} %get-tuple-element.25.solver, f32[256,256]{1,0:T(8,128)S(1)} %get-tuple-element.26.bounce), custom_call_target="tpu_custom_call" | custom-call | tf_op jit(solution)/shard_map/pallas_call | solution.py:55
  11.8 2.8 %collective-permute-done.2.c1 = f32[256,256]{1,0:T(8,128)S(1)} collective-permute-done((f32[256,256]{1,0:T(8,128)S(1)}, f32[256,256]{1,0:T(8,128)S(1)}, u32[]{:S(2)}, u32[]{:S(2)}) %collective-permute-start.2) | collective-permute-done | bytes 262176 | tf_op jit(solution)/shard_map/ppermute | solution.py:186
  14.6 0.4 shard_map.43
  15.0 0.1 collective-permute-start.3
  15.1 0.0 collective-permute-done.4.c2
  15.1 0.4 shard_map.44
  15.5 0.0 collective-permute-done.5
  15.6 1.6 %collective-permute-start.8 = (f32[256,256]{1,0:T(8,128)S(1)}, f32[256,256]{1,0:T(8,128)S(1)}, u32[]{:S(2)}, u32[]{:S(2)}) collective-permute-start(f32[256,256]{1,0:T(8,128)S(1)} %add.33.o3), channel_id=1, source_target_pairs={{0,2},{1,9},{2,10},{3,1},{4,12},{5,13},{6,14},{7,15},{8,0},{9,11},... | collective-permute-start | bytes 786440 | tf_op jit(solution)/shard_map/ppermute | solution.py:186
  17.2 0.1 collective-permute-start.9
  17.2 0.0 collective-permute-done.6.refl_b.c0
  17.2 2.0 %shard_map.45 = (f32[256,256]{1,0:T(8,128)S(1)}, f32[256,256]{1,0:T(8,128)S(1)}) custom-call(f32[256,256]{1,0:T(8,128)S(1)} %get-tuple-element.31.o0, f32[256,256]{1,0:T(8,128)S(1)} %get-tuple-element.30.o1, f32[256,256]{1,0:T(8,128)S(1)} %get-tuple-element.33.o2, f32[256,256]{1,0:T(8,128)S(1)} %add.33.o3, f32[256,256]{1,0:T(8,128)S(1)} %collective-permute-done.6.refl_b.c0), custom_call_target="tpu_custom_call" | custom-call | tf_op jit(solution)/shard_map/pallas_call | solution.py:55
  19.3 3.9 %collective-permute-start.10 = (f32[256,256]{1,0:T(8,128)S(1)}, f32[256,256]{1,0:T(8,128)S(1)}, u32[]{:S(2)}, u32[]{:S(2)}) collective-permute-start(f32[256,256]{1,0:T(8,128)S(1)} %get-tuple-element.39), channel_id=1, source_target_pairs={{0,8},{1,9},{2,10},{3,5},{4,2},{5,13},{6,14},{7,15},{8,0},{9,1},{1... | collective-permute-start | bytes 786440 | tf_op jit(solution)/shard_map/ppermute | solution.py:186
  23.1 0.0 collective-permute-done.3.left.c1
  23.1 0.3 shard_map.46
  23.4 0.8 %collective-permute-start.7 = (f32[256,256]{1,0:T(8,128)S(1)}, f32[256,256]{1,0:T(8,128)S(1)}, u32[]{:S(2)}, u32[]{:S(2)}) collective-permute-start(f32[256,256]{1,0:T(8,128)S(1)} %shard_map.46), channel_id=1, source_target_pairs={{0,8},{1,9},{2,10},{3,5},{4,2},{5,13},{6,14},{7,15},{8,0},{9,1},{1... | collective-permute-start | bytes 786440 | tf_op jit(solution)/shard_map/ppermute | solution.py:186
  24.2 0.0 collective-permute-done.8.c3
  24.2 2.0 %shard_map.47 = (f32[256,256]{1,0:T(8,128)S(1)}, f32[256,256]{1,0:T(8,128)S(1)}, f32[256,256]{1,0:T(8,128)S(1)}) custom-call(f32[256,256]{1,0:T(8,128)S(1)} %get-tuple-element.31.o0, f32[256,256]{1,0:T(8,128)S(1)} %get-tuple-element.30.o1, f32[256,256]{1,0:T(8,128)S(1)} %get-tuple-element.33.o2, f32[256,256]{1,0:T(8,128)S(1)} %add.33.o3, ...), custom_call_target="tpu_custom_call" | custom-call | tf_op jit(solution)/shard_map/pallas_call | solution.py:55
  26.2 0.0 collective-permute-done.9.c2
  26.3 0.0 collective-permute-done.10.refl_b.low_refl
  26.3 1.5 %shard_map.48.right.down = f32[256,256]{1,0:T(8,128)S(1)} custom-call(f32[256,256]{1,0:T(8,128)S(1)} %get-tuple-element.37.back_a, f32[256,256]{1,0:T(8,128)S(1)} %get-tuple-element.38.trans_a, f32[256,256]{1,0:T(8,128)S(1)} %collective-permute-done.10.refl_b.low_refl), custom_call_target="tpu_custom_call" | custom-call | tf_op jit(solution)/shard_map/pallas_call | solution.py:55
  27.8 0.0 collective-permute-done.7.left
  27.8 0.3 shard_map.49
  28.1 0.1 collective-permute-start.11
  28.2 0.5 collective-permute-start.12
  28.7 4.0 %collective-permute-start.13 = (f32[256,256]{1,0:T(8,128)S(1)}, f32[256,256]{1,0:T(8,128)S(1)}, u32[]{:S(2)}, u32[]{:S(2)}) collective-permute-start(f32[256,256]{1,0:T(8,128)S(1)} %shard_map.49), channel_id=1, source_target_pairs={{0,8},{1,9},{2,6},{3,11},{4,12},{5,13},{6,14},{7,3},{8,0},{9,1},{1... | collective-permute-start | bytes 786440 | tf_op jit(solution)/shard_map/ppermute | solution.py:186
  32.7 2.0 %shard_map.50 = f32[256,256]{1,0:T(8,128)S(1)} custom-call(f32[256,256]{1,0:T(8,128)S(1)} %get-tuple-element.31.o0, f32[256,256]{1,0:T(8,128)S(1)} %get-tuple-element.33.o2, f32[256,256]{1,0:T(8,128)S(1)} %add.33.o3, f32[256,256]{1,0:T(8,128)S(1)} %collective-permute-done.6.refl_b.c0, f32[256,256]{1,0:T(8,128)S(1)} %collective-permute-done.3.left.c1, ...), custom_call_target="tpu_custom_call" | custom-call | tf_op jit(solution)/shard_map/pallas_call | solution.py:55
  34.7 0.7 %collective-permute-start.16 = (f32[256,256]{1,0:T(8,128)S(1)}, f32[256,256]{1,0:T(8,128)S(1)}, u32[]{:S(2)}, u32[]{:S(2)}) collective-permute-start(f32[256,256]{1,0:T(8,128)S(1)} %shard_map.50), channel_id=1, source_target_pairs={{2,0},{11,9},{18,16},{27,25}} | collective-permute-start | bytes 786440 | tf_op jit(solution)/shard_map/ppermute | solution.py:186
  35.4 0.1 collective-permute-start
  35.5 0.0 collective-permute-done.11
  35.5 0.7 %collective-permute-start.17 = (f32[256,256]{1,0:T(8,128)S(1)}, f32[256,256]{1,0:T(8,128)S(1)}, u32[]{:S(2)}, u32[]{:S(2)}) collective-permute-start(f32[256,256]{1,0:T(8,128)S(1)} %shard_map.50), channel_id=1, source_target_pairs={{2,4},{11,13},{18,20},{27,29}} | collective-permute-start | bytes 786440 | tf_op jit(solution)/shard_map/ppermute | solution.py:186
  36.2 0.0 collective-permute-done.12
  36.2 0.7 %collective-permute-start.18 = (f32[256,256]{1,0:T(8,128)S(1)}, f32[256,256]{1,0:T(8,128)S(1)}, u32[]{:S(2)}, u32[]{:S(2)}) collective-permute-start(f32[256,256]{1,0:T(8,128)S(1)} %shard_map.50), channel_id=1, source_target_pairs={{2,6},{11,15},{18,22},{27,31}} | collective-permute-start | bytes 786440 | tf_op jit(solution)/shard_map/ppermute | solution.py:186
  36.9 0.0 collective-permute-done.13
  36.9 0.1 select_select_fusion.1
  36.9 1.3 %collective-permute-start.14 = (f32[256,256]{1,0:T(8,128)S(1)}, f32[256,256]{1,0:T(8,128)S(1)}, u32[]{:S(2)}, u32[]{:S(2)}) collective-permute-start(f32[256,256]{1,0:T(8,128)S(1)} %select_select_fusion.1), channel_id=1, source_target_pairs={{0,9},{2,11},{4,13},{6,15},{9,8},{11,10},{13,12},{15,14},{16,25},{... | collective-permute-start | bytes 786440 | tf_op jit(solution)/shard_map/ppermute | solution.py:186
  38.2 0.0 collective-permute-done.16
  38.3 4.7 %collective-permute-start.15 = (f32[256,256]{1,0:T(8,128)S(1)}, f32[256,256]{1,0:T(8,128)S(1)}, u32[]{:S(2)}, u32[]{:S(2)}) collective-permute-start(f32[256,256]{1,0:T(8,128)S(1)} %select_select_fusion.1), channel_id=1, source_target_pairs={{0,8},{1,9},{2,10},{3,11},{4,12},{5,13},{6,14},{7,15},{8,0},{9,1},... | collective-permute-start | bytes 786440 | tf_op jit(solution)/shard_map/ppermute | solution.py:186
  43.0 0.0 collective-permute-done.17
  43.0 0.0 collective-permute-done.18
  43.0 0.1 select_select_fusion
  43.1 4.0 %collective-permute-start.20 = (f32[256,256]{1,0:T(8,128)S(1)}, f32[256,256]{1,0:T(8,128)S(1)}, u32[]{:S(2)}, u32[]{:S(2)}) collective-permute-start(f32[256,256]{1,0:T(8,128)S(1)} %select_select_fusion), channel_id=1, source_target_pairs={{0,1},{1,9},{2,3},{3,11},{4,5},{5,13},{6,7},{7,15},{8,0},{9,8},{10... | collective-permute-start | bytes 786440 | tf_op jit(solution)/shard_map/ppermute | solution.py:186
  47.1 0.0 collective-permute-done
  47.1 0.0 collective-permute-done.14
  47.1 0.0 collective-permute-done.15
  47.1 0.3 fusion.1
  47.4 0.3 fusion.2
  47.8 1.3 %collective-permute-start.19 = (f32[256,256]{1,0:T(8,128)S(1)}, f32[256,256]{1,0:T(8,128)S(1)}, u32[]{:S(2)}, u32[]{:S(2)}) collective-permute-start(f32[256,256]{1,0:T(8,128)S(1)} %fusion.2), channel_id=1, source_target_pairs={{0,8},{1,9},{2,10},{3,11},{4,12},{5,13},{6,14},{7,15},{8,24},{9,25... | collective-permute-start | bytes 786440 | tf_op jit(solution)/shard_map/ppermute | solution.py:186
  49.1 0.9 %collective-permute-done.20 = f32[256,256]{1,0:T(8,128)S(1)} collective-permute-done((f32[256,256]{1,0:T(8,128)S(1)}, f32[256,256]{1,0:T(8,128)S(1)}, u32[]{:S(2)}, u32[]{:S(2)}) %collective-permute-start.20) | collective-permute-done | bytes 262176 | tf_op jit(solution)/shard_map/ppermute | solution.py:186
  50.0 2.3 %collective-permute-done.19 = f32[256,256]{1,0:T(8,128)S(1)} collective-permute-done((f32[256,256]{1,0:T(8,128)S(1)}, f32[256,256]{1,0:T(8,128)S(1)}, u32[]{:S(2)}, u32[]{:S(2)}) %collective-permute-start.19) | collective-permute-done | bytes 262176 | tf_op jit(solution)/shard_map/ppermute | solution.py:186
  52.4 1.9 %collective-permute-start.21 = (f32[256,256]{1,0:T(8,128)S(1)}, f32[256,256]{1,0:T(8,128)S(1)}, u32[]{:S(2)}, u32[]{:S(2)}) collective-permute-start(f32[256,256]{1,0:T(8,128)S(1)} %select_add_fusion), channel_id=1, source_target_pairs={{0,8},{1,9},{2,10},{3,11},{4,12},{5,13},{6,14},{7,15},{8,0},{9,1},... | collective-permute-start | bytes 786440 | tf_op jit(solution)/shard_map/ppermute | solution.py:186
  54.3 1.2 %collective-permute-done.21 = f32[256,256]{1,0:T(8,128)S(1)} collective-permute-done((f32[256,256]{1,0:T(8,128)S(1)}, f32[256,256]{1,0:T(8,128)S(1)}, u32[]{:S(2)}, u32[]{:S(2)}) %collective-permute-start.21) | collective-permute-done | bytes 262176 | tf_op jit(solution)/shard_map/ppermute | solution.py:186
  55.5 0.3 fusion
  55.8 0.0 copy-start.2
  55.8 1.0 %convolution_bitcast_fusion = f32[1,256,256]{2,1,0:T(8,128)} fusion(f32[256,256]{1,0:T(8,128)S(1)} %fusion, f32[256,256]{1,0:T(8,128)S(1)} %broadcast_select_fusion), kind=kOutput, calls=%fused_computation | convolution fusion | flops 100663296 | bytes 786432 | tf_op jit(solution)/shard_map/dot_general | solution.py:152
  (7 shorter events, 0.1 us)
Async XLA Ops:
  0.7 8.3 %copy-start = (f32[1,1,4,256,256]{4,3,2,1,0:T(8,128)S(1)}, f32[1,1,4,256,256]{4,3,2,1,0:T(8,128)}, u32[]{:S(2)}) copy-start(f32[1,1,4,256,256]{4,3,2,1,0:T(8,128)} %param.2) | copy-start | bytes 3145732
  1.7 7.2 %collective-permute-start.1 = (f32[256,256]{1,0:T(8,128)S(1)}, f32[256,256]{1,0:T(8,128)S(1)}, u32[]{:S(2)}, u32[]{:S(2)}) collective-permute-start(f32[256,256]{1,0:T(8,128)S(1)} %dynamic-slice_bitcast_fusion.1), channel_id=1, source_target_pairs={{0,8},{1,0},{2,10},{3,2},{4,12},{5,4},{6,7},{7,6},{8,9},{9,1},{10,... | collective-permute-start | bytes 786440 | tf_op jit(solution)/shard_map/ppermute | solution.py:186
  4.2 10.4 %collective-permute-start.2 = (f32[256,256]{1,0:T(8,128)S(1)}, f32[256,256]{1,0:T(8,128)S(1)}, u32[]{:S(2)}, u32[]{:S(2)}) collective-permute-start(f32[256,256]{1,0:T(8,128)S(1)} %get-tuple-element.46), channel_id=1, source_target_pairs={{0,8},{1,0},{2,10},{3,2},{4,12},{5,4},{6,7},{7,6},{8,9},{9,1},{10,... | collective-permute-start | bytes 786440 | tf_op jit(solution)/shard_map/ppermute | solution.py:186
  4.5 10.6 %collective-permute-start.4 = (f32[256,256]{1,0:T(8,128)S(1)}, f32[256,256]{1,0:T(8,128)S(1)}, u32[]{:S(2)}, u32[]{:S(2)}) collective-permute-start(f32[256,256]{1,0:T(8,128)S(1)} %get-tuple-element.45), channel_id=1, source_target_pairs={{0,8},{1,0},{2,10},{3,2},{4,12},{5,4},{6,14},{7,15},{8,9},{9,1},{1... | collective-permute-start | bytes 786440 | tf_op jit(solution)/shard_map/ppermute | solution.py:186
  5.7 9.8 %collective-permute-start.5 = (f32[256,256]{1,0:T(8,128)S(1)}, f32[256,256]{1,0:T(8,128)S(1)}, u32[]{:S(2)}, u32[]{:S(2)}) collective-permute-start(f32[256,256]{1,0:T(8,128)S(1)} %get-tuple-element.44), channel_id=1, source_target_pairs={{0,8},{1,0},{2,10},{3,2},{4,12},{5,4},{6,14},{7,15},{8,9},{9,1},{1... | collective-permute-start | bytes 786440 | tf_op jit(solution)/shard_map/ppermute | solution.py:186
  11.0 6.2 %collective-permute-start.6 = (f32[256,256]{1,0:T(8,128)S(1)}, f32[256,256]{1,0:T(8,128)S(1)}, u32[]{:S(2)}, u32[]{:S(2)}) collective-permute-start(f32[256,256]{1,0:T(8,128)S(1)} %get-tuple-element.31.o0), channel_id=1, source_target_pairs={{0,2},{1,9},{2,10},{3,1},{4,12},{5,6},{6,4},{7,15},{8,0},{9,11},{1... | collective-permute-start | bytes 786440 | tf_op jit(solution)/shard_map/ppermute | solution.py:186
  15.0 8.1 %collective-permute-start.3 = (f32[256,256]{1,0:T(8,128)S(1)}, f32[256,256]{1,0:T(8,128)S(1)}, u32[]{:S(2)}, u32[]{:S(2)}) collective-permute-start(f32[256,256]{1,0:T(8,128)S(1)} %get-tuple-element.30.o1), channel_id=1, source_target_pairs={{0,2},{1,9},{2,10},{3,1},{4,12},{5,6},{6,4},{7,15},{8,0},{9,11},{1... | collective-permute-start | bytes 786440 | tf_op jit(solution)/shard_map/ppermute | solution.py:186
  15.6 8.6 %collective-permute-start.8 = (f32[256,256]{1,0:T(8,128)S(1)}, f32[256,256]{1,0:T(8,128)S(1)}, u32[]{:S(2)}, u32[]{:S(2)}) collective-permute-start(f32[256,256]{1,0:T(8,128)S(1)} %add.33.o3), channel_id=1, source_target_pairs={{0,2},{1,9},{2,10},{3,1},{4,12},{5,13},{6,14},{7,15},{8,0},{9,11},... | collective-permute-start | bytes 786440 | tf_op jit(solution)/shard_map/ppermute | solution.py:186
  17.2 9.1 %collective-permute-start.9 = (f32[256,256]{1,0:T(8,128)S(1)}, f32[256,256]{1,0:T(8,128)S(1)}, u32[]{:S(2)}, u32[]{:S(2)}) collective-permute-start(f32[256,256]{1,0:T(8,128)S(1)} %get-tuple-element.33.o2), channel_id=1, source_target_pairs={{0,2},{1,9},{2,10},{3,1},{4,12},{5,13},{6,14},{7,15},{8,0},{9,11},... | collective-permute-start | bytes 786440 | tf_op jit(solution)/shard_map/ppermute | solution.py:186
  19.3 7.0 %collective-permute-start.10 = (f32[256,256]{1,0:T(8,128)S(1)}, f32[256,256]{1,0:T(8,128)S(1)}, u32[]{:S(2)}, u32[]{:S(2)}) collective-permute-start(f32[256,256]{1,0:T(8,128)S(1)} %get-tuple-element.39), channel_id=1, source_target_pairs={{0,8},{1,9},{2,10},{3,5},{4,2},{5,13},{6,14},{7,15},{8,0},{9,1},{1... | collective-permute-start | bytes 786440 | tf_op jit(solution)/shard_map/ppermute | solution.py:186
  23.4 4.4 %collective-permute-start.7 = (f32[256,256]{1,0:T(8,128)S(1)}, f32[256,256]{1,0:T(8,128)S(1)}, u32[]{:S(2)}, u32[]{:S(2)}) collective-permute-start(f32[256,256]{1,0:T(8,128)S(1)} %shard_map.46), channel_id=1, source_target_pairs={{0,8},{1,9},{2,10},{3,5},{4,2},{5,13},{6,14},{7,15},{8,0},{9,1},{1... | collective-permute-start | bytes 786440 | tf_op jit(solution)/shard_map/ppermute | solution.py:186
  28.1 7.4 %collective-permute-start.11 = (f32[256,256]{1,0:T(8,128)S(1)}, f32[256,256]{1,0:T(8,128)S(1)}, u32[]{:S(2)}, u32[]{:S(2)}) collective-permute-start(f32[256,256]{1,0:T(8,128)S(1)} %shard_map.49), channel_id=1, source_target_pairs={{0,8},{1,3},{2,0},{3,11},{4,12},{5,13},{6,14},{7,15},{8,10},{9,1},... | collective-permute-start | bytes 786440 | tf_op jit(solution)/shard_map/ppermute | solution.py:186
  28.2 8.0 %collective-permute-start.12 = (f32[256,256]{1,0:T(8,128)S(1)}, f32[256,256]{1,0:T(8,128)S(1)}, u32[]{:S(2)}, u32[]{:S(2)}) collective-permute-start(f32[256,256]{1,0:T(8,128)S(1)} %shard_map.49), channel_id=1, source_target_pairs={{0,8},{1,9},{2,4},{3,11},{4,12},{5,3},{6,14},{7,15},{8,0},{9,1},{1... | collective-permute-start | bytes 786440 | tf_op jit(solution)/shard_map/ppermute | solution.py:186
  28.7 8.2 %collective-permute-start.13 = (f32[256,256]{1,0:T(8,128)S(1)}, f32[256,256]{1,0:T(8,128)S(1)}, u32[]{:S(2)}, u32[]{:S(2)}) collective-permute-start(f32[256,256]{1,0:T(8,128)S(1)} %shard_map.49), channel_id=1, source_target_pairs={{0,8},{1,9},{2,6},{3,11},{4,12},{5,13},{6,14},{7,3},{8,0},{9,1},{1... | collective-permute-start | bytes 786440 | tf_op jit(solution)/shard_map/ppermute | solution.py:186
  32.7 2.7 %copy-start.1 = (f32[1,256,256]{2,1,0:T(8,128)S(1)}, f32[1,256,256]{2,1,0:T(8,128)}, u32[]{:S(2)}) copy-start(f32[1,256,256]{2,1,0:T(8,128)} %param.3) | copy-start | bytes 786436
  34.7 3.6 %collective-permute-start.16 = (f32[256,256]{1,0:T(8,128)S(1)}, f32[256,256]{1,0:T(8,128)S(1)}, u32[]{:S(2)}, u32[]{:S(2)}) collective-permute-start(f32[256,256]{1,0:T(8,128)S(1)} %shard_map.50), channel_id=1, source_target_pairs={{2,0},{11,9},{18,16},{27,25}} | collective-permute-start | bytes 786440 | tf_op jit(solution)/shard_map/ppermute | solution.py:186
  35.4 11.7 %collective-permute-start = (f32[256,256]{1,0:T(8,128)S(1)}, f32[256,256]{1,0:T(8,128)S(1)}, u32[]{:S(2)}, u32[]{:S(2)}) collective-permute-start(f32[256,256]{1,0:T(8,128)S(1)} %bitcast.27), channel_id=1, source_target_pairs={{0,8},{1,9},{2,10},{3,11},{4,12},{5,13},{6,14},{7,15},{8,0},{9,1},... | collective-permute-start | bytes 786440 | tf_op jit(solution)/shard_map/ppermute | solution.py:186
  35.5 7.5 %collective-permute-start.17 = (f32[256,256]{1,0:T(8,128)S(1)}, f32[256,256]{1,0:T(8,128)S(1)}, u32[]{:S(2)}, u32[]{:S(2)}) collective-permute-start(f32[256,256]{1,0:T(8,128)S(1)} %shard_map.50), channel_id=1, source_target_pairs={{2,4},{11,13},{18,20},{27,29}} | collective-permute-start | bytes 786440 | tf_op jit(solution)/shard_map/ppermute | solution.py:186
  36.2 6.8 %collective-permute-start.18 = (f32[256,256]{1,0:T(8,128)S(1)}, f32[256,256]{1,0:T(8,128)S(1)}, u32[]{:S(2)}, u32[]{:S(2)}) collective-permute-start(f32[256,256]{1,0:T(8,128)S(1)} %shard_map.50), channel_id=1, source_target_pairs={{2,6},{11,15},{18,22},{27,31}} | collective-permute-start | bytes 786440 | tf_op jit(solution)/shard_map/ppermute | solution.py:186
  36.9 10.1 %collective-permute-start.14 = (f32[256,256]{1,0:T(8,128)S(1)}, f32[256,256]{1,0:T(8,128)S(1)}, u32[]{:S(2)}, u32[]{:S(2)}) collective-permute-start(f32[256,256]{1,0:T(8,128)S(1)} %select_select_fusion.1), channel_id=1, source_target_pairs={{0,9},{2,11},{4,13},{6,15},{9,8},{11,10},{13,12},{15,14},{16,25},{... | collective-permute-start | bytes 786440 | tf_op jit(solution)/shard_map/ppermute | solution.py:186
  38.3 8.8 %collective-permute-start.15 = (f32[256,256]{1,0:T(8,128)S(1)}, f32[256,256]{1,0:T(8,128)S(1)}, u32[]{:S(2)}, u32[]{:S(2)}) collective-permute-start(f32[256,256]{1,0:T(8,128)S(1)} %select_select_fusion.1), channel_id=1, source_target_pairs={{0,8},{1,9},{2,10},{3,11},{4,12},{5,13},{6,14},{7,15},{8,0},{9,1},... | collective-permute-start | bytes 786440 | tf_op jit(solution)/shard_map/ppermute | solution.py:186
  43.1 6.9 %collective-permute-start.20 = (f32[256,256]{1,0:T(8,128)S(1)}, f32[256,256]{1,0:T(8,128)S(1)}, u32[]{:S(2)}, u32[]{:S(2)}) collective-permute-start(f32[256,256]{1,0:T(8,128)S(1)} %select_select_fusion), channel_id=1, source_target_pairs={{0,1},{1,9},{2,3},{3,11},{4,5},{5,13},{6,7},{7,15},{8,0},{9,8},{10... | collective-permute-start | bytes 786440 | tf_op jit(solution)/shard_map/ppermute | solution.py:186
  47.8 4.6 %collective-permute-start.19 = (f32[256,256]{1,0:T(8,128)S(1)}, f32[256,256]{1,0:T(8,128)S(1)}, u32[]{:S(2)}, u32[]{:S(2)}) collective-permute-start(f32[256,256]{1,0:T(8,128)S(1)} %fusion.2), channel_id=1, source_target_pairs={{0,8},{1,9},{2,10},{3,11},{4,12},{5,13},{6,14},{7,15},{8,24},{9,25... | collective-permute-start | bytes 786440 | tf_op jit(solution)/shard_map/ppermute | solution.py:186
  52.4 3.1 %collective-permute-start.21 = (f32[256,256]{1,0:T(8,128)S(1)}, f32[256,256]{1,0:T(8,128)S(1)}, u32[]{:S(2)}, u32[]{:S(2)}) collective-permute-start(f32[256,256]{1,0:T(8,128)S(1)} %select_add_fusion), channel_id=1, source_target_pairs={{0,8},{1,9},{2,10},{3,11},{4,12},{5,13},{6,14},{7,15},{8,0},{9,1},... | collective-permute-start | bytes 786440 | tf_op jit(solution)/shard_map/ppermute | solution.py:186
  55.8 1.1 %copy-start.2 = (f32[256,256]{1,0:T(8,128)}, f32[256,256]{1,0:T(8,128)S(1)}, u32[]{:S(2)}) copy-start(f32[256,256]{1,0:T(8,128)S(1)} %fusion) | copy-start | bytes 786436

commit v4 on v3

--- a/solution.py
+++ b/solution.py
@@ -22,30 +22,39 @@
     return dot(left_high, right_high) + (dot(left_high, right_low) + dot(left_low, right_high))
 
 
-def inverse(coupling, power, total):
+def rough(left, right):
+    return jnp.dot(left.astype(jnp.bfloat16), right.astype(jnp.bfloat16), preferred_element_type=jnp.float32)
+
+
+def solve(coupling, use, power, total):
     order = coupling.shape[0]
     row = lax.broadcasted_iota(jnp.int32, (order, order), 0)
     column = lax.broadcasted_iota(jnp.int32, (order, order), 1)
-    result = coupling + jnp.where(row == column, 1.0, 0.0)
-    for _ in range(2):
-        coupling = product(coupling, coupling)
-        result = result + product(result, coupling)
-    power[...] = coupling
-    total[...] = result
-
-    def more(state):
-        turn, size = state
-        return jnp.logical_and(turn < 40, size > 2.0**-24)
-
-    def step(state):
-        turn, _ = state
-        squared = product(power[...], power[...])
-        total[...] += product(total[...], squared)
-        power[...] = squared
-        return turn + 1, jnp.sum(squared * squared)
-
-    lax.while_loop(more, step, (0, jnp.sum(coupling * coupling)))
-    return total[...]
+    start = coupling + jnp.where(row == column, 1.0, 0.0)
+    squared = product(coupling, coupling)
+    power[...] = squared
+    total[...] = start
+    size = jnp.sum(squared * squared)
+    result = start + (squared + rough(coupling, squared))
+    use(result + rough(rough(squared, squared), result))
+
+    @pl.when(size > 2.0**-10)
+    def _():
+        total[...] += product(total[...], power[...])
+
+        def more(state):
+            turn, last = state
+            return jnp.logical_and(turn < 40, last > 2.0**-24)
+
+        def step(state):
+            turn, _ = state
+            following = product(power[...], power[...])
+            total[...] += product(total[...], following)
+            power[...] = following
+            return turn + 1, jnp.sum(following * following)
+
+        lax.while_loop(more, step, (0, size))
+        use(total[...])
 
 
 def call(body, blocks, outs, solves=False):
@@ -66,10 +75,14 @@
 def first_step(marks, own, c0, out0, down, solver, bounce, power, total):
     turned = 2 * marks()[0]
     refl, trans, behind, upward = own[turned], own[1 + turned], own[2 - turned], own[3 - turned]
-    solver[...] = inverse(product(behind, c0[...]), power, total)
-    down[...] = product(solver[...], trans)
     bounce[...] = product(upward, c0[...])
-    out0[...] = refl + product(bounce[...], down[...])
+
+    def use(value):
+        solver[...] = value
+        down[...] = product(value, trans)
+        out0[...] = refl + product(bounce[...], down[...])
+
+    solve(product(behind, c0[...]), use, power, total)
 
 
 def first_rest(marks, own, solver, bounce, back, up):
@@ -95,25 +108,36 @@
 
 
 def lower_run(marks, o0, o1, o2, o3, refl_b, refl, down, power, total):
-    mark = marks()
-    refl_a, back_a = ordered(mark[0] == 1, o0, o3)
-    solver = inverse(product(back_a, refl_b[...]), power, total)
-    down[...] = product(solver, o1[...])
-    refl[...] = refl_a + product(product(o2[...], refl_b[...]), down[...])
+    refl_a, back_a = ordered(marks()[0] == 1, o0, o3)
+    bounce = product(o2[...], refl_b[...])
+
+    def use(value):
+        down[...] = product(value, o1[...])
+        refl[...] = refl_a + product(bounce, down[...])
+
+    solve(product(back_a, refl_b[...]), use, power, total)
 
 
 def upper_run(marks, o0, o1, o2, o3, c0, c1, c3, back, trans, solver, power, total):
     mark = marks()
     refl_b, back_b = ordered(mark[0] == 1, o0, o3)
     _, back_a = ordered(mark[1] == 1, c0, c3)
-    solver[...] = inverse(product(back_a, refl_b), power, total)
-    through = product(o1[...], solver[...])
-    back[...] = back_b + product(through, product(back_a, o2[...]))
-    trans[...] = product(through, c1[...])
+    turned_up = product(back_a, o2[...])
+
+    def use(value):
+        solver[...] = value
+        through = product(o1[...], value)
+        back[...] = back_b + product(through, turned_up)
+        trans[...] = product(through, c1[...])
+
+    solve(product(back_a, refl_b), use, power, total)
 
 
 def whole_down(back_a, trans_a, refl_b, down, power, total):
-    down[...] = product(inverse(product(back_a[...], refl_b[...]), power, total), trans_a[...])
+    def use(value):
+        down[...] = product(value, trans_a[...])
+
+    solve(product(back_a[...], refl_b[...]), use, power, total)
 
 
 def whole_refl(marks, o0, o2, o3, c0, c1, c2, c3, solver, low_refl, down, refl):
@@ -134,14 +158,17 @@
     below = mark[2] == 1
     refl_a, trans_a, up_a, back_a = [jnp.where(below, c, o) for o, c in zip(own, came)]
     refl_b, trans_b, up_b, back_b = [jnp.where(below, o, c) for o, c in zip(own, came)]
-    solver = inverse(product(back_a, refl_b), power, total)
-    down = product(solver, trans_a)
     bounce = product(up_a, refl_b)
-    turned_up = product(solver, product(back_a, up_b))
-    back[...] = back_b + product(trans_b, turned_up)
-    trans[...] = product(trans_b, down)
-    up[...] = product(up_a, up_b) + product(bounce, turned_up)
-    refl[...] = refl_a + product(bounce, down)
+
+    def use(value):
+        down = product(value, trans_a)
+        turned_up = product(value, product(back_a, up_b))
+        back[...] = back_b + product(trans_b, turned_up)
+        trans[...] = product(trans_b, down)
+        up[...] = product(up_a, up_b) + product(bounce, turned_up)
+        refl[...] = refl_a + product(bounce, down)
+
+    solve(product(back_a, refl_b), use, power, total)
 
 
 def times(left, right, out):
@@ -152,6 +179,40 @@
     return lax.dot_general(
         rows, matrix, (((1,), (1,)), ((), ())), precision=lax.Precision.HIGH, preferred_element_type=jnp.float32
     )
+
+
+def last_step(odd, even, refl, field_out, bounced_out, field, bounced, sems):
+    field[...] = jnp.where(lax.axis_index("depth") % 2 == 1, odd[...], even[...])
+    rows = pltpu.make_async_copy(field, field_out, sems.at[0])
+    rows.start()
+    half = field.shape[0] // 2
+    matrix_high, matrix_low = split(refl[...])
+    dot = functools.partial(
+        lax.dot_general, dimension_numbers=(((1,), (1,)), ((), ())), preferred_element_type=jnp.float32
+    )
+    copies = []
+    for i in range(2):
+        part = pl.ds(i * half, half)
+        high, low = split(field[part, :])
+        bounced[part, :] = dot(high, matrix_high) + (dot(high, matrix_low) + dot(low, matrix_high))
+        copies.append(pltpu.make_async_copy(bounced.at[part, :], bounced_out.at[part, :], sems.at[1 + i]))
+        copies[-1].start()
+    rows.wait()
+    for copy in copies:
+        copy.wait()
+
+
+def finish(odd, even, refl):
+    shape = jax.ShapeDtypeStruct(odd.shape, jnp.float32)
+    vmem, hbm = pl.BlockSpec(memory_space=pltpu.VMEM), pl.BlockSpec(memory_space=pl.ANY)
+    return pl.pallas_call(
+        last_step,
+        out_shape=[shape, shape],
+        in_specs=[vmem] * 3,
+        out_specs=[hbm, hbm],
+        scratch_shapes=[pltpu.VMEM(odd.shape, jnp.float32)] * 2 + [pltpu.SemaphoreType.DMA((3,))],
+        compiler_params=pltpu.CompilerParams(vmem_limit_bytes=12 * 2**20),
+    )(odd, even, refl)
 
 
 def filled(useful, groups, count):
@@ -280,16 +341,16 @@
                 else:
                     steps.append([(near, far)])
             got = block
-            for step in zip(*steps):
+            for step, full in zip(zip(*steps), fill):
                 fresh = is_one([target for _, target in step])
                 route = {line(g, a): line(g, b) for a, b in step for g in range(groups)}
-                got = jnp.where(fresh, send(block, route, fill), got)
+                got = jnp.where(fresh, send(block, route, full), got)
             block = got
             level -= 2
         return block
 
-    trans, _ = lax.optimization_barrier((hand_out(trans, True), refl))
-    refl = hand_out(refl, False)
+    trans, _ = lax.optimization_barrier((hand_out(trans, (True, True, False)), refl))
+    refl = hand_out(refl, (False, False, False))
 
     across = {}
     for g in range(groups):
@@ -311,8 +372,7 @@
             arriving = send(leaving, {(j + 1, s): (j + 3, s) for s in range(count)})
             arriving, _ = lax.optimization_barrier((arriving, spread_refl))
             handed = jnp.where(group // 2 == j // 2 + 1, arriving, handed)
-    field = jnp.where(parity == 1, field_odd, send(field_even, swap))
-    bounced = times_transpose(field, spread_refl)
+    field, bounced = finish(field_odd, send(field_even, swap), spread_refl)
     return (field[None], bounced[None])
 
 

time: 57.7 us -> 56.7 us (0.983)
  starting transfers between devices: 29.2 us -> 27.8 us
  Pallas kernels: 11.7 us -> 12.8 us
  matrix products: 2.07 us -> 1.02 us
    ppermute x22, starting transfers between devices: 29.2 us -> 27.8 us  [send(): return lax.ppermute(block, AXES, route)]
    pallas_call x0 -> x1, Pallas kernels: none -> 1.11 us  [finish(): pl.pallas_call(last_step, out_shape=[shape, shape], in_specs=[vmem] * 3,...]
    dot_general x4 -> x3, matrix products: 2.07 us -> 1.02 us  [times_transpose(): lax.dot_general(rows, matrix, (((1,), (1,)), ((), ())), precision=lax.Pre...]
  transfers between devices with their start and end apart: 22 -> 22, of which waited for: 5 -> 5; matrix products, arithmetic and copies ran while one was open for 4% -> 4% of each run, Pallas kernels for 20% -> 21%
where the time goes in v4:
time: 56.7 us; the launch traced here: 55.6 us
  starting transfers between devices  27.8 us (49%)
  Pallas kernels  12.8 us (23%)
  waiting for transfers between devices  10.6 us (19%)
  local copies, waits for them, and re-layouts  2.23 us (4%)
  matrix products  1.02 us (2%)
  between operations  0.97 us (2%)
    ppermute x22, starting transfers between devices, send(): return lax.ppermute(block, AXES, route)  27.8 us
    pallas_call x10, Pallas kernels, call(): pl.pallas_call(body, out_shape=[square] * outs, in_specs=[vmem] * len(blo...  11.7 us
    ppermute x22, waiting for transfers between devices, send(): return lax.ppermute(block, AXES, route)  10.6 us
    squeeze x1, local copies, waits for them, and re-layouts, shards(): lax.dynamic_index_in_dim(after, 2 - 2 * turned, keepdims=False)  1.16 us
  transfers between devices with their start and end apart: 22, of which 5 were waited for; matrix products, arithmetic and copies ran while one was open for 4% of the time, Pallas kernels for 21%

profile of v4, /device:TPU:25, one launch (start us, length us, event | category | flops | bytes accessed | tf_op | source)
XLA Modules:
  0.0 55.6 jit_solution(7952221676103974053)
XLA Ops:
  0.7 0.0 copy-start
  0.7 1.1 %dynamic-slice_bitcast_fusion.1 = f32[256,256]{1,0:T(8,128)S(1)} fusion(f32[1,1,4,256,256]{4,3,2,1,0:T(8,128)} %param.2, s32[]{:T(128)S(6)} %select_n.91), kind=kLoop, calls=%fused_computation.11 | loop fusion | bytes 524292 | tf_op jit(solution)/shard_map/jit(dynamic_index_in_dim)/squeeze | solution.py:296
  1.7 1.3 %collective-permute-start.1 = (f32[256,256]{1,0:T(8,128)S(1)}, f32[256,256]{1,0:T(8,128)S(1)}, u32[]{:S(2)}, u32[]{:S(2)}) collective-permute-start(f32[256,256]{1,0:T(8,128)S(1)} %dynamic-slice_bitcast_fusion.1), channel_id=1, source_target_pairs={{0,8},{1,0},{2,10},{3,2},{4,12},{5,4},{6,7},{7,6},{8,9},{9,1},{10,... | collective-permute-start | bytes 786440 | tf_op jit(solution)/shard_map/ppermute | solution.py:247
  3.0 1.2 %dynamic-slice_bitcast_fusion = (f32[256,256]{1,0:T(8,128)S(1)}, f32[256,256]{1,0:T(8,128)S(1)}, f32[256,256]{1,0:T(8,128)S(1)}) fusion(f32[4,256,256]{2,1,0:T(8,128)} %bitcast.21, s32[]{:T(128)S(6)} %select_n.92), kind=kLoop, calls=%fused_computation.8 | loop fusion | bytes 1572868 | tf_op jit(solution)/shard_map/jit(dynamic_index_in_dim)/squeeze | solution.py:299
  4.2 0.3 collective-permute-start.2
  4.5 1.2 %collective-permute-start.4 = (f32[256,256]{1,0:T(8,128)S(1)}, f32[256,256]{1,0:T(8,128)S(1)}, u32[]{:S(2)}, u32[]{:S(2)}) collective-permute-start(f32[256,256]{1,0:T(8,128)S(1)} %get-tuple-element.49), channel_id=1, source_target_pairs={{0,8},{1,0},{2,10},{3,2},{4,12},{5,4},{6,14},{7,15},{8,9},{9,1},{1... | collective-permute-start | bytes 786440 | tf_op jit(solution)/shard_map/ppermute | solution.py:247
  5.7 0.0 collective-permute-start.5
  5.7 3.3 %collective-permute-done.1.c0 = f32[256,256]{1,0:T(8,128)S(1)} collective-permute-done((f32[256,256]{1,0:T(8,128)S(1)}, f32[256,256]{1,0:T(8,128)S(1)}, u32[]{:S(2)}, u32[]{:S(2)}) %collective-permute-start.1) | collective-permute-done | bytes 262176 | tf_op jit(solution)/shard_map/ppermute | solution.py:247
  9.0 1.7 %shard_map.41 = (f32[256,256]{1,0:T(8,128)S(1)}, f32[256,256]{1,0:T(8,128)S(1)}, f32[256,256]{1,0:T(8,128)S(1)}, f32[256,256]{1,0:T(8,128)S(1)}) custom-call(f32[4,256,256]{2,1,0:T(8,128)S(1)} %bitcast.22, f32[256,256]{1,0:T(8,128)S(1)} %collective-permute-done.1.c0), custom_call_target="tpu_custom_call" | custom-call | tf_op jit(solution)/shard_map/pallas_call | solution.py:64
  10.6 0.1 collective-permute-start.6
  10.7 0.7 %shard_map.42 = (f32[256,256]{1,0:T(8,128)S(1)}, f32[256,256]{1,0:T(8,128)S(1)}) custom-call(f32[4,256,256]{2,1,0:T(8,128)S(1)} %bitcast.23, f32[256,256]{1,0:T(8,128)S(1)} %get-tuple-element.27.solver, f32[256,256]{1,0:T(8,128)S(1)} %get-tuple-element.28.bounce), custom_call_target="tpu_custom_call" | custom-call | tf_op jit(solution)/shard_map/pallas_call | solution.py:64
  11.4 3.2 %collective-permute-done.2.c1 = f32[256,256]{1,0:T(8,128)S(1)} collective-permute-done((f32[256,256]{1,0:T(8,128)S(1)}, f32[256,256]{1,0:T(8,128)S(1)}, u32[]{:S(2)}, u32[]{:S(2)}) %collective-permute-start.2) | collective-permute-done | bytes 262176 | tf_op jit(solution)/shard_map/ppermute | solution.py:247
  14.6 0.4 shard_map.43
  15.0 0.1 collective-permute-start.3
  15.1 0.0 collective-permute-done.4.c2
  15.1 0.4 shard_map.44
  15.5 0.0 collective-permute-done.5
  15.6 1.6 %collective-permute-start.8 = (f32[256,256]{1,0:T(8,128)S(1)}, f32[256,256]{1,0:T(8,128)S(1)}, u32[]{:S(2)}, u32[]{:S(2)}) collective-permute-start(f32[256,256]{1,0:T(8,128)S(1)} %add.33.o3), channel_id=1, source_target_pairs={{0,2},{1,9},{2,10},{3,1},{4,12},{5,13},{6,14},{7,15},{8,0},{9,11},... | collective-permute-start | bytes 786440 | tf_op jit(solution)/shard_map/ppermute | solution.py:247
  17.2 0.1 collective-permute-start.9
  17.2 0.0 collective-permute-done.6.refl_b.c0
  17.2 1.7 %shard_map.45 = (f32[256,256]{1,0:T(8,128)S(1)}, f32[256,256]{1,0:T(8,128)S(1)}) custom-call(f32[256,256]{1,0:T(8,128)S(1)} %get-tuple-element.33.o0, f32[256,256]{1,0:T(8,128)S(1)} %get-tuple-element.32.o1, f32[256,256]{1,0:T(8,128)S(1)} %get-tuple-element.35.o2, f32[256,256]{1,0:T(8,128)S(1)} %add.33.o3, f32[256,256]{1,0:T(8,128)S(1)} %collective-permute-done.6.refl_b.c0), custom_call_target="tpu_custom_call" | custom-call | tf_op jit(solution)/shard_map/pallas_call | solution.py:64
  18.9 3.5 %collective-permute-start.10 = (f32[256,256]{1,0:T(8,128)S(1)}, f32[256,256]{1,0:T(8,128)S(1)}, u32[]{:S(2)}, u32[]{:S(2)}) collective-permute-start(f32[256,256]{1,0:T(8,128)S(1)} %get-tuple-element.41), channel_id=1, source_target_pairs={{0,8},{1,9},{2,10},{3,5},{4,2},{5,13},{6,14},{7,15},{8,0},{9,1},{1... | collective-permute-start | bytes 786440 | tf_op jit(solution)/shard_map/ppermute | solution.py:247
  22.4 0.0 collective-permute-done.3.left.c1
  22.4 0.3 shard_map.46
  22.7 1.6 %collective-permute-start.7 = (f32[256,256]{1,0:T(8,128)S(1)}, f32[256,256]{1,0:T(8,128)S(1)}, u32[]{:S(2)}, u32[]{:S(2)}) collective-permute-start(f32[256,256]{1,0:T(8,128)S(1)} %shard_map.46), channel_id=1, source_target_pairs={{0,8},{1,9},{2,10},{3,5},{4,2},{5,13},{6,14},{7,15},{8,0},{9,1},{1... | collective-permute-start | bytes 786440 | tf_op jit(solution)/shard_map/ppermute | solution.py:247
  24.2 0.0 collective-permute-done.8.c3
  24.2 1.8 %shard_map.47 = (f32[256,256]{1,0:T(8,128)S(1)}, f32[256,256]{1,0:T(8,128)S(1)}, f32[256,256]{1,0:T(8,128)S(1)}) custom-call(f32[256,256]{1,0:T(8,128)S(1)} %get-tuple-element.33.o0, f32[256,256]{1,0:T(8,128)S(1)} %get-tuple-element.32.o1, f32[256,256]{1,0:T(8,128)S(1)} %get-tuple-element.35.o2, f32[256,256]{1,0:T(8,128)S(1)} %add.33.o3, ...), custom_call_target="tpu_custom_call" | custom-call | tf_op jit(solution)/shard_map/pallas_call | solution.py:64
  26.0 0.0 collective-permute-done.9.c2
  26.0 0.0 collective-permute-done.10.refl_b.low_refl
  26.1 2.5 %shard_map.48.right.down = f32[256,256]{1,0:T(8,128)S(1)} custom-call(f32[256,256]{1,0:T(8,128)S(1)} %get-tuple-element.39.back_a, f32[256,256]{1,0:T(8,128)S(1)} %get-tuple-element.40.trans_a, f32[256,256]{1,0:T(8,128)S(1)} %collective-permute-done.10.refl_b.low_refl), custom_call_target="tpu_custom_call" | custom-call | tf_op jit(solution)/shard_map/pallas_call | solution.py:64
  28.6 0.0 collective-permute-done.7.left
  28.6 0.3 shard_map.49
  28.9 0.7 %collective-permute-start.11 = (f32[256,256]{1,0:T(8,128)S(1)}, f32[256,256]{1,0:T(8,128)S(1)}, u32[]{:S(2)}, u32[]{:S(2)}) collective-permute-start(f32[256,256]{1,0:T(8,128)S(1)} %shard_map.49), channel_id=1, source_target_pairs={{2,0},{11,9},{18,16},{27,25}} | collective-permute-start | bytes 786440 | tf_op jit(solution)/shard_map/ppermute | solution.py:247
  29.5 0.1 collective-permute-start.12
  29.6 3.3 %collective-permute-start.13 = (f32[256,256]{1,0:T(8,128)S(1)}, f32[256,256]{1,0:T(8,128)S(1)}, u32[]{:S(2)}, u32[]{:S(2)}) collective-permute-start(f32[256,256]{1,0:T(8,128)S(1)} %shard_map.49), channel_id=1, source_target_pairs={{0,8},{1,9},{2,6},{3,11},{4,12},{5,13},{6,14},{7,3},{8,0},{9,1},{1... | collective-permute-start | bytes 786440 | tf_op jit(solution)/shard_map/ppermute | solution.py:247
  32.9 2.0 %shard_map.50 = f32[256,256]{1,0:T(8,128)S(1)} custom-call(f32[256,256]{1,0:T(8,128)S(1)} %get-tuple-element.33.o0, f32[256,256]{1,0:T(8,128)S(1)} %get-tuple-element.35.o2, f32[256,256]{1,0:T(8,128)S(1)} %add.33.o3, f32[256,256]{1,0:T(8,128)S(1)} %collective-permute-done.6.refl_b.c0, f32[256,256]{1,0:T(8,128)S(1)} %collective-permute-done.3.left.c1, ...), custom_call_target="tpu_custom_call" | custom-call | tf_op jit(solution)/shard_map/pallas_call | solution.py:64
  34.9 0.7 %collective-permute-start.16 = (f32[256,256]{1,0:T(8,128)S(1)}, f32[256,256]{1,0:T(8,128)S(1)}, u32[]{:S(2)}, u32[]{:S(2)}) collective-permute-start(f32[256,256]{1,0:T(8,128)S(1)} %shard_map.50), channel_id=1, source_target_pairs={{2,0},{11,9},{18,16},{27,25}} | collective-permute-start | bytes 786440 | tf_op jit(solution)/shard_map/ppermute | solution.py:247
  35.6 0.0 copy-done.1
  35.6 0.1 collective-permute-start
  35.7 0.0 collective-permute-done.11
  35.7 0.7 %collective-permute-start.17 = (f32[256,256]{1,0:T(8,128)S(1)}, f32[256,256]{1,0:T(8,128)S(1)}, u32[]{:S(2)}, u32[]{:S(2)}) collective-permute-start(f32[256,256]{1,0:T(8,128)S(1)} %shard_map.50), channel_id=1, source_target_pairs={{2,4},{11,13},{18,20},{27,29}} | collective-permute-start | bytes 786440 | tf_op jit(solution)/shard_map/ppermute | solution.py:247
  36.4 0.0 collective-permute-done.12
  36.4 0.7 %collective-permute-start.18 = (f32[256,256]{1,0:T(8,128)S(1)}, f32[256,256]{1,0:T(8,128)S(1)}, u32[]{:S(2)}, u32[]{:S(2)}) collective-permute-start(f32[256,256]{1,0:T(8,128)S(1)} %shard_map.50), channel_id=1, source_target_pairs={{2,6},{11,15},{18,22},{27,31}} | collective-permute-start | bytes 786440 | tf_op jit(solution)/shard_map/ppermute | solution.py:247
  37.1 0.0 collective-permute-done.13
  37.1 0.1 select_select_fusion.1
  37.2 1.3 %collective-permute-start.14 = (f32[256,256]{1,0:T(8,128)S(1)}, f32[256,256]{1,0:T(8,128)S(1)}, u32[]{:S(2)}, u32[]{:S(2)}) collective-permute-start(f32[256,256]{1,0:T(8,128)S(1)} %select_select_fusion.1), channel_id=1, source_target_pairs={{0,9},{2,11},{4,13},{6,15},{9,8},{11,10},{13,12},{15,14},{16,25},{... | collective-permute-start | bytes 786440 | tf_op jit(solution)/shard_map/ppermute | solution.py:247
  38.5 0.0 collective-permute-done.16
  38.5 3.3 %collective-permute-start.15 = (f32[256,256]{1,0:T(8,128)S(1)}, f32[256,256]{1,0:T(8,128)S(1)}, u32[]{:S(2)}, u32[]{:S(2)}) collective-permute-start(f32[256,256]{1,0:T(8,128)S(1)} %select_select_fusion.1), channel_id=1, source_target_pairs={{0,8},{1,9},{2,10},{3,11},{4,12},{5,13},{6,14},{7,15},{8,0},{9,1},... | collective-permute-start | bytes 786440 | tf_op jit(solution)/shard_map/ppermute | solution.py:247
  41.8 0.0 collective-permute-done.17
  41.8 0.0 collective-permute-done.18
  41.8 0.1 select_select_fusion
  41.9 4.3 %collective-permute-start.20 = (f32[256,256]{1,0:T(8,128)S(1)}, f32[256,256]{1,0:T(8,128)S(1)}, u32[]{:S(2)}, u32[]{:S(2)}) collective-permute-start(f32[256,256]{1,0:T(8,128)S(1)} %select_select_fusion), channel_id=1, source_target_pairs={{0,1},{1,9},{2,3},{3,11},{4,5},{5,13},{6,7},{7,15},{8,0},{9,8},{10... | collective-permute-start | bytes 786440 | tf_op jit(solution)/shard_map/ppermute | solution.py:247
  46.1 0.0 collective-permute-done
  46.1 0.0 collective-permute-done.14
  46.1 0.0 collective-permute-done.15
  46.1 0.3 fusion
  46.5 0.3 fusion.1
  46.8 1.3 %collective-permute-start.19 = (f32[256,256]{1,0:T(8,128)S(1)}, f32[256,256]{1,0:T(8,128)S(1)}, u32[]{:S(2)}, u32[]{:S(2)}) collective-permute-start(f32[256,256]{1,0:T(8,128)S(1)} %fusion.1), channel_id=1, source_target_pairs={{0,8},{1,9},{2,10},{3,11},{4,12},{5,13},{6,14},{7,15},{8,24},{9,25... | collective-permute-start | bytes 786440 | tf_op jit(solution)/shard_map/ppermute | solution.py:247
  48.1 2.1 %collective-permute-done.20 = f32[256,256]{1,0:T(8,128)S(1)} collective-permute-done((f32[256,256]{1,0:T(8,128)S(1)}, f32[256,256]{1,0:T(8,128)S(1)}, u32[]{:S(2)}, u32[]{:S(2)}) %collective-permute-start.20) | collective-permute-done | bytes 262176 | tf_op jit(solution)/shard_map/ppermute | solution.py:247
  50.2 1.2 %collective-permute-done.19 = f32[256,256]{1,0:T(8,128)S(1)} collective-permute-done((f32[256,256]{1,0:T(8,128)S(1)}, f32[256,256]{1,0:T(8,128)S(1)}, u32[]{:S(2)}, u32[]{:S(2)}) %collective-permute-start.19) | collective-permute-done | bytes 262176 | tf_op jit(solution)/shard_map/ppermute | solution.py:247
  51.4 1.9 %collective-permute-start.21 = (f32[256,256]{1,0:T(8,128)S(1)}, f32[256,256]{1,0:T(8,128)S(1)}, u32[]{:S(2)}, u32[]{:S(2)}) collective-permute-start(f32[256,256]{1,0:T(8,128)S(1)} %select_add_fusion), channel_id=1, source_target_pairs={{0,8},{1,9},{2,10},{3,11},{4,12},{5,13},{6,14},{7,15},{8,0},{9,1},... | collective-permute-start | bytes 786440 | tf_op jit(solution)/shard_map/ppermute | solution.py:247
  53.4 0.3 convolution_add_fusion.odd
  53.7 0.8 %collective-permute-done.21.even = f32[256,256]{1,0:T(8,128)S(1)} collective-permute-done((f32[256,256]{1,0:T(8,128)S(1)}, f32[256,256]{1,0:T(8,128)S(1)}, u32[]{:S(2)}, u32[]{:S(2)}) %collective-permute-start.21) | collective-permute-done | bytes 262176 | tf_op jit(solution)/shard_map/ppermute | solution.py:247
  54.5 1.1 %shard_map.51 = (f32[256,256]{1,0:T(8,128)}, f32[256,256]{1,0:T(8,128)}) custom-call(f32[256,256]{1,0:T(8,128)S(1)} %convolution_add_fusion.odd, f32[256,256]{1,0:T(8,128)S(1)} %collective-permute-done.21.even, f32[256,256]{1,0:T(8,128)S(1)} %broadcast_select_fusion.refl), custom_call_target="tpu_custom_call" | custom-call | tf_op jit(solution)/shard_map/pallas_call | solution.py:208
  (5 shorter events, 0.1 us)
Async XLA Ops:
  0.7 8.3 %copy-start = (f32[1,1,4,256,256]{4,3,2,1,0:T(8,128)S(1)}, f32[1,1,4,256,256]{4,3,2,1,0:T(8,128)}, u32[]{:S(2)}) copy-start(f32[1,1,4,256,256]{4,3,2,1,0:T(8,128)} %param.2) | copy-start | bytes 3145732
  1.7 7.2 %collective-permute-start.1 = (f32[256,256]{1,0:T(8,128)S(1)}, f32[256,256]{1,0:T(8,128)S(1)}, u32[]{:S(2)}, u32[]{:S(2)}) collective-permute-start(f32[256,256]{1,0:T(8,128)S(1)} %dynamic-slice_bitcast_fusion.1), channel_id=1, source_target_pairs={{0,8},{1,0},{2,10},{3,2},{4,12},{5,4},{6,7},{7,6},{8,9},{9,1},{10,... | collective-permute-start | bytes 786440 | tf_op jit(solution)/shard_map/ppermute | solution.py:247
  4.2 10.4 %collective-permute-start.2 = (f32[256,256]{1,0:T(8,128)S(1)}, f32[256,256]{1,0:T(8,128)S(1)}, u32[]{:S(2)}, u32[]{:S(2)}) collective-permute-start(f32[256,256]{1,0:T(8,128)S(1)} %get-tuple-element.50), channel_id=1, source_target_pairs={{0,8},{1,0},{2,10},{3,2},{4,12},{5,4},{6,7},{7,6},{8,9},{9,1},{10,... | collective-permute-start | bytes 786440 | tf_op jit(solution)/shard_map/ppermute | solution.py:247
  4.5 10.6 %collective-permute-start.4 = (f32[256,256]{1,0:T(8,128)S(1)}, f32[256,256]{1,0:T(8,128)S(1)}, u32[]{:S(2)}, u32[]{:S(2)}) collective-permute-start(f32[256,256]{1,0:T(8,128)S(1)} %get-tuple-element.49), channel_id=1, source_target_pairs={{0,8},{1,0},{2,10},{3,2},{4,12},{5,4},{6,14},{7,15},{8,9},{9,1},{1... | collective-permute-start | bytes 786440 | tf_op jit(solution)/shard_map/ppermute | solution.py:247
  5.7 9.8 %collective-permute-start.5 = (f32[256,256]{1,0:T(8,128)S(1)}, f32[256,256]{1,0:T(8,128)S(1)}, u32[]{:S(2)}, u32[]{:S(2)}) collective-permute-start(f32[256,256]{1,0:T(8,128)S(1)} %get-tuple-element.48), channel_id=1, source_target_pairs={{0,8},{1,0},{2,10},{3,2},{4,12},{5,4},{6,14},{7,15},{8,9},{9,1},{1... | collective-permute-start | bytes 786440 | tf_op jit(solution)/shard_map/ppermute | solution.py:247
  10.6 6.6 %collective-permute-start.6 = (f32[256,256]{1,0:T(8,128)S(1)}, f32[256,256]{1,0:T(8,128)S(1)}, u32[]{:S(2)}, u32[]{:S(2)}) collective-permute-start(f32[256,256]{1,0:T(8,128)S(1)} %get-tuple-element.33.o0), channel_id=1, source_target_pairs={{0,2},{1,9},{2,10},{3,1},{4,12},{5,6},{6,4},{7,15},{8,0},{9,11},{1... | collective-permute-start | bytes 786440 | tf_op jit(solution)/shard_map/ppermute | solution.py:247
  15.0 7.4 %collective-permute-start.3 = (f32[256,256]{1,0:T(8,128)S(1)}, f32[256,256]{1,0:T(8,128)S(1)}, u32[]{:S(2)}, u32[]{:S(2)}) collective-permute-start(f32[256,256]{1,0:T(8,128)S(1)} %get-tuple-element.32.o1), channel_id=1, source_target_pairs={{0,2},{1,9},{2,10},{3,1},{4,12},{5,6},{6,4},{7,15},{8,0},{9,11},{1... | collective-permute-start | bytes 786440 | tf_op jit(solution)/shard_map/ppermute | solution.py:247
  15.6 8.6 %collective-permute-start.8 = (f32[256,256]{1,0:T(8,128)S(1)}, f32[256,256]{1,0:T(8,128)S(1)}, u32[]{:S(2)}, u32[]{:S(2)}) collective-permute-start(f32[256,256]{1,0:T(8,128)S(1)} %add.33.o3), channel_id=1, source_target_pairs={{0,2},{1,9},{2,10},{3,1},{4,12},{5,13},{6,14},{7,15},{8,0},{9,11},... | collective-permute-start | bytes 786440 | tf_op jit(solution)/shard_map/ppermute | solution.py:247
  17.2 8.8 %collective-permute-start.9 = (f32[256,256]{1,0:T(8,128)S(1)}, f32[256,256]{1,0:T(8,128)S(1)}, u32[]{:S(2)}, u32[]{:S(2)}) collective-permute-start(f32[256,256]{1,0:T(8,128)S(1)} %get-tuple-element.35.o2), channel_id=1, source_target_pairs={{0,2},{1,9},{2,10},{3,1},{4,12},{5,13},{6,14},{7,15},{8,0},{9,11},... | collective-permute-start | bytes 786440 | tf_op jit(solution)/shard_map/ppermute | solution.py:247
  18.9 7.1 %collective-permute-start.10 = (f32[256,256]{1,0:T(8,128)S(1)}, f32[256,256]{1,0:T(8,128)S(1)}, u32[]{:S(2)}, u32[]{:S(2)}) collective-permute-start(f32[256,256]{1,0:T(8,128)S(1)} %get-tuple-element.41), channel_id=1, source_target_pairs={{0,8},{1,9},{2,10},{3,5},{4,2},{5,13},{6,14},{7,15},{8,0},{9,1},{1... | collective-permute-start | bytes 786440 | tf_op jit(solution)/shard_map/ppermute | solution.py:247
  22.7 5.9 %collective-permute-start.7 = (f32[256,256]{1,0:T(8,128)S(1)}, f32[256,256]{1,0:T(8,128)S(1)}, u32[]{:S(2)}, u32[]{:S(2)}) collective-permute-start(f32[256,256]{1,0:T(8,128)S(1)} %shard_map.46), channel_id=1, source_target_pairs={{0,8},{1,9},{2,10},{3,5},{4,2},{5,13},{6,14},{7,15},{8,0},{9,1},{1... | collective-permute-start | bytes 786440 | tf_op jit(solution)/shard_map/ppermute | solution.py:247
  28.9 6.9 %collective-permute-start.11 = (f32[256,256]{1,0:T(8,128)S(1)}, f32[256,256]{1,0:T(8,128)S(1)}, u32[]{:S(2)}, u32[]{:S(2)}) collective-permute-start(f32[256,256]{1,0:T(8,128)S(1)} %shard_map.49), channel_id=1, source_target_pairs={{2,0},{11,9},{18,16},{27,25}} | collective-permute-start | bytes 786440 | tf_op jit(solution)/shard_map/ppermute | solution.py:247
  29.5 6.9 %collective-permute-start.12 = (f32[256,256]{1,0:T(8,128)S(1)}, f32[256,256]{1,0:T(8,128)S(1)}, u32[]{:S(2)}, u32[]{:S(2)}) collective-permute-start(f32[256,256]{1,0:T(8,128)S(1)} %shard_map.49), channel_id=1, source_target_pairs={{0,8},{1,9},{2,4},{3,11},{4,12},{5,3},{6,14},{7,15},{8,0},{9,1},{1... | collective-permute-start | bytes 786440 | tf_op jit(solution)/shard_map/ppermute | solution.py:247
  29.6 7.5 %collective-permute-start.13 = (f32[256,256]{1,0:T(8,128)S(1)}, f32[256,256]{1,0:T(8,128)S(1)}, u32[]{:S(2)}, u32[]{:S(2)}) collective-permute-start(f32[256,256]{1,0:T(8,128)S(1)} %shard_map.49), channel_id=1, source_target_pairs={{0,8},{1,9},{2,6},{3,11},{4,12},{5,13},{6,14},{7,3},{8,0},{9,1},{1... | collective-permute-start | bytes 786440 | tf_op jit(solution)/shard_map/ppermute | solution.py:247
  32.9 2.7 %copy-start.1 = (f32[1,256,256]{2,1,0:T(8,128)S(1)}, f32[1,256,256]{2,1,0:T(8,128)}, u32[]{:S(2)}) copy-start(f32[1,256,256]{2,1,0:T(8,128)} %param.3) | copy-start | bytes 786436
  34.9 3.6 %collective-permute-start.16 = (f32[256,256]{1,0:T(8,128)S(1)}, f32[256,256]{1,0:T(8,128)S(1)}, u32[]{:S(2)}, u32[]{:S(2)}) collective-permute-start(f32[256,256]{1,0:T(8,128)S(1)} %shard_map.50), channel_id=1, source_target_pairs={{2,0},{11,9},{18,16},{27,25}} | collective-permute-start | bytes 786440 | tf_op jit(solution)/shard_map/ppermute | solution.py:247
  35.6 10.5 %collective-permute-start = (f32[256,256]{1,0:T(8,128)S(1)}, f32[256,256]{1,0:T(8,128)S(1)}, u32[]{:S(2)}, u32[]{:S(2)}) collective-permute-start(f32[256,256]{1,0:T(8,128)S(1)} %bitcast.24), channel_id=1, source_target_pairs={{0,8},{1,9},{2,10},{3,11},{4,12},{5,13},{6,14},{7,15},{8,0},{9,1},... | collective-permute-start | bytes 786440 | tf_op jit(solution)/shard_map/ppermute | solution.py:247
  35.7 6.1 %collective-permute-start.17 = (f32[256,256]{1,0:T(8,128)S(1)}, f32[256,256]{1,0:T(8,128)S(1)}, u32[]{:S(2)}, u32[]{:S(2)}) collective-permute-start(f32[256,256]{1,0:T(8,128)S(1)} %shard_map.50), channel_id=1, source_target_pairs={{2,4},{11,13},{18,20},{27,29}} | collective-permute-start | bytes 786440 | tf_op jit(solution)/shard_map/ppermute | solution.py:247
  36.4 5.4 %collective-permute-start.18 = (f32[256,256]{1,0:T(8,128)S(1)}, f32[256,256]{1,0:T(8,128)S(1)}, u32[]{:S(2)}, u32[]{:S(2)}) collective-permute-start(f32[256,256]{1,0:T(8,128)S(1)} %shard_map.50), channel_id=1, source_target_pairs={{2,6},{11,15},{18,22},{27,31}} | collective-permute-start | bytes 786440 | tf_op jit(solution)/shard_map/ppermute | solution.py:247
  37.2 9.0 %collective-permute-start.14 = (f32[256,256]{1,0:T(8,128)S(1)}, f32[256,256]{1,0:T(8,128)S(1)}, u32[]{:S(2)}, u32[]{:S(2)}) collective-permute-start(f32[256,256]{1,0:T(8,128)S(1)} %select_select_fusion.1), channel_id=1, source_target_pairs={{0,9},{2,11},{4,13},{6,15},{9,8},{11,10},{13,12},{15,14},{16,25},{... | collective-permute-start | bytes 786440 | tf_op jit(solution)/shard_map/ppermute | solution.py:247
  38.5 7.6 %collective-permute-start.15 = (f32[256,256]{1,0:T(8,128)S(1)}, f32[256,256]{1,0:T(8,128)S(1)}, u32[]{:S(2)}, u32[]{:S(2)}) collective-permute-start(f32[256,256]{1,0:T(8,128)S(1)} %select_select_fusion.1), channel_id=1, source_target_pairs={{0,8},{1,9},{2,10},{3,11},{4,12},{5,13},{6,14},{7,15},{8,0},{9,1},... | collective-permute-start | bytes 786440 | tf_op jit(solution)/shard_map/ppermute | solution.py:247
  41.9 8.3 %collective-permute-start.20 = (f32[256,256]{1,0:T(8,128)S(1)}, f32[256,256]{1,0:T(8,128)S(1)}, u32[]{:S(2)}, u32[]{:S(2)}) collective-permute-start(f32[256,256]{1,0:T(8,128)S(1)} %select_select_fusion), channel_id=1, source_target_pairs={{0,1},{1,9},{2,3},{3,11},{4,5},{5,13},{6,7},{7,15},{8,0},{9,8},{10... | collective-permute-start | bytes 786440 | tf_op jit(solution)/shard_map/ppermute | solution.py:247
  46.8 4.6 %collective-permute-start.19 = (f32[256,256]{1,0:T(8,128)S(1)}, f32[256,256]{1,0:T(8,128)S(1)}, u32[]{:S(2)}, u32[]{:S(2)}) collective-permute-start(f32[256,256]{1,0:T(8,128)S(1)} %fusion.1), channel_id=1, source_target_pairs={{0,8},{1,9},{2,10},{3,11},{4,12},{5,13},{6,14},{7,15},{8,24},{9,25... | collective-permute-start | bytes 786440 | tf_op jit(solution)/shard_map/ppermute | solution.py:247
  51.4 3.1 %collective-permute-start.21 = (f32[256,256]{1,0:T(8,128)S(1)}, f32[256,256]{1,0:T(8,128)S(1)}, u32[]{:S(2)}, u32[]{:S(2)}) collective-permute-start(f32[256,256]{1,0:T(8,128)S(1)} %select_add_fusion), channel_id=1, source_target_pairs={{0,8},{1,9},{2,10},{3,11},{4,12},{5,13},{6,14},{7,15},{8,0},{9,1},... | collective-permute-start | bytes 786440 | tf_op jit(solution)/shard_map/ppermute | solution.py:247

commit v5 on v4

--- a/solution.py
+++ b/solution.py
@@ -330,14 +330,14 @@
     def line(g, k):
         return (g, 2 * k + g % 2)
 
-    def hand_out(block, fill):
+    def hand_out(block, fill, order):
         level = levels - 1
         while level > 0:
             steps = []
             for far, near, _ in merges[level - 1]:
                 if level > 1:
                     below = {m[1]: m[0] for m in merges[level - 2]}
-                    steps.append([(near, below[far]), (near, far), (near, below[near])])
+                    steps.append([[(near, below[far]), (near, far), (near, below[near])][n] for n in order])
                 else:
                     steps.append([(near, far)])
             got = block
@@ -349,8 +349,8 @@
             level -= 2
         return block
 
-    trans, _ = lax.optimization_barrier((hand_out(trans, (True, True, False)), refl))
-    refl = hand_out(refl, (False, False, False))
+    trans, _ = lax.optimization_barrier((hand_out(trans, (True, True, True), (1, 0, 2)), refl))
+    refl = hand_out(refl, (False, False, False), (0, 1, 2))
 
     across = {}
     for g in range(groups):

time: 56.7 us -> 56.1 us (0.989); the launches traced: 55.6 us -> 55.6 us
  no operation moved by 1% of the time
where the time goes in v5:
time: 56.1 us; the launch traced here: 55.6 us
  starting transfers between devices  27.8 us (50%)
  Pallas kernels  12.8 us (23%)
  waiting for transfers between devices  10.6 us (19%)
  local copies, waits for them, and re-layouts  2.23 us (4%)
  matrix products  1.02 us (2%)
  between operations  0.94 us (2%)
    ppermute x22, starting transfers between devices, send(): return lax.ppermute(block, AXES, route)  27.8 us
    pallas_call x10, Pallas kernels, call(): pl.pallas_call(body, out_shape=[square] * outs, in_specs=[vmem] * len(blo...  11.7 us
    ppermute x22, waiting for transfers between devices, send(): return lax.ppermute(block, AXES, route)  10.6 us
    squeeze x1, local copies, waits for them, and re-layouts, shards(): lax.dynamic_index_in_dim(after, 2 - 2 * turned, keepdims=False)  1.16 us
  transfers between devices with their start and end apart: 22, of which 5 were waited for; matrix products, arithmetic and copies ran while one was open for 4% of the time, Pallas kernels for 21%

profile of v5, /device:TPU:25, one launch (start us, length us, event | category | flops | bytes accessed | tf_op | source)
XLA Modules:
  0.0 55.6 jit_solution(16022125780144923388)
XLA Ops:
  0.7 0.0 copy-start
  0.7 1.1 %dynamic-slice_bitcast_fusion.1 = f32[256,256]{1,0:T(8,128)S(1)} fusion(f32[1,1,4,256,256]{4,3,2,1,0:T(8,128)} %param.2, s32[]{:T(128)S(6)} %select_n.91), kind=kLoop, calls=%fused_computation.11 | loop fusion | bytes 524292 | tf_op jit(solution)/shard_map/jit(dynamic_index_in_dim)/squeeze | solution.py:296
  1.7 1.3 %collective-permute-start.1 = (f32[256,256]{1,0:T(8,128)S(1)}, f32[256,256]{1,0:T(8,128)S(1)}, u32[]{:S(2)}, u32[]{:S(2)}) collective-permute-start(f32[256,256]{1,0:T(8,128)S(1)} %dynamic-slice_bitcast_fusion.1), channel_id=1, source_target_pairs={{0,8},{1,0},{2,10},{3,2},{4,12},{5,4},{6,7},{7,6},{8,9},{9,1},{10,... | collective-permute-start | bytes 786440 | tf_op jit(solution)/shard_map/ppermute | solution.py:247
  3.0 1.2 %dynamic-slice_bitcast_fusion = (f32[256,256]{1,0:T(8,128)S(1)}, f32[256,256]{1,0:T(8,128)S(1)}, f32[256,256]{1,0:T(8,128)S(1)}) fusion(f32[4,256,256]{2,1,0:T(8,128)} %bitcast.21, s32[]{:T(128)S(6)} %select_n.92), kind=kLoop, calls=%fused_computation.8 | loop fusion | bytes 1572868 | tf_op jit(solution)/shard_map/jit(dynamic_index_in_dim)/squeeze | solution.py:299
  4.2 0.3 collective-permute-start.2
  4.5 1.2 %collective-permute-start.4 = (f32[256,256]{1,0:T(8,128)S(1)}, f32[256,256]{1,0:T(8,128)S(1)}, u32[]{:S(2)}, u32[]{:S(2)}) collective-permute-start(f32[256,256]{1,0:T(8,128)S(1)} %get-tuple-element.49), channel_id=1, source_target_pairs={{0,8},{1,0},{2,10},{3,2},{4,12},{5,4},{6,14},{7,15},{8,9},{9,1},{1... | collective-permute-start | bytes 786440 | tf_op jit(solution)/shard_map/ppermute | solution.py:247
  5.7 0.0 collective-permute-start.5
  5.7 3.3 %collective-permute-done.1.c0 = f32[256,256]{1,0:T(8,128)S(1)} collective-permute-done((f32[256,256]{1,0:T(8,128)S(1)}, f32[256,256]{1,0:T(8,128)S(1)}, u32[]{:S(2)}, u32[]{:S(2)}) %collective-permute-start.1) | collective-permute-done | bytes 262176 | tf_op jit(solution)/shard_map/ppermute | solution.py:247
  9.0 0.0 copy-done
  9.0 1.7 %shard_map.41 = (f32[256,256]{1,0:T(8,128)S(1)}, f32[256,256]{1,0:T(8,128)S(1)}, f32[256,256]{1,0:T(8,128)S(1)}, f32[256,256]{1,0:T(8,128)S(1)}) custom-call(f32[4,256,256]{2,1,0:T(8,128)S(1)} %bitcast.22, f32[256,256]{1,0:T(8,128)S(1)} %collective-permute-done.1.c0), custom_call_target="tpu_custom_call" | custom-call | tf_op jit(solution)/shard_map/pallas_call | solution.py:64
  10.6 0.1 collective-permute-start.6
  10.7 0.7 %shard_map.42 = (f32[256,256]{1,0:T(8,128)S(1)}, f32[256,256]{1,0:T(8,128)S(1)}) custom-call(f32[4,256,256]{2,1,0:T(8,128)S(1)} %bitcast.23, f32[256,256]{1,0:T(8,128)S(1)} %get-tuple-element.27.solver, f32[256,256]{1,0:T(8,128)S(1)} %get-tuple-element.28.bounce), custom_call_target="tpu_custom_call" | custom-call | tf_op jit(solution)/shard_map/pallas_call | solution.py:64
  11.4 3.2 %collective-permute-done.2.c1 = f32[256,256]{1,0:T(8,128)S(1)} collective-permute-done((f32[256,256]{1,0:T(8,128)S(1)}, f32[256,256]{1,0:T(8,128)S(1)}, u32[]{:S(2)}, u32[]{:S(2)}) %collective-permute-start.2) | collective-permute-done | bytes 262176 | tf_op jit(solution)/shard_map/ppermute | solution.py:247
  14.6 0.4 shard_map.43
  15.0 0.1 collective-permute-start.3
  15.1 0.0 collective-permute-done.4.c2
  15.1 0.4 shard_map.44
  15.5 0.0 collective-permute-done.5
  15.6 1.6 %collective-permute-start.8 = (f32[256,256]{1,0:T(8,128)S(1)}, f32[256,256]{1,0:T(8,128)S(1)}, u32[]{:S(2)}, u32[]{:S(2)}) collective-permute-start(f32[256,256]{1,0:T(8,128)S(1)} %add.33.o3), channel_id=1, source_target_pairs={{0,2},{1,9},{2,10},{3,1},{4,12},{5,13},{6,14},{7,15},{8,0},{9,11},... | collective-permute-start | bytes 786440 | tf_op jit(solution)/shard_map/ppermute | solution.py:247
  17.2 0.1 collective-permute-start.9
  17.2 0.0 collective-permute-done.6.refl_b.c0
  17.2 1.7 %shard_map.45 = (f32[256,256]{1,0:T(8,128)S(1)}, f32[256,256]{1,0:T(8,128)S(1)}) custom-call(f32[256,256]{1,0:T(8,128)S(1)} %get-tuple-element.33.o0, f32[256,256]{1,0:T(8,128)S(1)} %get-tuple-element.32.o1, f32[256,256]{1,0:T(8,128)S(1)} %get-tuple-element.35.o2, f32[256,256]{1,0:T(8,128)S(1)} %add.33.o3, f32[256,256]{1,0:T(8,128)S(1)} %collective-permute-done.6.refl_b.c0), custom_call_target="tpu_custom_call" | custom-call | tf_op jit(solution)/shard_map/pallas_call | solution.py:64
  18.9 3.5 %collective-permute-start.10 = (f32[256,256]{1,0:T(8,128)S(1)}, f32[256,256]{1,0:T(8,128)S(1)}, u32[]{:S(2)}, u32[]{:S(2)}) collective-permute-start(f32[256,256]{1,0:T(8,128)S(1)} %get-tuple-element.41), channel_id=1, source_target_pairs={{0,8},{1,9},{2,10},{3,5},{4,2},{5,13},{6,14},{7,15},{8,0},{9,1},{1... | collective-permute-start | bytes 786440 | tf_op jit(solution)/shard_map/ppermute | solution.py:247
  22.4 0.0 collective-permute-done.3.left.c1
  22.4 0.3 shard_map.46
  22.7 1.6 %collective-permute-start.7 = (f32[256,256]{1,0:T(8,128)S(1)}, f32[256,256]{1,0:T(8,128)S(1)}, u32[]{:S(2)}, u32[]{:S(2)}) collective-permute-start(f32[256,256]{1,0:T(8,128)S(1)} %shard_map.46), channel_id=1, source_target_pairs={{0,8},{1,9},{2,10},{3,5},{4,2},{5,13},{6,14},{7,15},{8,0},{9,1},{1... | collective-permute-start | bytes 786440 | tf_op jit(solution)/shard_map/ppermute | solution.py:247
  24.2 0.0 collective-permute-done.8.c3
  24.2 1.8 %shard_map.47 = (f32[256,256]{1,0:T(8,128)S(1)}, f32[256,256]{1,0:T(8,128)S(1)}, f32[256,256]{1,0:T(8,128)S(1)}) custom-call(f32[256,256]{1,0:T(8,128)S(1)} %get-tuple-element.33.o0, f32[256,256]{1,0:T(8,128)S(1)} %get-tuple-element.32.o1, f32[256,256]{1,0:T(8,128)S(1)} %get-tuple-element.35.o2, f32[256,256]{1,0:T(8,128)S(1)} %add.33.o3, ...), custom_call_target="tpu_custom_call" | custom-call | tf_op jit(solution)/shard_map/pallas_call | solution.py:64
  26.0 0.0 collective-permute-done.9.c2
  26.0 0.0 collective-permute-done.10.refl_b.low_refl
  26.1 2.5 %shard_map.48.right.down = f32[256,256]{1,0:T(8,128)S(1)} custom-call(f32[256,256]{1,0:T(8,128)S(1)} %get-tuple-element.39.back_a, f32[256,256]{1,0:T(8,128)S(1)} %get-tuple-element.40.trans_a, f32[256,256]{1,0:T(8,128)S(1)} %collective-permute-done.10.refl_b.low_refl), custom_call_target="tpu_custom_call" | custom-call | tf_op jit(solution)/shard_map/pallas_call | solution.py:64
  28.6 0.0 collective-permute-done.7.left
  28.6 0.3 shard_map.49
  28.9 0.1 collective-permute-start.11
  28.9 2.7 %collective-permute-start.12 = (f32[256,256]{1,0:T(8,128)S(1)}, f32[256,256]{1,0:T(8,128)S(1)}, u32[]{:S(2)}, u32[]{:S(2)}) collective-permute-start(f32[256,256]{1,0:T(8,128)S(1)} %shard_map.49), channel_id=1, source_target_pairs={{0,8},{1,9},{2,6},{3,11},{4,12},{5,13},{6,14},{7,3},{8,0},{9,1},{1... | collective-permute-start | bytes 786440 | tf_op jit(solution)/shard_map/ppermute | solution.py:247
  31.6 0.0 collective-permute-start.13
  31.6 2.0 %shard_map.50 = f32[256,256]{1,0:T(8,128)S(1)} custom-call(f32[256,256]{1,0:T(8,128)S(1)} %get-tuple-element.33.o0, f32[256,256]{1,0:T(8,128)S(1)} %get-tuple-element.35.o2, f32[256,256]{1,0:T(8,128)S(1)} %add.33.o3, f32[256,256]{1,0:T(8,128)S(1)} %collective-permute-done.6.refl_b.c0, f32[256,256]{1,0:T(8,128)S(1)} %collective-permute-done.3.left.c1, ...), custom_call_target="tpu_custom_call" | custom-call | tf_op jit(solution)/shard_map/pallas_call | solution.py:64
  33.7 0.7 %collective-permute-start.16 = (f32[256,256]{1,0:T(8,128)S(1)}, f32[256,256]{1,0:T(8,128)S(1)}, u32[]{:S(2)}, u32[]{:S(2)}) collective-permute-start(f32[256,256]{1,0:T(8,128)S(1)} %shard_map.50), channel_id=1, source_target_pairs={{2,0},{11,9},{18,16},{27,25}} | collective-permute-start | bytes 786440 | tf_op jit(solution)/shard_map/ppermute | solution.py:247
  34.3 0.6 %collective-permute-start = (f32[256,256]{1,0:T(8,128)S(1)}, f32[256,256]{1,0:T(8,128)S(1)}, u32[]{:S(2)}, u32[]{:S(2)}) collective-permute-start(f32[256,256]{1,0:T(8,128)S(1)} %bitcast.24), channel_id=1, source_target_pairs={{0,8},{1,9},{2,10},{3,11},{4,12},{5,13},{6,14},{7,15},{8,0},{9,1},... | collective-permute-start | bytes 786440 | tf_op jit(solution)/shard_map/ppermute | solution.py:247
  34.9 0.0 collective-permute-done.11
  34.9 0.7 %collective-permute-start.17 = (f32[256,256]{1,0:T(8,128)S(1)}, f32[256,256]{1,0:T(8,128)S(1)}, u32[]{:S(2)}, u32[]{:S(2)}) collective-permute-start(f32[256,256]{1,0:T(8,128)S(1)} %shard_map.50), channel_id=1, source_target_pairs={{2,4},{11,13},{18,20},{27,29}} | collective-permute-start | bytes 786440 | tf_op jit(solution)/shard_map/ppermute | solution.py:247
  35.6 0.0 collective-permute-done.12
  35.6 0.7 %collective-permute-start.18 = (f32[256,256]{1,0:T(8,128)S(1)}, f32[256,256]{1,0:T(8,128)S(1)}, u32[]{:S(2)}, u32[]{:S(2)}) collective-permute-start(f32[256,256]{1,0:T(8,128)S(1)} %shard_map.50), channel_id=1, source_target_pairs={{2,6},{11,15},{18,22},{27,31}} | collective-permute-start | bytes 786440 | tf_op jit(solution)/shard_map/ppermute | solution.py:247
  36.3 0.0 collective-permute-done.13
  36.3 0.1 select_select_fusion.1
  36.4 1.3 %collective-permute-start.14 = (f32[256,256]{1,0:T(8,128)S(1)}, f32[256,256]{1,0:T(8,128)S(1)}, u32[]{:S(2)}, u32[]{:S(2)}) collective-permute-start(f32[256,256]{1,0:T(8,128)S(1)} %select_select_fusion.1), channel_id=1, source_target_pairs={{0,9},{2,11},{4,13},{6,15},{9,8},{11,10},{13,12},{15,14},{16,25},{... | collective-permute-start | bytes 786440 | tf_op jit(solution)/shard_map/ppermute | solution.py:247
  37.7 0.0 collective-permute-done.16
  37.7 1.8 %collective-permute-start.15 = (f32[256,256]{1,0:T(8,128)S(1)}, f32[256,256]{1,0:T(8,128)S(1)}, u32[]{:S(2)}, u32[]{:S(2)}) collective-permute-start(f32[256,256]{1,0:T(8,128)S(1)} %select_select_fusion.1), channel_id=1, source_target_pairs={{0,8},{1,9},{2,10},{3,11},{4,12},{5,13},{6,14},{7,15},{8,0},{9,1},... | collective-permute-start | bytes 786440 | tf_op jit(solution)/shard_map/ppermute | solution.py:247
  39.4 0.0 collective-permute-done.17
  39.4 0.0 collective-permute-done.18
  39.5 0.1 select_select_fusion
  39.5 6.6 %collective-permute-start.20 = (f32[256,256]{1,0:T(8,128)S(1)}, f32[256,256]{1,0:T(8,128)S(1)}, u32[]{:S(2)}, u32[]{:S(2)}) collective-permute-start(f32[256,256]{1,0:T(8,128)S(1)} %select_select_fusion), channel_id=1, source_target_pairs={{0,1},{1,9},{2,3},{3,11},{4,5},{5,13},{6,7},{7,15},{8,0},{9,8},{10... | collective-permute-start | bytes 786440 | tf_op jit(solution)/shard_map/ppermute | solution.py:247
  46.1 0.0 collective-permute-done
  46.1 0.0 collective-permute-done.14
  46.1 0.0 collective-permute-done.15
  46.1 0.3 fusion
  46.5 0.3 fusion.1
  46.8 1.3 %collective-permute-start.19 = (f32[256,256]{1,0:T(8,128)S(1)}, f32[256,256]{1,0:T(8,128)S(1)}, u32[]{:S(2)}, u32[]{:S(2)}) collective-permute-start(f32[256,256]{1,0:T(8,128)S(1)} %fusion.1), channel_id=1, source_target_pairs={{0,8},{1,9},{2,10},{3,11},{4,12},{5,13},{6,14},{7,15},{8,24},{9,25... | collective-permute-start | bytes 786440 | tf_op jit(solution)/shard_map/ppermute | solution.py:247
  48.1 1.1 %collective-permute-done.20 = f32[256,256]{1,0:T(8,128)S(1)} collective-permute-done((f32[256,256]{1,0:T(8,128)S(1)}, f32[256,256]{1,0:T(8,128)S(1)}, u32[]{:S(2)}, u32[]{:S(2)}) %collective-permute-start.20) | collective-permute-done | bytes 262176 | tf_op jit(solution)/shard_map/ppermute | solution.py:247
  49.2 2.2 %collective-permute-done.19 = f32[256,256]{1,0:T(8,128)S(1)} collective-permute-done((f32[256,256]{1,0:T(8,128)S(1)}, f32[256,256]{1,0:T(8,128)S(1)}, u32[]{:S(2)}, u32[]{:S(2)}) %collective-permute-start.19) | collective-permute-done | bytes 262176 | tf_op jit(solution)/shard_map/ppermute | solution.py:247
  51.4 1.9 %collective-permute-start.21 = (f32[256,256]{1,0:T(8,128)S(1)}, f32[256,256]{1,0:T(8,128)S(1)}, u32[]{:S(2)}, u32[]{:S(2)}) collective-permute-start(f32[256,256]{1,0:T(8,128)S(1)} %select_add_fusion), channel_id=1, source_target_pairs={{0,8},{1,9},{2,10},{3,11},{4,12},{5,13},{6,14},{7,15},{8,0},{9,1},... | collective-permute-start | bytes 786440 | tf_op jit(solution)/shard_map/ppermute | solution.py:247
  53.4 0.3 convolution_add_fusion.odd
  53.7 0.8 %collective-permute-done.21.even = f32[256,256]{1,0:T(8,128)S(1)} collective-permute-done((f32[256,256]{1,0:T(8,128)S(1)}, f32[256,256]{1,0:T(8,128)S(1)}, u32[]{:S(2)}, u32[]{:S(2)}) %collective-permute-start.21) | collective-permute-done | bytes 262176 | tf_op jit(solution)/shard_map/ppermute | solution.py:247
  54.5 1.1 %shard_map.51 = (f32[256,256]{1,0:T(8,128)}, f32[256,256]{1,0:T(8,128)}) custom-call(f32[256,256]{1,0:T(8,128)S(1)} %convolution_add_fusion.odd, f32[256,256]{1,0:T(8,128)S(1)} %collective-permute-done.21.even, f32[256,256]{1,0:T(8,128)S(1)} %broadcast_select_fusion.refl), custom_call_target="tpu_custom_call" | custom-call | tf_op jit(solution)/shard_map/pallas_call | solution.py:208
  (5 shorter events, 0.1 us)
Async XLA Ops:
  0.7 8.3 %copy-start = (f32[1,1,4,256,256]{4,3,2,1,0:T(8,128)S(1)}, f32[1,1,4,256,256]{4,3,2,1,0:T(8,128)}, u32[]{:S(2)}) copy-start(f32[1,1,4,256,256]{4,3,2,1,0:T(8,128)} %param.2) | copy-start | bytes 3145732
  1.7 7.2 %collective-permute-start.1 = (f32[256,256]{1,0:T(8,128)S(1)}, f32[256,256]{1,0:T(8,128)S(1)}, u32[]{:S(2)}, u32[]{:S(2)}) collective-permute-start(f32[256,256]{1,0:T(8,128)S(1)} %dynamic-slice_bitcast_fusion.1), channel_id=1, source_target_pairs={{0,8},{1,0},{2,10},{3,2},{4,12},{5,4},{6,7},{7,6},{8,9},{9,1},{10,... | collective-permute-start | bytes 786440 | tf_op jit(solution)/shard_map/ppermute | solution.py:247
  4.2 10.4 %collective-permute-start.2 = (f32[256,256]{1,0:T(8,128)S(1)}, f32[256,256]{1,0:T(8,128)S(1)}, u32[]{:S(2)}, u32[]{:S(2)}) collective-permute-start(f32[256,256]{1,0:T(8,128)S(1)} %get-tuple-element.50), channel_id=1, source_target_pairs={{0,8},{1,0},{2,10},{3,2},{4,12},{5,4},{6,7},{7,6},{8,9},{9,1},{10,... | collective-permute-start | bytes 786440 | tf_op jit(solution)/shard_map/ppermute | solution.py:247
  4.5 10.6 %collective-permute-start.4 = (f32[256,256]{1,0:T(8,128)S(1)}, f32[256,256]{1,0:T(8,128)S(1)}, u32[]{:S(2)}, u32[]{:S(2)}) collective-permute-start(f32[256,256]{1,0:T(8,128)S(1)} %get-tuple-element.49), channel_id=1, source_target_pairs={{0,8},{1,0},{2,10},{3,2},{4,12},{5,4},{6,14},{7,15},{8,9},{9,1},{1... | collective-permute-start | bytes 786440 | tf_op jit(solution)/shard_map/ppermute | solution.py:247
  5.7 9.8 %collective-permute-start.5 = (f32[256,256]{1,0:T(8,128)S(1)}, f32[256,256]{1,0:T(8,128)S(1)}, u32[]{:S(2)}, u32[]{:S(2)}) collective-permute-start(f32[256,256]{1,0:T(8,128)S(1)} %get-tuple-element.48), channel_id=1, source_target_pairs={{0,8},{1,0},{2,10},{3,2},{4,12},{5,4},{6,14},{7,15},{8,9},{9,1},{1... | collective-permute-start | bytes 786440 | tf_op jit(solution)/shard_map/ppermute | solution.py:247
  10.6 6.6 %collective-permute-start.6 = (f32[256,256]{1,0:T(8,128)S(1)}, f32[256,256]{1,0:T(8,128)S(1)}, u32[]{:S(2)}, u32[]{:S(2)}) collective-permute-start(f32[256,256]{1,0:T(8,128)S(1)} %get-tuple-element.33.o0), channel_id=1, source_target_pairs={{0,2},{1,9},{2,10},{3,1},{4,12},{5,6},{6,4},{7,15},{8,0},{9,11},{1... | collective-permute-start | bytes 786440 | tf_op jit(solution)/shard_map/ppermute | solution.py:247
  15.0 7.4 %collective-permute-start.3 = (f32[256,256]{1,0:T(8,128)S(1)}, f32[256,256]{1,0:T(8,128)S(1)}, u32[]{:S(2)}, u32[]{:S(2)}) collective-permute-start(f32[256,256]{1,0:T(8,128)S(1)} %get-tuple-element.32.o1), channel_id=1, source_target_pairs={{0,2},{1,9},{2,10},{3,1},{4,12},{5,6},{6,4},{7,15},{8,0},{9,11},{1... | collective-permute-start | bytes 786440 | tf_op jit(solution)/shard_map/ppermute | solution.py:247
  15.6 8.6 %collective-permute-start.8 = (f32[256,256]{1,0:T(8,128)S(1)}, f32[256,256]{1,0:T(8,128)S(1)}, u32[]{:S(2)}, u32[]{:S(2)}) collective-permute-start(f32[256,256]{1,0:T(8,128)S(1)} %add.33.o3), channel_id=1, source_target_pairs={{0,2},{1,9},{2,10},{3,1},{4,12},{5,13},{6,14},{7,15},{8,0},{9,11},... | collective-permute-start | bytes 786440 | tf_op jit(solution)/shard_map/ppermute | solution.py:247
  17.2 8.8 %collective-permute-start.9 = (f32[256,256]{1,0:T(8,128)S(1)}, f32[256,256]{1,0:T(8,128)S(1)}, u32[]{:S(2)}, u32[]{:S(2)}) collective-permute-start(f32[256,256]{1,0:T(8,128)S(1)} %get-tuple-element.35.o2), channel_id=1, source_target_pairs={{0,2},{1,9},{2,10},{3,1},{4,12},{5,13},{6,14},{7,15},{8,0},{9,11},... | collective-permute-start | bytes 786440 | tf_op jit(solution)/shard_map/ppermute | solution.py:247
  18.9 7.1 %collective-permute-start.10 = (f32[256,256]{1,0:T(8,128)S(1)}, f32[256,256]{1,0:T(8,128)S(1)}, u32[]{:S(2)}, u32[]{:S(2)}) collective-permute-start(f32[256,256]{1,0:T(8,128)S(1)} %get-tuple-element.41), channel_id=1, source_target_pairs={{0,8},{1,9},{2,10},{3,5},{4,2},{5,13},{6,14},{7,15},{8,0},{9,1},{1... | collective-permute-start | bytes 786440 | tf_op jit(solution)/shard_map/ppermute | solution.py:247
  22.7 5.9 %collective-permute-start.7 = (f32[256,256]{1,0:T(8,128)S(1)}, f32[256,256]{1,0:T(8,128)S(1)}, u32[]{:S(2)}, u32[]{:S(2)}) collective-permute-start(f32[256,256]{1,0:T(8,128)S(1)} %shard_map.46), channel_id=1, source_target_pairs={{0,8},{1,9},{2,10},{3,5},{4,2},{5,13},{6,14},{7,15},{8,0},{9,1},{1... | collective-permute-start | bytes 786440 | tf_op jit(solution)/shard_map/ppermute | solution.py:247
  28.9 6.1 %collective-permute-start.11 = (f32[256,256]{1,0:T(8,128)S(1)}, f32[256,256]{1,0:T(8,128)S(1)}, u32[]{:S(2)}, u32[]{:S(2)}) collective-permute-start(f32[256,256]{1,0:T(8,128)S(1)} %shard_map.49), channel_id=1, source_target_pairs={{0,8},{1,3},{2,0},{3,11},{4,12},{5,13},{6,14},{7,15},{8,10},{9,1},... | collective-permute-start | bytes 786440 | tf_op jit(solution)/shard_map/ppermute | solution.py:247
  28.9 6.7 %collective-permute-start.12 = (f32[256,256]{1,0:T(8,128)S(1)}, f32[256,256]{1,0:T(8,128)S(1)}, u32[]{:S(2)}, u32[]{:S(2)}) collective-permute-start(f32[256,256]{1,0:T(8,128)S(1)} %shard_map.49), channel_id=1, source_target_pairs={{0,8},{1,9},{2,6},{3,11},{4,12},{5,13},{6,14},{7,3},{8,0},{9,1},{1... | collective-permute-start | bytes 786440 | tf_op jit(solution)/shard_map/ppermute | solution.py:247
  31.6 4.7 %collective-permute-start.13 = (f32[256,256]{1,0:T(8,128)S(1)}, f32[256,256]{1,0:T(8,128)S(1)}, u32[]{:S(2)}, u32[]{:S(2)}) collective-permute-start(f32[256,256]{1,0:T(8,128)S(1)} %shard_map.49), channel_id=1, source_target_pairs={{0,8},{1,9},{2,4},{3,11},{4,12},{5,3},{6,14},{7,15},{8,0},{9,1},{1... | collective-permute-start | bytes 786440 | tf_op jit(solution)/shard_map/ppermute | solution.py:247
  31.6 2.7 %copy-start.1 = (f32[1,256,256]{2,1,0:T(8,128)S(1)}, f32[1,256,256]{2,1,0:T(8,128)}, u32[]{:S(2)}) copy-start(f32[1,256,256]{2,1,0:T(8,128)} %param.3) | copy-start | bytes 786436
  33.7 4.0 %collective-permute-start.16 = (f32[256,256]{1,0:T(8,128)S(1)}, f32[256,256]{1,0:T(8,128)S(1)}, u32[]{:S(2)}, u32[]{:S(2)}) collective-permute-start(f32[256,256]{1,0:T(8,128)S(1)} %shard_map.50), channel_id=1, source_target_pairs={{2,0},{11,9},{18,16},{27,25}} | collective-permute-start | bytes 786440 | tf_op jit(solution)/shard_map/ppermute | solution.py:247
  34.3 11.8 %collective-permute-start = (f32[256,256]{1,0:T(8,128)S(1)}, f32[256,256]{1,0:T(8,128)S(1)}, u32[]{:S(2)}, u32[]{:S(2)}) collective-permute-start(f32[256,256]{1,0:T(8,128)S(1)} %bitcast.24), channel_id=1, source_target_pairs={{0,8},{1,9},{2,10},{3,11},{4,12},{5,13},{6,14},{7,15},{8,0},{9,1},... | collective-permute-start | bytes 786440 | tf_op jit(solution)/shard_map/ppermute | solution.py:247
  34.9 4.5 %collective-permute-start.17 = (f32[256,256]{1,0:T(8,128)S(1)}, f32[256,256]{1,0:T(8,128)S(1)}, u32[]{:S(2)}, u32[]{:S(2)}) collective-permute-start(f32[256,256]{1,0:T(8,128)S(1)} %shard_map.50), channel_id=1, source_target_pairs={{2,4},{11,13},{18,20},{27,29}} | collective-permute-start | bytes 786440 | tf_op jit(solution)/shard_map/ppermute | solution.py:247
  35.6 3.8 %collective-permute-start.18 = (f32[256,256]{1,0:T(8,128)S(1)}, f32[256,256]{1,0:T(8,128)S(1)}, u32[]{:S(2)}, u32[]{:S(2)}) collective-permute-start(f32[256,256]{1,0:T(8,128)S(1)} %shard_map.50), channel_id=1, source_target_pairs={{2,6},{11,15},{18,22},{27,31}} | collective-permute-start | bytes 786440 | tf_op jit(solution)/shard_map/ppermute | solution.py:247
  36.4 9.8 %collective-permute-start.14 = (f32[256,256]{1,0:T(8,128)S(1)}, f32[256,256]{1,0:T(8,128)S(1)}, u32[]{:S(2)}, u32[]{:S(2)}) collective-permute-start(f32[256,256]{1,0:T(8,128)S(1)} %select_select_fusion.1), channel_id=1, source_target_pairs={{0,9},{2,11},{4,13},{6,15},{9,8},{11,10},{13,12},{15,14},{16,25},{... | collective-permute-start | bytes 786440 | tf_op jit(solution)/shard_map/ppermute | solution.py:247
  37.7 8.5 %collective-permute-start.15 = (f32[256,256]{1,0:T(8,128)S(1)}, f32[256,256]{1,0:T(8,128)S(1)}, u32[]{:S(2)}, u32[]{:S(2)}) collective-permute-start(f32[256,256]{1,0:T(8,128)S(1)} %select_select_fusion.1), channel_id=1, source_target_pairs={{0,8},{1,9},{2,10},{3,11},{4,12},{5,13},{6,14},{7,15},{8,0},{9,1},... | collective-permute-start | bytes 786440 | tf_op jit(solution)/shard_map/ppermute | solution.py:247
  39.5 9.7 %collective-permute-start.20 = (f32[256,256]{1,0:T(8,128)S(1)}, f32[256,256]{1,0:T(8,128)S(1)}, u32[]{:S(2)}, u32[]{:S(2)}) collective-permute-start(f32[256,256]{1,0:T(8,128)S(1)} %select_select_fusion), channel_id=1, source_target_pairs={{0,1},{1,9},{2,3},{3,11},{4,5},{5,13},{6,7},{7,15},{8,0},{9,8},{10... | collective-permute-start | bytes 786440 | tf_op jit(solution)/shard_map/ppermute | solution.py:247
  46.8 4.6 %collective-permute-start.19 = (f32[256,256]{1,0:T(8,128)S(1)}, f32[256,256]{1,0:T(8,128)S(1)}, u32[]{:S(2)}, u32[]{:S(2)}) collective-permute-start(f32[256,256]{1,0:T(8,128)S(1)} %fusion.1), channel_id=1, source_target_pairs={{0,8},{1,9},{2,10},{3,11},{4,12},{5,13},{6,14},{7,15},{8,24},{9,25... | collective-permute-start | bytes 786440 | tf_op jit(solution)/shard_map/ppermute | solution.py:247
  51.4 3.1 %collective-permute-start.21 = (f32[256,256]{1,0:T(8,128)S(1)}, f32[256,256]{1,0:T(8,128)S(1)}, u32[]{:S(2)}, u32[]{:S(2)}) collective-permute-start(f32[256,256]{1,0:T(8,128)S(1)} %select_add_fusion), channel_id=1, source_target_pairs={{0,8},{1,9},{2,10},{3,11},{4,12},{5,13},{6,14},{7,15},{8,0},{9,1},... | collective-permute-start | bytes 786440 | tf_op jit(solution)/shard_map/ppermute | solution.py:247

commit v6 on v5

--- a/solution.py
+++ b/solution.py
@@ -72,23 +72,46 @@
     return list(results)
 
 
-def first_step(marks, own, c0, out0, down, solver, bounce, power, total):
-    turned = 2 * marks()[0]
-    refl, trans, behind, upward = own[turned], own[1 + turned], own[2 - turned], own[3 - turned]
-    bounce[...] = product(upward, c0[...])
+def first_step(marks, refl, trans, up, behind, c0, out0, down, solver, bounce, power, total):
+    turned = marks()[0] == 1
+    bounce[...] = product(jnp.where(turned, trans[...], up[...]), c0[...])
 
     def use(value):
         solver[...] = value
-        down[...] = product(value, trans)
-        out0[...] = refl + product(bounce[...], down[...])
-
-    solve(product(behind, c0[...]), use, power, total)
-
-
-def first_rest(marks, own, solver, bounce, back, up):
+        down[...] = product(value, jnp.where(turned, up[...], trans[...]))
+        out0[...] = refl[...] + product(bounce[...], down[...])
+
+    solve(product(behind[...], c0[...]), use, power, total)
+
+
+def first_rest(marks, trans, up, behind, solver, bounce, back, upward):
+    turned = marks()[0] == 1
+    back[...] = product(solver[...], behind[...])
+    upward[...] = jnp.where(turned, trans[...], up[...]) + product(bounce[...], back[...])
+
+
+def pick(marks, which, own, *rest):
+    outs, sems = rest[:-1], rest[-1]
     turned = 2 * marks()[0]
-    back[...] = product(solver[...], own[2 - turned])
-    up[...] = own[3 - turned] + product(bounce[...], back[...])
+    places = (turned, 1, 3, 2 - turned)
+    copies = [pltpu.make_async_copy(own.at[places[i]], out, sems.at[n]) for n, (i, out) in enumerate(zip(which, outs))]
+    for copy in copies:
+        copy.start()
+    for copy in copies:
+        copy.wait()
+
+
+def picked(marks, which, own):
+    block = jax.ShapeDtypeStruct(own.shape[1:], jnp.float32)
+    vmem = pl.BlockSpec(memory_space=pltpu.VMEM)
+    return list(pl.pallas_call(
+        functools.partial(pick, marks, which),
+        out_shape=[block] * len(which),
+        in_specs=[pl.BlockSpec(memory_space=pltpu.HBM)],
+        out_specs=[vmem] * len(which),
+        scratch_shapes=[pltpu.SemaphoreType.DMA((len(which),))],
+        compiler_params=pltpu.CompilerParams(vmem_limit_bytes=12 * 2**20),
+    )(pltpu.with_memory_space_constraint(own, pltpu.HBM)))
 
 
 def second_step(marks, down, back, up, c1, out1, kept):
@@ -293,16 +316,16 @@
     injected = incident[0]
     spread = {guest(g, k): home(g, k) for g in range(groups) for k in range(pairs)}
     spread_late = {guest(g, k): home(g, k) for g in range(groups) for k in range(pairs - 1)}
-    chosen = lax.dynamic_index_in_dim(own, 2 * turned, keepdims=False)
-    chosen, after = lax.optimization_barrier((chosen, own))
-    came = [send(chosen, spread), send(after[1], spread), send(after[3], spread_late)]
-    came.append(send(lax.dynamic_index_in_dim(after, 2 - 2 * turned, keepdims=False), spread_late))
     first = functools.partial(marks, 1)
+    mine = picked(first, (0,), own)
+    later, _ = lax.optimization_barrier((own, mine[0]))
+    mine += picked(first, (1, 2, 3), later)
+    came = [send(block, spread if n < 2 else spread_late) for n, block in enumerate(mine)]
     split_level = levels - 2
     late = split_level == 1
-    out0, down, solver, bounce = call(functools.partial(first_step, first), [own, came[0]], 4, True)
+    out0, down, solver, bounce = call(functools.partial(first_step, first), mine + came[:1], 4, True)
     sent = [send(out0, routes(1))]
-    back, up = call(functools.partial(first_rest, first), [own, solver, bounce], 2)
+    back, up = call(functools.partial(first_rest, first), mine[1:] + [solver, bounce], 2)
     out1, kept = call(functools.partial(second_step, first), [down, back, up, came[1]], 2)
     sent.append(send(out1, routes(1)))
     out2, rest = call(functools.partial(third_step, first), [down, up, kept, came[2]], 2)
@@ -330,7 +353,7 @@
     def line(g, k):
         return (g, 2 * k + g % 2)
 
-    def hand_out(block, fill, order):
+    def hand_out(block, fill, order, last=0):
         level = levels - 1
         while level > 0:
             steps = []
@@ -343,17 +366,17 @@
             got = block
             for step, full in zip(zip(*steps), fill):
                 fresh = is_one([target for _, target in step])
-                route = {line(g, a): line(g, b) for a, b in step for g in range(groups)}
+                route = {line(g, a): line(g, b) for a, b in step for g in range(groups - last)}
                 got = jnp.where(fresh, send(block, route, full), got)
             block = got
             level -= 2
         return block
 
-    trans, _ = lax.optimization_barrier((hand_out(trans, (True, True, True), (1, 0, 2)), refl))
+    trans, _ = lax.optimization_barrier((hand_out(trans, (True, True, True), (1, 0, 2), 1), refl))
     refl = hand_out(refl, (False, False, False), (0, 1, 2))
 
     across = {}
-    for g in range(groups):
+    for g in range(groups - 1):
         for k in range(pairs):
             across[line(g, k)] = (g | 1, 2 * k + 1 - g % 2)
     swap = {(g, s): (g ^ 1, s) for g in range(groups) for s in range(count)}

time: 56.1 us -> 56 us (level)
  local copies, waits for them, and re-layouts: 2.23 us -> 0.01 us
  Pallas kernels: 12.8 us -> 14.9 us
    squeeze x2 -> x0, local copies, waits for them, and re-layouts: 2.22 us -> none  [the longest x1 1.16 us: shards(): lax.dynamic_index_in_dim(after, 2 - 2 * turned, keepdims=False)]
    pallas_call x0 -> x2, Pallas kernels: none -> 2.11 us  [picked(): pl.pallas_call(functools.partial(pick, marks, which), out_shape=[block] *...]
  transfers between devices with their start and end apart: 22 -> 22, of which waited for: 5 -> 5; matrix products, arithmetic and copies ran while one was open for 4% -> 2% of each run, Pallas kernels for 21% -> 23%
where the time goes in v6:
time: 56 us; the launch traced here: 55.5 us
  starting transfers between devices  27.8 us (50%)
  Pallas kernels  14.9 us (27%)
  waiting for transfers between devices  10.6 us (19%)
  matrix products  1.01 us (2%)
  between operations  0.91 us (2%)
    ppermute x22, starting transfers between devices, send(): return lax.ppermute(block, AXES, route)  27.8 us
    pallas_call x10, Pallas kernels, call(): pl.pallas_call(body, out_shape=[square] * outs, in_specs=[vmem] * len(blo...  11.7 us
    ppermute x22, waiting for transfers between devices, send(): return lax.ppermute(block, AXES, route)  10.6 us
    pallas_call x2, Pallas kernels, picked(): pl.pallas_call(functools.partial(pick, marks, which), out_shape=[block] *...  2.11 us
  transfers between devices with their start and end apart: 22, of which 5 were waited for; matrix products, arithmetic and copies ran while one was open for 2% of the time, Pallas kernels for 23%

profile of v6, /device:TPU:25, one launch (start us, length us, event | category | flops | bytes accessed | tf_op | source)
XLA Modules:
  0.0 55.5 jit_solution(2663553613141744782)
XLA Ops:
  0.6 1.0 %shard_map.41.refl = f32[256,256]{1,0:T(8,128)S(1)} custom-call(f32[4,256,256]{2,1,0:T(8,128)} %bitcast.13), custom_call_target="tpu_custom_call" | custom-call | tf_op jit(solution)/shard_map/pallas_call | solution.py:107
  1.6 1.3 %collective-permute-start.1 = (f32[256,256]{1,0:T(8,128)S(1)}, f32[256,256]{1,0:T(8,128)S(1)}, u32[]{:S(2)}, u32[]{:S(2)}) collective-permute-start(f32[256,256]{1,0:T(8,128)S(1)} %shard_map.41.refl), channel_id=1, source_target_pairs={{0,8},{1,0},{2,10},{3,2},{4,12},{5,4},{6,7},{7,6},{8,9},{9,1},{10,... | collective-permute-start | bytes 786440 | tf_op jit(solution)/shard_map/ppermute | solution.py:270
  2.9 1.1 %shard_map.42 = (f32[256,256]{1,0:T(8,128)S(1)}, f32[256,256]{1,0:T(8,128)S(1)}, f32[256,256]{1,0:T(8,128)S(1)}) custom-call(f32[4,256,256]{2,1,0:T(8,128)} %bitcast.14), custom_call_target="tpu_custom_call" | custom-call | tf_op jit(solution)/shard_map/pallas_call | solution.py:107
  4.0 0.3 collective-permute-start.2
  4.3 1.2 %collective-permute-start.4 = (f32[256,256]{1,0:T(8,128)S(1)}, f32[256,256]{1,0:T(8,128)S(1)}, u32[]{:S(2)}, u32[]{:S(2)}) collective-permute-start(f32[256,256]{1,0:T(8,128)S(1)} %get-tuple-element.29.up), channel_id=1, source_target_pairs={{0,8},{1,0},{2,10},{3,2},{4,12},{5,4},{6,14},{7,15},{8,9},{9,1},{1... | collective-permute-start | bytes 786440 | tf_op jit(solution)/shard_map/ppermute | solution.py:270
  5.6 0.0 collective-permute-start.5
  5.6 3.3 %collective-permute-done.1.c0 = f32[256,256]{1,0:T(8,128)S(1)} collective-permute-done((f32[256,256]{1,0:T(8,128)S(1)}, f32[256,256]{1,0:T(8,128)S(1)}, u32[]{:S(2)}, u32[]{:S(2)}) %collective-permute-start.1) | collective-permute-done | bytes 262176 | tf_op jit(solution)/shard_map/ppermute | solution.py:270
  8.8 1.7 %shard_map.43 = (f32[256,256]{1,0:T(8,128)S(1)}, f32[256,256]{1,0:T(8,128)S(1)}, f32[256,256]{1,0:T(8,128)S(1)}, f32[256,256]{1,0:T(8,128)S(1)}) custom-call(f32[256,256]{1,0:T(8,128)S(1)} %shard_map.41.refl, f32[256,256]{1,0:T(8,128)S(1)} %get-tuple-element.28.trans, f32[256,256]{1,0:T(8,128)S(1)} %get-tuple-element.29.up, ...), custom_call_target="tpu_custom_call" | custom-call | tf_op jit(solution)/shard_map/pallas_call | solution.py:64
  10.5 0.1 collective-permute-start.6
  10.6 0.7 %shard_map.44 = (f32[256,256]{1,0:T(8,128)S(1)}, f32[256,256]{1,0:T(8,128)S(1)}) custom-call(f32[256,256]{1,0:T(8,128)S(1)} %get-tuple-element.28.trans, f32[256,256]{1,0:T(8,128)S(1)} %get-tuple-element.29.up, f32[256,256]{1,0:T(8,128)S(1)} %get-tuple-element.30.behind, f32[256,256]{1,0:T(8,128)S(1)} %get-tuple-element.32.solver, ...), custom_call_target="tpu_custom_call" | custom-call | tf_op jit(solution)/shard_map/pallas_call | solution.py:64
  11.3 3.2 %collective-permute-done.2.c1 = f32[256,256]{1,0:T(8,128)S(1)} collective-permute-done((f32[256,256]{1,0:T(8,128)S(1)}, f32[256,256]{1,0:T(8,128)S(1)}, u32[]{:S(2)}, u32[]{:S(2)}) %collective-permute-start.2) | collective-permute-done | bytes 262176 | tf_op jit(solution)/shard_map/ppermute | solution.py:270
  14.5 0.4 shard_map.45
  14.9 0.1 collective-permute-start.3
  15.0 0.0 collective-permute-done.4.c2
  15.0 0.4 shard_map.46
  15.4 0.0 collective-permute-done.5
  15.5 1.6 %collective-permute-start.8 = (f32[256,256]{1,0:T(8,128)S(1)}, f32[256,256]{1,0:T(8,128)S(1)}, u32[]{:S(2)}, u32[]{:S(2)}) collective-permute-start(f32[256,256]{1,0:T(8,128)S(1)} %add.22.o3), channel_id=1, source_target_pairs={{0,2},{1,9},{2,10},{3,1},{4,12},{5,13},{6,14},{7,15},{8,0},{9,11},... | collective-permute-start | bytes 786440 | tf_op jit(solution)/shard_map/ppermute | solution.py:270
  17.1 0.1 collective-permute-start.9
  17.1 0.0 collective-permute-done.6.refl_b.c0
  17.1 1.7 %shard_map.47 = (f32[256,256]{1,0:T(8,128)S(1)}, f32[256,256]{1,0:T(8,128)S(1)}) custom-call(f32[256,256]{1,0:T(8,128)S(1)} %get-tuple-element.37.o0, f32[256,256]{1,0:T(8,128)S(1)} %get-tuple-element.36.o1, f32[256,256]{1,0:T(8,128)S(1)} %get-tuple-element.39.o2, f32[256,256]{1,0:T(8,128)S(1)} %add.22.o3, f32[256,256]{1,0:T(8,128)S(1)} %collective-permute-done.6.refl_b.c0), custom_call_target="tpu_custom_call" | custom-call | tf_op jit(solution)/shard_map/pallas_call | solution.py:64
  18.8 3.5 %collective-permute-start.10 = (f32[256,256]{1,0:T(8,128)S(1)}, f32[256,256]{1,0:T(8,128)S(1)}, u32[]{:S(2)}, u32[]{:S(2)}) collective-permute-start(f32[256,256]{1,0:T(8,128)S(1)} %get-tuple-element.45), channel_id=1, source_target_pairs={{0,8},{1,9},{2,10},{3,5},{4,2},{5,13},{6,14},{7,15},{8,0},{9,1},{1... | collective-permute-start | bytes 786440 | tf_op jit(solution)/shard_map/ppermute | solution.py:270
  22.3 0.0 collective-permute-done.3.left.c1
  22.3 0.3 shard_map.48
  22.5 1.6 %collective-permute-start.7 = (f32[256,256]{1,0:T(8,128)S(1)}, f32[256,256]{1,0:T(8,128)S(1)}, u32[]{:S(2)}, u32[]{:S(2)}) collective-permute-start(f32[256,256]{1,0:T(8,128)S(1)} %shard_map.48), channel_id=1, source_target_pairs={{0,8},{1,9},{2,10},{3,5},{4,2},{5,13},{6,14},{7,15},{8,0},{9,1},{1... | collective-permute-start | bytes 786440 | tf_op jit(solution)/shard_map/ppermute | solution.py:270
  24.1 0.0 collective-permute-done.8.c3
  24.1 1.8 %shard_map.49 = (f32[256,256]{1,0:T(8,128)S(1)}, f32[256,256]{1,0:T(8,128)S(1)}, f32[256,256]{1,0:T(8,128)S(1)}) custom-call(f32[256,256]{1,0:T(8,128)S(1)} %get-tuple-element.37.o0, f32[256,256]{1,0:T(8,128)S(1)} %get-tuple-element.36.o1, f32[256,256]{1,0:T(8,128)S(1)} %get-tuple-element.39.o2, f32[256,256]{1,0:T(8,128)S(1)} %add.22.o3, ...), custom_call_target="tpu_custom_call" | custom-call | tf_op jit(solution)/shard_map/pallas_call | solution.py:64
  25.9 0.0 collective-permute-done.9.c2
  25.9 0.0 collective-permute-done.10.refl_b.low_refl
  25.9 2.5 %shard_map.50.right.down = f32[256,256]{1,0:T(8,128)S(1)} custom-call(f32[256,256]{1,0:T(8,128)S(1)} %get-tuple-element.43.back_a, f32[256,256]{1,0:T(8,128)S(1)} %get-tuple-element.44.trans_a, f32[256,256]{1,0:T(8,128)S(1)} %collective-permute-done.10.refl_b.low_refl), custom_call_target="tpu_custom_call" | custom-call | tf_op jit(solution)/shard_map/pallas_call | solution.py:64
  28.4 0.0 collective-permute-done.7.left
  28.5 0.3 shard_map.51
  28.7 0.1 collective-permute-start.11
  28.8 2.7 %collective-permute-start.12 = (f32[256,256]{1,0:T(8,128)S(1)}, f32[256,256]{1,0:T(8,128)S(1)}, u32[]{:S(2)}, u32[]{:S(2)}) collective-permute-start(f32[256,256]{1,0:T(8,128)S(1)} %shard_map.51), channel_id=1, source_target_pairs={{0,8},{1,9},{2,6},{3,11},{4,12},{5,13},{6,14},{7,3},{8,0},{9,1},{1... | collective-permute-start | bytes 786440 | tf_op jit(solution)/shard_map/ppermute | solution.py:270
  31.5 0.0 collective-permute-start.13
  31.5 0.0 copy-start
  31.5 2.0 %shard_map.52 = f32[256,256]{1,0:T(8,128)S(1)} custom-call(f32[256,256]{1,0:T(8,128)S(1)} %get-tuple-element.37.o0, f32[256,256]{1,0:T(8,128)S(1)} %get-tuple-element.39.o2, f32[256,256]{1,0:T(8,128)S(1)} %add.22.o3, f32[256,256]{1,0:T(8,128)S(1)} %collective-permute-done.6.refl_b.c0, f32[256,256]{1,0:T(8,128)S(1)} %collective-permute-done.3.left.c1, ...), custom_call_target="tpu_custom_call" | custom-call | tf_op jit(solution)/shard_map/pallas_call | solution.py:64
  33.5 0.7 %collective-permute-start.16 = (f32[256,256]{1,0:T(8,128)S(1)}, f32[256,256]{1,0:T(8,128)S(1)}, u32[]{:S(2)}, u32[]{:S(2)}) collective-permute-start(f32[256,256]{1,0:T(8,128)S(1)} %shard_map.52), channel_id=1, source_target_pairs={{2,0},{11,9},{18,16},{27,25}} | collective-permute-start | bytes 786440 | tf_op jit(solution)/shard_map/ppermute | solution.py:270
  34.2 0.0 copy-done
  34.2 0.6 %collective-permute-start = (f32[256,256]{1,0:T(8,128)S(1)}, f32[256,256]{1,0:T(8,128)S(1)}, u32[]{:S(2)}, u32[]{:S(2)}) collective-permute-start(f32[256,256]{1,0:T(8,128)S(1)} %bitcast.15), channel_id=1, source_target_pairs={{0,8},{1,9},{2,10},{3,11},{4,12},{5,13},{6,14},{7,15},{8,0},{9,1},... | collective-permute-start | bytes 786440 | tf_op jit(solution)/shard_map/ppermute | solution.py:270
  34.8 0.0 collective-permute-done.11
  34.8 0.7 %collective-permute-start.17 = (f32[256,256]{1,0:T(8,128)S(1)}, f32[256,256]{1,0:T(8,128)S(1)}, u32[]{:S(2)}, u32[]{:S(2)}) collective-permute-start(f32[256,256]{1,0:T(8,128)S(1)} %shard_map.52), channel_id=1, source_target_pairs={{2,4},{11,13},{18,20},{27,29}} | collective-permute-start | bytes 786440 | tf_op jit(solution)/shard_map/ppermute | solution.py:270
  35.5 0.0 collective-permute-done.12
  35.5 0.7 %collective-permute-start.18 = (f32[256,256]{1,0:T(8,128)S(1)}, f32[256,256]{1,0:T(8,128)S(1)}, u32[]{:S(2)}, u32[]{:S(2)}) collective-permute-start(f32[256,256]{1,0:T(8,128)S(1)} %shard_map.52), channel_id=1, source_target_pairs={{2,6},{11,15},{18,22},{27,31}} | collective-permute-start | bytes 786440 | tf_op jit(solution)/shard_map/ppermute | solution.py:270
  36.2 0.0 collective-permute-done.13
  36.2 0.1 select_select_fusion.1
  36.3 1.3 %collective-permute-start.14 = (f32[256,256]{1,0:T(8,128)S(1)}, f32[256,256]{1,0:T(8,128)S(1)}, u32[]{:S(2)}, u32[]{:S(2)}) collective-permute-start(f32[256,256]{1,0:T(8,128)S(1)} %select_select_fusion.1), channel_id=1, source_target_pairs={{0,9},{2,11},{4,13},{6,15},{9,8},{11,10},{13,12},{15,14},{16,25},{... | collective-permute-start | bytes 786440 | tf_op jit(solution)/shard_map/ppermute | solution.py:270
  37.6 0.0 collective-permute-done.16
  37.6 1.8 %collective-permute-start.15 = (f32[256,256]{1,0:T(8,128)S(1)}, f32[256,256]{1,0:T(8,128)S(1)}, u32[]{:S(2)}, u32[]{:S(2)}) collective-permute-start(f32[256,256]{1,0:T(8,128)S(1)} %select_select_fusion.1), channel_id=1, source_target_pairs={{0,8},{1,9},{2,10},{3,11},{4,12},{5,13},{6,14},{7,15},{8,0},{9,1},... | collective-permute-start | bytes 786440 | tf_op jit(solution)/shard_map/ppermute | solution.py:270
  39.3 0.0 collective-permute-done.17
  39.3 0.0 collective-permute-done.18
  39.3 0.1 select_select_fusion
  39.4 6.6 %collective-permute-start.20 = (f32[256,256]{1,0:T(8,128)S(1)}, f32[256,256]{1,0:T(8,128)S(1)}, u32[]{:S(2)}, u32[]{:S(2)}) collective-permute-start(f32[256,256]{1,0:T(8,128)S(1)} %select_select_fusion), channel_id=1, source_target_pairs={{0,1},{1,9},{2,3},{3,11},{4,5},{5,13},{6,7},{7,15},{8,0},{9,8},{10... | collective-permute-start | bytes 786440 | tf_op jit(solution)/shard_map/ppermute | solution.py:270
  46.0 0.0 collective-permute-done
  46.0 0.0 collective-permute-done.14
  46.0 0.0 collective-permute-done.15
  46.0 0.3 fusion
  46.4 0.3 fusion.1
  46.7 1.3 %collective-permute-start.19 = (f32[256,256]{1,0:T(8,128)S(1)}, f32[256,256]{1,0:T(8,128)S(1)}, u32[]{:S(2)}, u32[]{:S(2)}) collective-permute-start(f32[256,256]{1,0:T(8,128)S(1)} %fusion.1), channel_id=1, source_target_pairs={{0,8},{1,9},{2,10},{3,11},{4,12},{5,13},{6,14},{7,15},{8,24},{9,25... | collective-permute-start | bytes 786440 | tf_op jit(solution)/shard_map/ppermute | solution.py:270
  48.0 1.1 %collective-permute-done.20 = f32[256,256]{1,0:T(8,128)S(1)} collective-permute-done((f32[256,256]{1,0:T(8,128)S(1)}, f32[256,256]{1,0:T(8,128)S(1)}, u32[]{:S(2)}, u32[]{:S(2)}) %collective-permute-start.20) | collective-permute-done | bytes 262176 | tf_op jit(solution)/shard_map/ppermute | solution.py:270
  49.1 2.1 %collective-permute-done.19 = f32[256,256]{1,0:T(8,128)S(1)} collective-permute-done((f32[256,256]{1,0:T(8,128)S(1)}, f32[256,256]{1,0:T(8,128)S(1)}, u32[]{:S(2)}, u32[]{:S(2)}) %collective-permute-start.19) | collective-permute-done | bytes 262176 | tf_op jit(solution)/shard_map/ppermute | solution.py:270
  51.3 1.9 %collective-permute-start.21 = (f32[256,256]{1,0:T(8,128)S(1)}, f32[256,256]{1,0:T(8,128)S(1)}, u32[]{:S(2)}, u32[]{:S(2)}) collective-permute-start(f32[256,256]{1,0:T(8,128)S(1)} %select_add_fusion), channel_id=1, source_target_pairs={{0,8},{1,9},{2,10},{3,11},{4,12},{5,13},{6,14},{7,15},{8,0},{9,1},... | collective-permute-start | bytes 786440 | tf_op jit(solution)/shard_map/ppermute | solution.py:270
  53.2 0.3 convolution_add_fusion.odd
  53.6 0.8 %collective-permute-done.21.even = f32[256,256]{1,0:T(8,128)S(1)} collective-permute-done((f32[256,256]{1,0:T(8,128)S(1)}, f32[256,256]{1,0:T(8,128)S(1)}, u32[]{:S(2)}, u32[]{:S(2)}) %collective-permute-start.21) | collective-permute-done | bytes 262176 | tf_op jit(solution)/shard_map/ppermute | solution.py:270
  54.4 1.1 %shard_map.53 = (f32[256,256]{1,0:T(8,128)}, f32[256,256]{1,0:T(8,128)}) custom-call(f32[256,256]{1,0:T(8,128)S(1)} %convolution_add_fusion.odd, f32[256,256]{1,0:T(8,128)S(1)} %collective-permute-done.21.even, f32[256,256]{1,0:T(8,128)S(1)} %broadcast_select_fusion.refl), custom_call_target="tpu_custom_call" | custom-call | tf_op jit(solution)/shard_map/pallas_call | solution.py:231
  (3 shorter events, 0.1 us)
Async XLA Ops:
  1.6 7.2 %collective-permute-start.1 = (f32[256,256]{1,0:T(8,128)S(1)}, f32[256,256]{1,0:T(8,128)S(1)}, u32[]{:S(2)}, u32[]{:S(2)}) collective-permute-start(f32[256,256]{1,0:T(8,128)S(1)} %shard_map.41.refl), channel_id=1, source_target_pairs={{0,8},{1,0},{2,10},{3,2},{4,12},{5,4},{6,7},{7,6},{8,9},{9,1},{10,... | collective-permute-start | bytes 786440 | tf_op jit(solution)/shard_map/ppermute | solution.py:270
  4.0 10.4 %collective-permute-start.2 = (f32[256,256]{1,0:T(8,128)S(1)}, f32[256,256]{1,0:T(8,128)S(1)}, u32[]{:S(2)}, u32[]{:S(2)}) collective-permute-start(f32[256,256]{1,0:T(8,128)S(1)} %get-tuple-element.28.trans), channel_id=1, source_target_pairs={{0,8},{1,0},{2,10},{3,2},{4,12},{5,4},{6,7},{7,6},{8,9},{9,1},{10,... | collective-permute-start | bytes 786440 | tf_op jit(solution)/shard_map/ppermute | solution.py:270
  4.3 10.6 %collective-permute-start.4 = (f32[256,256]{1,0:T(8,128)S(1)}, f32[256,256]{1,0:T(8,128)S(1)}, u32[]{:S(2)}, u32[]{:S(2)}) collective-permute-start(f32[256,256]{1,0:T(8,128)S(1)} %get-tuple-element.29.up), channel_id=1, source_target_pairs={{0,8},{1,0},{2,10},{3,2},{4,12},{5,4},{6,14},{7,15},{8,9},{9,1},{1... | collective-permute-start | bytes 786440 | tf_op jit(solution)/shard_map/ppermute | solution.py:270
  5.6 9.9 %collective-permute-start.5 = (f32[256,256]{1,0:T(8,128)S(1)}, f32[256,256]{1,0:T(8,128)S(1)}, u32[]{:S(2)}, u32[]{:S(2)}) collective-permute-start(f32[256,256]{1,0:T(8,128)S(1)} %get-tuple-element.30.behind), channel_id=1, source_target_pairs={{0,8},{1,0},{2,10},{3,2},{4,12},{5,4},{6,14},{7,15},{8,9},{9,1},{1... | collective-permute-start | bytes 786440 | tf_op jit(solution)/shard_map/ppermute | solution.py:270
  10.5 6.6 %collective-permute-start.6 = (f32[256,256]{1,0:T(8,128)S(1)}, f32[256,256]{1,0:T(8,128)S(1)}, u32[]{:S(2)}, u32[]{:S(2)}) collective-permute-start(f32[256,256]{1,0:T(8,128)S(1)} %get-tuple-element.37.o0), channel_id=1, source_target_pairs={{0,2},{1,9},{2,10},{3,1},{4,12},{5,6},{6,4},{7,15},{8,0},{9,11},{1... | collective-permute-start | bytes 786440 | tf_op jit(solution)/shard_map/ppermute | solution.py:270
  14.9 7.4 %collective-permute-start.3 = (f32[256,256]{1,0:T(8,128)S(1)}, f32[256,256]{1,0:T(8,128)S(1)}, u32[]{:S(2)}, u32[]{:S(2)}) collective-permute-start(f32[256,256]{1,0:T(8,128)S(1)} %get-tuple-element.36.o1), channel_id=1, source_target_pairs={{0,2},{1,9},{2,10},{3,1},{4,12},{5,6},{6,4},{7,15},{8,0},{9,11},{1... | collective-permute-start | bytes 786440 | tf_op jit(solution)/shard_map/ppermute | solution.py:270
  15.5 8.6 %collective-permute-start.8 = (f32[256,256]{1,0:T(8,128)S(1)}, f32[256,256]{1,0:T(8,128)S(1)}, u32[]{:S(2)}, u32[]{:S(2)}) collective-permute-start(f32[256,256]{1,0:T(8,128)S(1)} %add.22.o3), channel_id=1, source_target_pairs={{0,2},{1,9},{2,10},{3,1},{4,12},{5,13},{6,14},{7,15},{8,0},{9,11},... | collective-permute-start | bytes 786440 | tf_op jit(solution)/shard_map/ppermute | solution.py:270
  17.1 8.8 %collective-permute-start.9 = (f32[256,256]{1,0:T(8,128)S(1)}, f32[256,256]{1,0:T(8,128)S(1)}, u32[]{:S(2)}, u32[]{:S(2)}) collective-permute-start(f32[256,256]{1,0:T(8,128)S(1)} %get-tuple-element.39.o2), channel_id=1, source_target_pairs={{0,2},{1,9},{2,10},{3,1},{4,12},{5,13},{6,14},{7,15},{8,0},{9,11},... | collective-permute-start | bytes 786440 | tf_op jit(solution)/shard_map/ppermute | solution.py:270
  18.8 7.1 %collective-permute-start.10 = (f32[256,256]{1,0:T(8,128)S(1)}, f32[256,256]{1,0:T(8,128)S(1)}, u32[]{:S(2)}, u32[]{:S(2)}) collective-permute-start(f32[256,256]{1,0:T(8,128)S(1)} %get-tuple-element.45), channel_id=1, source_target_pairs={{0,8},{1,9},{2,10},{3,5},{4,2},{5,13},{6,14},{7,15},{8,0},{9,1},{1... | collective-permute-start | bytes 786440 | tf_op jit(solution)/shard_map/ppermute | solution.py:270
  22.5 5.9 %collective-permute-start.7 = (f32[256,256]{1,0:T(8,128)S(1)}, f32[256,256]{1,0:T(8,128)S(1)}, u32[]{:S(2)}, u32[]{:S(2)}) collective-permute-start(f32[256,256]{1,0:T(8,128)S(1)} %shard_map.48), channel_id=1, source_target_pairs={{0,8},{1,9},{2,10},{3,5},{4,2},{5,13},{6,14},{7,15},{8,0},{9,1},{1... | collective-permute-start | bytes 786440 | tf_op jit(solution)/shard_map/ppermute | solution.py:270
  28.7 6.1 %collective-permute-start.11 = (f32[256,256]{1,0:T(8,128)S(1)}, f32[256,256]{1,0:T(8,128)S(1)}, u32[]{:S(2)}, u32[]{:S(2)}) collective-permute-start(f32[256,256]{1,0:T(8,128)S(1)} %shard_map.51), channel_id=1, source_target_pairs={{0,8},{1,3},{2,0},{3,11},{4,12},{5,13},{6,14},{7,15},{8,10},{9,1},... | collective-permute-start | bytes 786440 | tf_op jit(solution)/shard_map/ppermute | solution.py:270
  28.8 6.7 %collective-permute-start.12 = (f32[256,256]{1,0:T(8,128)S(1)}, f32[256,256]{1,0:T(8,128)S(1)}, u32[]{:S(2)}, u32[]{:S(2)}) collective-permute-start(f32[256,256]{1,0:T(8,128)S(1)} %shard_map.51), channel_id=1, source_target_pairs={{0,8},{1,9},{2,6},{3,11},{4,12},{5,13},{6,14},{7,3},{8,0},{9,1},{1... | collective-permute-start | bytes 786440 | tf_op jit(solution)/shard_map/ppermute | solution.py:270
  31.5 4.7 %collective-permute-start.13 = (f32[256,256]{1,0:T(8,128)S(1)}, f32[256,256]{1,0:T(8,128)S(1)}, u32[]{:S(2)}, u32[]{:S(2)}) collective-permute-start(f32[256,256]{1,0:T(8,128)S(1)} %shard_map.51), channel_id=1, source_target_pairs={{0,8},{1,9},{2,4},{3,11},{4,12},{5,3},{6,14},{7,15},{8,0},{9,1},{1... | collective-permute-start | bytes 786440 | tf_op jit(solution)/shard_map/ppermute | solution.py:270
  31.5 2.7 %copy-start = (f32[1,256,256]{2,1,0:T(8,128)S(1)}, f32[1,256,256]{2,1,0:T(8,128)}, u32[]{:S(2)}) copy-start(f32[1,256,256]{2,1,0:T(8,128)} %param.3) | copy-start | bytes 786436
  33.5 4.0 %collective-permute-start.16 = (f32[256,256]{1,0:T(8,128)S(1)}, f32[256,256]{1,0:T(8,128)S(1)}, u32[]{:S(2)}, u32[]{:S(2)}) collective-permute-start(f32[256,256]{1,0:T(8,128)S(1)} %shard_map.52), channel_id=1, source_target_pairs={{2,0},{11,9},{18,16},{27,25}} | collective-permute-start | bytes 786440 | tf_op jit(solution)/shard_map/ppermute | solution.py:270
  34.2 11.8 %collective-permute-start = (f32[256,256]{1,0:T(8,128)S(1)}, f32[256,256]{1,0:T(8,128)S(1)}, u32[]{:S(2)}, u32[]{:S(2)}) collective-permute-start(f32[256,256]{1,0:T(8,128)S(1)} %bitcast.15), channel_id=1, source_target_pairs={{0,8},{1,9},{2,10},{3,11},{4,12},{5,13},{6,14},{7,15},{8,0},{9,1},... | collective-permute-start | bytes 786440 | tf_op jit(solution)/shard_map/ppermute | solution.py:270
  34.8 4.5 %collective-permute-start.17 = (f32[256,256]{1,0:T(8,128)S(1)}, f32[256,256]{1,0:T(8,128)S(1)}, u32[]{:S(2)}, u32[]{:S(2)}) collective-permute-start(f32[256,256]{1,0:T(8,128)S(1)} %shard_map.52), channel_id=1, source_target_pairs={{2,4},{11,13},{18,20},{27,29}} | collective-permute-start | bytes 786440 | tf_op jit(solution)/shard_map/ppermute | solution.py:270
  35.5 3.9 %collective-permute-start.18 = (f32[256,256]{1,0:T(8,128)S(1)}, f32[256,256]{1,0:T(8,128)S(1)}, u32[]{:S(2)}, u32[]{:S(2)}) collective-permute-start(f32[256,256]{1,0:T(8,128)S(1)} %shard_map.52), channel_id=1, source_target_pairs={{2,6},{11,15},{18,22},{27,31}} | collective-permute-start | bytes 786440 | tf_op jit(solution)/shard_map/ppermute | solution.py:270
  36.3 9.8 %collective-permute-start.14 = (f32[256,256]{1,0:T(8,128)S(1)}, f32[256,256]{1,0:T(8,128)S(1)}, u32[]{:S(2)}, u32[]{:S(2)}) collective-permute-start(f32[256,256]{1,0:T(8,128)S(1)} %select_select_fusion.1), channel_id=1, source_target_pairs={{0,9},{2,11},{4,13},{6,15},{9,8},{11,10},{13,12},{15,14},{16,25},{... | collective-permute-start | bytes 786440 | tf_op jit(solution)/shard_map/ppermute | solution.py:270
  37.6 8.5 %collective-permute-start.15 = (f32[256,256]{1,0:T(8,128)S(1)}, f32[256,256]{1,0:T(8,128)S(1)}, u32[]{:S(2)}, u32[]{:S(2)}) collective-permute-start(f32[256,256]{1,0:T(8,128)S(1)} %select_select_fusion.1), channel_id=1, source_target_pairs={{0,8},{1,9},{2,10},{3,11},{4,12},{5,13},{6,14},{7,15},{8,0},{9,1},... | collective-permute-start | bytes 786440 | tf_op jit(solution)/shard_map/ppermute | solution.py:270
  39.4 9.7 %collective-permute-start.20 = (f32[256,256]{1,0:T(8,128)S(1)}, f32[256,256]{1,0:T(8,128)S(1)}, u32[]{:S(2)}, u32[]{:S(2)}) collective-permute-start(f32[256,256]{1,0:T(8,128)S(1)} %select_select_fusion), channel_id=1, source_target_pairs={{0,1},{1,9},{2,3},{3,11},{4,5},{5,13},{6,7},{7,15},{8,0},{9,8},{10... | collective-permute-start | bytes 786440 | tf_op jit(solution)/shard_map/ppermute | solution.py:270
  46.7 4.6 %collective-permute-start.19 = (f32[256,256]{1,0:T(8,128)S(1)}, f32[256,256]{1,0:T(8,128)S(1)}, u32[]{:S(2)}, u32[]{:S(2)}) collective-permute-start(f32[256,256]{1,0:T(8,128)S(1)} %fusion.1), channel_id=1, source_target_pairs={{0,8},{1,9},{2,10},{3,11},{4,12},{5,13},{6,14},{7,15},{8,24},{9,25... | collective-permute-start | bytes 786440 | tf_op jit(solution)/shard_map/ppermute | solution.py:270
  51.3 3.1 %collective-permute-start.21 = (f32[256,256]{1,0:T(8,128)S(1)}, f32[256,256]{1,0:T(8,128)S(1)}, u32[]{:S(2)}, u32[]{:S(2)}) collective-permute-start(f32[256,256]{1,0:T(8,128)S(1)} %select_add_fusion), channel_id=1, source_target_pairs={{0,8},{1,9},{2,10},{3,11},{4,12},{5,13},{6,14},{7,15},{8,0},{9,1},... | collective-permute-start | bytes 786440 | tf_op jit(solution)/shard_map/ppermute | solution.py:270

commit v7 on v6

--- a/solution.py
+++ b/solution.py
@@ -202,6 +202,26 @@
     return lax.dot_general(
         rows, matrix, (((1,), (1,)), ((), ())), precision=lax.Precision.HIGH, preferred_element_type=jnp.float32
     )
+
+
+def rows_times(rows, matrix):
+    rows_high, rows_low = split(rows)
+    high, low = split(matrix)
+    dot = functools.partial(
+        lax.dot_general, dimension_numbers=(((1,), (1,)), ((), ())), preferred_element_type=jnp.float32
+    )
+    return dot(rows_high, high) + (dot(rows_high, low) + dot(rows_low, high))
+
+
+def sweep_odd(even, injected, trans, crossed, swapped, field):
+    lower_side = lax.axis_index("slab") % 2 == 1
+    field[...] = injected[...] + rows_times(even[...], jnp.where(lower_side, crossed[...], swapped[...]))
+
+
+def sweep_on(even, injected, trans, crossed, swapped, leaving):
+    lower_side = lax.axis_index("slab") % 2 == 1
+    field = injected[...] + rows_times(even[...], jnp.where(lower_side, crossed[...], swapped[...]))
+    leaving[...] = rows_times(field, jnp.where(lower_side, trans[...], crossed[...]))
 
 
 def last_step(odd, even, refl, field_out, bounced_out, field, bounced, sems):
@@ -381,20 +401,21 @@
             across[line(g, k)] = (g | 1, 2 * k + 1 - g % 2)
     swap = {(g, s): (g ^ 1, s) for g in range(groups) for s in range(count)}
     crossed = send(trans, across, False)
-    trans_even = jnp.where(side == 1, crossed, send(trans, swap))
-    trans_odd = jnp.where(side == 1, trans, crossed)
+    swapped = send(trans, swap)
     even = send(injected, swap)
     opposite = {line(g, k): (g, line(g, k)[1] ^ 1) for g in range(groups) for k in range(pairs)}
     spread_refl = jnp.where(side == parity, refl, send(refl, opposite))
     handed = jnp.zeros_like(injected)
     for j in range(0, groups, 2):
         field_even = even + handed
-        field_odd = injected + times_transpose(field_even, trans_even)
+        known = [field_even, injected, trans, crossed, swapped]
         if j + 2 < groups:
-            leaving, _ = lax.optimization_barrier((times_transpose(field_odd, trans_odd), refl))
+            (leaving,) = call(sweep_on, known, 1)
+            leaving, _ = lax.optimization_barrier((leaving, refl))
             arriving = send(leaving, {(j + 1, s): (j + 3, s) for s in range(count)})
             arriving, _ = lax.optimization_barrier((arriving, spread_refl))
             handed = jnp.where(group // 2 == j // 2 + 1, arriving, handed)
+    (field_odd,) = call(sweep_odd, known, 1)
     field, bounced = finish(field_odd, send(field_even, swap), spread_refl)
     return (field[None], bounced[None])
 

time: 56 us -> 55.9 us (level)
  the two profiles are of different devices: /device:TPU:25 before, /device:TPU:9 now
where the time goes in v7:
time: 55.9 us; the launch traced here: 55.7 us
  starting transfers between devices  26 us (47%)
  Pallas kernels  15.9 us (28%)
  waiting for transfers between devices  12.7 us (23%)
  between operations  0.9 us (2%)
    ppermute x22, starting transfers between devices, send(): return lax.ppermute(block, AXES, route)  26 us
    ppermute x22, waiting for transfers between devices, send(): return lax.ppermute(block, AXES, route)  12.7 us
    pallas_call x12, Pallas kernels, call(): pl.pallas_call(body, out_shape=[square] * outs, in_specs=[vmem] * len(blo...  12.6 us
    pallas_call x2, Pallas kernels, picked(): pl.pallas_call(functools.partial(pick, marks, which), out_shape=[block] *...  2.11 us
  transfers between devices with their start and end apart: 22, of which 9 were waited for; matrix products, arithmetic and copies ran while one was open for 0% of the time, Pallas kernels for 24%

profile of v7, /device:TPU:9, one launch (start us, length us, event | category | flops | bytes accessed | tf_op | source)
XLA Modules:
  0.0 55.7 jit_solution(10129072117812174327)
XLA Ops:
  0.6 1.0 %shard_map.41.refl = f32[256,256]{1,0:T(8,128)S(1)} custom-call(f32[4,256,256]{2,1,0:T(8,128)} %bitcast.7), custom_call_target="tpu_custom_call" | custom-call | tf_op jit(solution)/shard_map/pallas_call | solution.py:107
  1.6 1.3 %collective-permute-start.1 = (f32[256,256]{1,0:T(8,128)S(1)}, f32[256,256]{1,0:T(8,128)S(1)}, u32[]{:S(2)}, u32[]{:S(2)}) collective-permute-start(f32[256,256]{1,0:T(8,128)S(1)} %shard_map.41.refl), channel_id=1, source_target_pairs={{0,8},{1,0},{2,10},{3,2},{4,12},{5,4},{6,7},{7,6},{8,9},{9,1},{10,... | collective-permute-start | bytes 786440 | tf_op jit(solution)/shard_map/ppermute | solution.py:290
  2.9 1.1 %shard_map.42 = (f32[256,256]{1,0:T(8,128)S(1)}, f32[256,256]{1,0:T(8,128)S(1)}, f32[256,256]{1,0:T(8,128)S(1)}) custom-call(f32[4,256,256]{2,1,0:T(8,128)} %bitcast.8), custom_call_target="tpu_custom_call" | custom-call | tf_op jit(solution)/shard_map/pallas_call | solution.py:107
  4.0 0.7 %collective-permute-start.2 = (f32[256,256]{1,0:T(8,128)S(1)}, f32[256,256]{1,0:T(8,128)S(1)}, u32[]{:S(2)}, u32[]{:S(2)}) collective-permute-start(f32[256,256]{1,0:T(8,128)S(1)} %get-tuple-element.28.trans), channel_id=1, source_target_pairs={{0,8},{1,0},{2,10},{3,2},{4,12},{5,4},{6,7},{7,6},{8,9},{9,1},{10,... | collective-permute-start | bytes 786440 | tf_op jit(solution)/shard_map/ppermute | solution.py:290
  4.8 0.5 collective-permute-start.4
  5.3 0.1 collective-permute-start.5
  5.4 0.8 %collective-permute-done.1.c0 = f32[256,256]{1,0:T(8,128)S(1)} collective-permute-done((f32[256,256]{1,0:T(8,128)S(1)}, f32[256,256]{1,0:T(8,128)S(1)}, u32[]{:S(2)}, u32[]{:S(2)}) %collective-permute-start.1) | collective-permute-done | bytes 262176 | tf_op jit(solution)/shard_map/ppermute | solution.py:290
  6.2 1.7 %shard_map.43 = (f32[256,256]{1,0:T(8,128)S(1)}, f32[256,256]{1,0:T(8,128)S(1)}, f32[256,256]{1,0:T(8,128)S(1)}, f32[256,256]{1,0:T(8,128)S(1)}) custom-call(f32[256,256]{1,0:T(8,128)S(1)} %shard_map.41.refl, f32[256,256]{1,0:T(8,128)S(1)} %get-tuple-element.28.trans, f32[256,256]{1,0:T(8,128)S(1)} %get-tuple-element.29.up, ...), custom_call_target="tpu_custom_call" | custom-call | tf_op jit(solution)/shard_map/pallas_call | solution.py:64
  7.9 0.2 collective-permute-start.6
  8.1 0.7 %shard_map.44 = (f32[256,256]{1,0:T(8,128)S(1)}, f32[256,256]{1,0:T(8,128)S(1)}) custom-call(f32[256,256]{1,0:T(8,128)S(1)} %get-tuple-element.28.trans, f32[256,256]{1,0:T(8,128)S(1)} %get-tuple-element.29.up, f32[256,256]{1,0:T(8,128)S(1)} %get-tuple-element.30.behind, f32[256,256]{1,0:T(8,128)S(1)} %get-tuple-element.32.solver, ...), custom_call_target="tpu_custom_call" | custom-call | tf_op jit(solution)/shard_map/pallas_call | solution.py:64
  8.8 0.2 collective-permute-done.2.c1
  9.0 0.4 shard_map.45
  9.4 1.8 %collective-permute-start.3 = (f32[256,256]{1,0:T(8,128)S(1)}, f32[256,256]{1,0:T(8,128)S(1)}, u32[]{:S(2)}, u32[]{:S(2)}) collective-permute-start(f32[256,256]{1,0:T(8,128)S(1)} %get-tuple-element.36.o1), channel_id=1, source_target_pairs={{0,2},{1,9},{2,10},{3,1},{4,12},{5,6},{6,4},{7,15},{8,0},{9,11},{1... | collective-permute-start | bytes 786440 | tf_op jit(solution)/shard_map/ppermute | solution.py:290
  11.3 0.5 collective-permute-done.4.c2
  11.8 0.4 shard_map.46
  12.3 2.4 %collective-permute-done.5 = f32[256,256]{1,0:T(8,128)S(1)} collective-permute-done((f32[256,256]{1,0:T(8,128)S(1)}, f32[256,256]{1,0:T(8,128)S(1)}, u32[]{:S(2)}, u32[]{:S(2)}) %collective-permute-start.5) | collective-permute-done | bytes 262176 | tf_op jit(solution)/shard_map/ppermute | solution.py:290
  14.7 0.3 collective-permute-start.8
  14.9 2.0 %collective-permute-start.9 = (f32[256,256]{1,0:T(8,128)S(1)}, f32[256,256]{1,0:T(8,128)S(1)}, u32[]{:S(2)}, u32[]{:S(2)}) collective-permute-start(f32[256,256]{1,0:T(8,128)S(1)} %get-tuple-element.39.o2), channel_id=1, source_target_pairs={{0,2},{1,9},{2,10},{3,1},{4,12},{5,13},{6,14},{7,15},{8,0},{9,11},... | collective-permute-start | bytes 786440 | tf_op jit(solution)/shard_map/ppermute | solution.py:290
  16.9 0.0 collective-permute-done.6.refl_b.c0
  16.9 1.7 %shard_map.47 = (f32[256,256]{1,0:T(8,128)S(1)}, f32[256,256]{1,0:T(8,128)S(1)}) custom-call(f32[256,256]{1,0:T(8,128)S(1)} %get-tuple-element.37.o0, f32[256,256]{1,0:T(8,128)S(1)} %get-tuple-element.36.o1, f32[256,256]{1,0:T(8,128)S(1)} %get-tuple-element.39.o2, f32[256,256]{1,0:T(8,128)S(1)} %add.15.o3, f32[256,256]{1,0:T(8,128)S(1)} %collective-permute-done.6.refl_b.c0), custom_call_target="tpu_custom_call" | custom-call | tf_op jit(solution)/shard_map/pallas_call | solution.py:64
  18.6 3.2 %collective-permute-start.10 = (f32[256,256]{1,0:T(8,128)S(1)}, f32[256,256]{1,0:T(8,128)S(1)}, u32[]{:S(2)}, u32[]{:S(2)}) collective-permute-start(f32[256,256]{1,0:T(8,128)S(1)} %get-tuple-element.45), channel_id=1, source_target_pairs={{0,8},{1,9},{2,10},{3,5},{4,2},{5,13},{6,14},{7,15},{8,0},{9,1},{1... | collective-permute-start | bytes 786440 | tf_op jit(solution)/shard_map/ppermute | solution.py:290
  21.8 0.0 collective-permute-done.3.left.c1
  21.8 0.3 shard_map.48
  22.1 1.7 %collective-permute-start.7 = (f32[256,256]{1,0:T(8,128)S(1)}, f32[256,256]{1,0:T(8,128)S(1)}, u32[]{:S(2)}, u32[]{:S(2)}) collective-permute-start(f32[256,256]{1,0:T(8,128)S(1)} %shard_map.48), channel_id=1, source_target_pairs={{0,8},{1,9},{2,10},{3,5},{4,2},{5,13},{6,14},{7,15},{8,0},{9,1},{1... | collective-permute-start | bytes 786440 | tf_op jit(solution)/shard_map/ppermute | solution.py:290
  23.8 0.0 collective-permute-done.8.c3
  23.8 1.8 %shard_map.49 = (f32[256,256]{1,0:T(8,128)S(1)}, f32[256,256]{1,0:T(8,128)S(1)}, f32[256,256]{1,0:T(8,128)S(1)}) custom-call(f32[256,256]{1,0:T(8,128)S(1)} %get-tuple-element.37.o0, f32[256,256]{1,0:T(8,128)S(1)} %get-tuple-element.36.o1, f32[256,256]{1,0:T(8,128)S(1)} %get-tuple-element.39.o2, f32[256,256]{1,0:T(8,128)S(1)} %add.15.o3, ...), custom_call_target="tpu_custom_call" | custom-call | tf_op jit(solution)/shard_map/pallas_call | solution.py:64
  25.6 0.0 collective-permute-done.9.c2
  25.6 0.0 collective-permute-done.10.refl_b.low_refl
  25.6 2.5 %shard_map.50.right.down = f32[256,256]{1,0:T(8,128)S(1)} custom-call(f32[256,256]{1,0:T(8,128)S(1)} %get-tuple-element.43.back_a, f32[256,256]{1,0:T(8,128)S(1)} %get-tuple-element.44.trans_a, f32[256,256]{1,0:T(8,128)S(1)} %collective-permute-done.10.refl_b.low_refl), custom_call_target="tpu_custom_call" | custom-call | tf_op jit(solution)/shard_map/pallas_call | solution.py:64
  28.1 0.0 collective-permute-done.7.left
  28.1 0.3 shard_map.51
  28.4 3.0 %collective-permute-start.11 = (f32[256,256]{1,0:T(8,128)S(1)}, f32[256,256]{1,0:T(8,128)S(1)}, u32[]{:S(2)}, u32[]{:S(2)}) collective-permute-start(f32[256,256]{1,0:T(8,128)S(1)} %shard_map.51), channel_id=1, source_target_pairs={{0,8},{1,3},{2,0},{3,11},{4,12},{5,13},{6,14},{7,15},{8,10},{9,1},... | collective-permute-start | bytes 786440 | tf_op jit(solution)/shard_map/ppermute | solution.py:290
  31.4 0.1 collective-permute-start.12
  31.5 0.4 collective-permute-start.13
  31.9 0.0 copy-start
  31.9 2.0 %shard_map.52 = f32[256,256]{1,0:T(8,128)S(1)} custom-call(f32[256,256]{1,0:T(8,128)S(1)} %get-tuple-element.37.o0, f32[256,256]{1,0:T(8,128)S(1)} %get-tuple-element.39.o2, f32[256,256]{1,0:T(8,128)S(1)} %add.15.o3, f32[256,256]{1,0:T(8,128)S(1)} %collective-permute-done.6.refl_b.c0, f32[256,256]{1,0:T(8,128)S(1)} %collective-permute-done.3.left.c1, ...), custom_call_target="tpu_custom_call" | custom-call | tf_op jit(solution)/shard_map/pallas_call | solution.py:64
  33.9 0.7 %collective-permute-start.16 = (f32[256,256]{1,0:T(8,128)S(1)}, f32[256,256]{1,0:T(8,128)S(1)}, u32[]{:S(2)}, u32[]{:S(2)}) collective-permute-start(f32[256,256]{1,0:T(8,128)S(1)} %shard_map.52), channel_id=1, source_target_pairs={{2,0},{11,9},{18,16},{27,25}} | collective-permute-start | bytes 786440 | tf_op jit(solution)/shard_map/ppermute | solution.py:290
  34.6 0.7 %collective-permute-start.17 = (f32[256,256]{1,0:T(8,128)S(1)}, f32[256,256]{1,0:T(8,128)S(1)}, u32[]{:S(2)}, u32[]{:S(2)}) collective-permute-start(f32[256,256]{1,0:T(8,128)S(1)} %shard_map.52), channel_id=1, source_target_pairs={{2,4},{11,13},{18,20},{27,29}} | collective-permute-start | bytes 786440 | tf_op jit(solution)/shard_map/ppermute | solution.py:290
  35.3 0.0 collective-permute-done.11
  35.3 0.7 %collective-permute-start.18 = (f32[256,256]{1,0:T(8,128)S(1)}, f32[256,256]{1,0:T(8,128)S(1)}, u32[]{:S(2)}, u32[]{:S(2)}) collective-permute-start(f32[256,256]{1,0:T(8,128)S(1)} %shard_map.52), channel_id=1, source_target_pairs={{2,6},{11,15},{18,22},{27,31}} | collective-permute-start | bytes 786440 | tf_op jit(solution)/shard_map/ppermute | solution.py:290
  36.0 1.7 %collective-permute-done.12 = f32[256,256]{1,0:T(8,128)S(1)} collective-permute-done((f32[256,256]{1,0:T(8,128)S(1)}, f32[256,256]{1,0:T(8,128)S(1)}, u32[]{:S(2)}, u32[]{:S(2)}) %collective-permute-start.12) | collective-permute-done | bytes 262176 | tf_op jit(solution)/shard_map/ppermute | solution.py:290
  37.7 0.0 copy-done
  37.7 2.4 %collective-permute-start = (f32[256,256]{1,0:T(8,128)S(1)}, f32[256,256]{1,0:T(8,128)S(1)}, u32[]{:S(2)}, u32[]{:S(2)}) collective-permute-start(f32[256,256]{1,0:T(8,128)S(1)} %bitcast.4), channel_id=1, source_target_pairs={{0,8},{1,9},{2,10},{3,11},{4,12},{5,13},{6,14},{7,15},{8,0},{9,1},... | collective-permute-start | bytes 786440 | tf_op jit(solution)/shard_map/ppermute | solution.py:290
  40.0 0.0 collective-permute-done.13
  40.0 0.1 select_select_fusion.1.trans
  40.1 1.3 %collective-permute-start.14 = (f32[256,256]{1,0:T(8,128)S(1)}, f32[256,256]{1,0:T(8,128)S(1)}, u32[]{:S(2)}, u32[]{:S(2)}) collective-permute-start(f32[256,256]{1,0:T(8,128)S(1)} %select_select_fusion.1.trans), channel_id=1, source_target_pairs={{0,9},{2,11},{4,13},{6,15},{9,8},{11,10},{13,12},{15,14},{16,25},{... | collective-permute-start | bytes 786440 | tf_op jit(solution)/shard_map/ppermute | solution.py:290
  41.4 0.0 collective-permute-done.16
  41.4 1.1 %collective-permute-start.15 = (f32[256,256]{1,0:T(8,128)S(1)}, f32[256,256]{1,0:T(8,128)S(1)}, u32[]{:S(2)}, u32[]{:S(2)}) collective-permute-start(f32[256,256]{1,0:T(8,128)S(1)} %select_select_fusion.1.trans), channel_id=1, source_target_pairs={{0,8},{1,9},{2,10},{3,11},{4,12},{5,13},{6,14},{7,15},{8,0},{9,1},... | collective-permute-start | bytes 786440 | tf_op jit(solution)/shard_map/ppermute | solution.py:290
  42.5 0.0 collective-permute-done.17
  42.5 0.0 collective-permute-done.18
  42.5 0.1 select_select_fusion
  42.5 1.7 %collective-permute-start.20 = (f32[256,256]{1,0:T(8,128)S(1)}, f32[256,256]{1,0:T(8,128)S(1)}, u32[]{:S(2)}, u32[]{:S(2)}) collective-permute-start(f32[256,256]{1,0:T(8,128)S(1)} %select_select_fusion), channel_id=1, source_target_pairs={{0,1},{1,9},{2,3},{3,11},{4,5},{5,13},{6,7},{7,15},{8,0},{9,8},{10... | collective-permute-start | bytes 786440 | tf_op jit(solution)/shard_map/ppermute | solution.py:290
  44.3 0.0 collective-permute-done.even
  44.3 2.9 %collective-permute-done.14.crossed = f32[256,256]{1,0:T(8,128)S(1)} collective-permute-done((f32[256,256]{1,0:T(8,128)S(1)}, f32[256,256]{1,0:T(8,128)S(1)}, u32[]{:S(2)}, u32[]{:S(2)}) %collective-permute-start.14) | collective-permute-done | bytes 262176 | tf_op jit(solution)/shard_map/ppermute | solution.py:290
  47.2 0.0 collective-permute-done.15.swapped
  47.2 0.6 %shard_map.53 = f32[256,256]{1,0:T(8,128)S(1)} custom-call(f32[256,256]{1,0:T(8,128)S(1)} %collective-permute-done.even, f32[256,256]{1,0:T(8,128)S(1)} %bitcast.5, f32[256,256]{1,0:T(8,128)S(1)} %select_select_fusion.1.trans, f32[256,256]{1,0:T(8,128)S(1)} %collective-permute-done.14.crossed, f32[256,256]{1,0:T(8,128)S(1)} %collective-permute-done.15.swapped), custom_call_target="tpu_custom_call" | custom-call | tf_op jit(solution)/shard_map/pallas_call | solution.py:64
  47.9 0.0 collective-permute-start.19
  47.9 2.4 %collective-permute-done.20 = f32[256,256]{1,0:T(8,128)S(1)} collective-permute-done((f32[256,256]{1,0:T(8,128)S(1)}, f32[256,256]{1,0:T(8,128)S(1)}, u32[]{:S(2)}, u32[]{:S(2)}) %collective-permute-start.20) | collective-permute-done | bytes 262176 | tf_op jit(solution)/shard_map/ppermute | solution.py:290
  50.4 0.9 %collective-permute-done.19 = f32[256,256]{1,0:T(8,128)S(1)} collective-permute-done((f32[256,256]{1,0:T(8,128)S(1)}, f32[256,256]{1,0:T(8,128)S(1)}, u32[]{:S(2)}, u32[]{:S(2)}) %collective-permute-start.19) | collective-permute-done | bytes 262176 | tf_op jit(solution)/shard_map/ppermute | solution.py:290
  51.3 2.1 %collective-permute-start.21 = (f32[256,256]{1,0:T(8,128)S(1)}, f32[256,256]{1,0:T(8,128)S(1)}, u32[]{:S(2)}, u32[]{:S(2)}) collective-permute-start(f32[256,256]{1,0:T(8,128)S(1)} %select_add_fusion.even), channel_id=1, source_target_pairs={{0,8},{1,9},{2,10},{3,11},{4,12},{5,13},{6,14},{7,15},{8,0},{9,1},... | collective-permute-start | bytes 786440 | tf_op jit(solution)/shard_map/ppermute | solution.py:290
  53.4 0.3 shard_map.54.odd
  53.7 0.8 %collective-permute-done.21.even = f32[256,256]{1,0:T(8,128)S(1)} collective-permute-done((f32[256,256]{1,0:T(8,128)S(1)}, f32[256,256]{1,0:T(8,128)S(1)}, u32[]{:S(2)}, u32[]{:S(2)}) %collective-permute-start.21) | collective-permute-done | bytes 262176 | tf_op jit(solution)/shard_map/ppermute | solution.py:290
  54.6 1.1 %shard_map.55 = (f32[256,256]{1,0:T(8,128)}, f32[256,256]{1,0:T(8,128)}) custom-call(f32[256,256]{1,0:T(8,128)S(1)} %shard_map.54.odd, f32[256,256]{1,0:T(8,128)S(1)} %collective-permute-done.21.even, f32[256,256]{1,0:T(8,128)S(1)} %broadcast_select_fusion.refl), custom_call_target="tpu_custom_call" | custom-call | tf_op jit(solution)/shard_map/pallas_call | solution.py:251
  (3 shorter events, 0.1 us)
Async XLA Ops:
  1.6 4.6 %collective-permute-start.1 = (f32[256,256]{1,0:T(8,128)S(1)}, f32[256,256]{1,0:T(8,128)S(1)}, u32[]{:S(2)}, u32[]{:S(2)}) collective-permute-start(f32[256,256]{1,0:T(8,128)S(1)} %shard_map.41.refl), channel_id=1, source_target_pairs={{0,8},{1,0},{2,10},{3,2},{4,12},{5,4},{6,7},{7,6},{8,9},{9,1},{10,... | collective-permute-start | bytes 786440 | tf_op jit(solution)/shard_map/ppermute | solution.py:290
  4.0 5.0 %collective-permute-start.2 = (f32[256,256]{1,0:T(8,128)S(1)}, f32[256,256]{1,0:T(8,128)S(1)}, u32[]{:S(2)}, u32[]{:S(2)}) collective-permute-start(f32[256,256]{1,0:T(8,128)S(1)} %get-tuple-element.28.trans), channel_id=1, source_target_pairs={{0,8},{1,0},{2,10},{3,2},{4,12},{5,4},{6,7},{7,6},{8,9},{9,1},{10,... | collective-permute-start | bytes 786440 | tf_op jit(solution)/shard_map/ppermute | solution.py:290
  4.8 7.1 %collective-permute-start.4 = (f32[256,256]{1,0:T(8,128)S(1)}, f32[256,256]{1,0:T(8,128)S(1)}, u32[]{:S(2)}, u32[]{:S(2)}) collective-permute-start(f32[256,256]{1,0:T(8,128)S(1)} %get-tuple-element.29.up), channel_id=1, source_target_pairs={{0,8},{1,0},{2,10},{3,2},{4,12},{5,4},{6,14},{7,15},{8,9},{9,1},{1... | collective-permute-start | bytes 786440 | tf_op jit(solution)/shard_map/ppermute | solution.py:290
  5.3 9.3 %collective-permute-start.5 = (f32[256,256]{1,0:T(8,128)S(1)}, f32[256,256]{1,0:T(8,128)S(1)}, u32[]{:S(2)}, u32[]{:S(2)}) collective-permute-start(f32[256,256]{1,0:T(8,128)S(1)} %get-tuple-element.30.behind), channel_id=1, source_target_pairs={{0,8},{1,0},{2,10},{3,2},{4,12},{5,4},{6,14},{7,15},{8,9},{9,1},{1... | collective-permute-start | bytes 786440 | tf_op jit(solution)/shard_map/ppermute | solution.py:290
  7.9 9.1 %collective-permute-start.6 = (f32[256,256]{1,0:T(8,128)S(1)}, f32[256,256]{1,0:T(8,128)S(1)}, u32[]{:S(2)}, u32[]{:S(2)}) collective-permute-start(f32[256,256]{1,0:T(8,128)S(1)} %get-tuple-element.37.o0), channel_id=1, source_target_pairs={{0,2},{1,9},{2,10},{3,1},{4,12},{5,6},{6,4},{7,15},{8,0},{9,11},{1... | collective-permute-start | bytes 786440 | tf_op jit(solution)/shard_map/ppermute | solution.py:290
  9.4 12.3 %collective-permute-start.3 = (f32[256,256]{1,0:T(8,128)S(1)}, f32[256,256]{1,0:T(8,128)S(1)}, u32[]{:S(2)}, u32[]{:S(2)}) collective-permute-start(f32[256,256]{1,0:T(8,128)S(1)} %get-tuple-element.36.o1), channel_id=1, source_target_pairs={{0,2},{1,9},{2,10},{3,1},{4,12},{5,6},{6,4},{7,15},{8,0},{9,11},{1... | collective-permute-start | bytes 786440 | tf_op jit(solution)/shard_map/ppermute | solution.py:290
  14.7 9.1 %collective-permute-start.8 = (f32[256,256]{1,0:T(8,128)S(1)}, f32[256,256]{1,0:T(8,128)S(1)}, u32[]{:S(2)}, u32[]{:S(2)}) collective-permute-start(f32[256,256]{1,0:T(8,128)S(1)} %add.15.o3), channel_id=1, source_target_pairs={{0,2},{1,9},{2,10},{3,1},{4,12},{5,13},{6,14},{7,15},{8,0},{9,11},... | collective-permute-start | bytes 786440 | tf_op jit(solution)/shard_map/ppermute | solution.py:290
  14.9 10.6 %collective-permute-start.9 = (f32[256,256]{1,0:T(8,128)S(1)}, f32[256,256]{1,0:T(8,128)S(1)}, u32[]{:S(2)}, u32[]{:S(2)}) collective-permute-start(f32[256,256]{1,0:T(8,128)S(1)} %get-tuple-element.39.o2), channel_id=1, source_target_pairs={{0,2},{1,9},{2,10},{3,1},{4,12},{5,13},{6,14},{7,15},{8,0},{9,11},... | collective-permute-start | bytes 786440 | tf_op jit(solution)/shard_map/ppermute | solution.py:290
  18.6 7.0 %collective-permute-start.10 = (f32[256,256]{1,0:T(8,128)S(1)}, f32[256,256]{1,0:T(8,128)S(1)}, u32[]{:S(2)}, u32[]{:S(2)}) collective-permute-start(f32[256,256]{1,0:T(8,128)S(1)} %get-tuple-element.45), channel_id=1, source_target_pairs={{0,8},{1,9},{2,10},{3,5},{4,2},{5,13},{6,14},{7,15},{8,0},{9,1},{1... | collective-permute-start | bytes 786440 | tf_op jit(solution)/shard_map/ppermute | solution.py:290
  22.1 6.0 %collective-permute-start.7 = (f32[256,256]{1,0:T(8,128)S(1)}, f32[256,256]{1,0:T(8,128)S(1)}, u32[]{:S(2)}, u32[]{:S(2)}) collective-permute-start(f32[256,256]{1,0:T(8,128)S(1)} %shard_map.48), channel_id=1, source_target_pairs={{0,8},{1,9},{2,10},{3,5},{4,2},{5,13},{6,14},{7,15},{8,0},{9,1},{1... | collective-permute-start | bytes 786440 | tf_op jit(solution)/shard_map/ppermute | solution.py:290
  28.4 6.9 %collective-permute-start.11 = (f32[256,256]{1,0:T(8,128)S(1)}, f32[256,256]{1,0:T(8,128)S(1)}, u32[]{:S(2)}, u32[]{:S(2)}) collective-permute-start(f32[256,256]{1,0:T(8,128)S(1)} %shard_map.51), channel_id=1, source_target_pairs={{0,8},{1,3},{2,0},{3,11},{4,12},{5,13},{6,14},{7,15},{8,10},{9,1},... | collective-permute-start | bytes 786440 | tf_op jit(solution)/shard_map/ppermute | solution.py:290
  31.4 6.2 %collective-permute-start.12 = (f32[256,256]{1,0:T(8,128)S(1)}, f32[256,256]{1,0:T(8,128)S(1)}, u32[]{:S(2)}, u32[]{:S(2)}) collective-permute-start(f32[256,256]{1,0:T(8,128)S(1)} %shard_map.51), channel_id=1, source_target_pairs={{0,8},{1,9},{2,6},{3,11},{4,12},{5,13},{6,14},{7,3},{8,0},{9,1},{1... | collective-permute-start | bytes 786440 | tf_op jit(solution)/shard_map/ppermute | solution.py:290
  31.5 8.5 %collective-permute-start.13 = (f32[256,256]{1,0:T(8,128)S(1)}, f32[256,256]{1,0:T(8,128)S(1)}, u32[]{:S(2)}, u32[]{:S(2)}) collective-permute-start(f32[256,256]{1,0:T(8,128)S(1)} %shard_map.51), channel_id=1, source_target_pairs={{0,8},{1,9},{2,4},{3,11},{4,12},{5,3},{6,14},{7,15},{8,0},{9,1},{1... | collective-permute-start | bytes 786440 | tf_op jit(solution)/shard_map/ppermute | solution.py:290
  31.9 5.8 %copy-start = (f32[1,256,256]{2,1,0:T(8,128)S(1)}, f32[1,256,256]{2,1,0:T(8,128)}, u32[]{:S(2)}) copy-start(f32[1,256,256]{2,1,0:T(8,128)} %param.3) | copy-start | bytes 786436
  33.9 7.5 %collective-permute-start.16 = (f32[256,256]{1,0:T(8,128)S(1)}, f32[256,256]{1,0:T(8,128)S(1)}, u32[]{:S(2)}, u32[]{:S(2)}) collective-permute-start(f32[256,256]{1,0:T(8,128)S(1)} %shard_map.52), channel_id=1, source_target_pairs={{2,0},{11,9},{18,16},{27,25}} | collective-permute-start | bytes 786440 | tf_op jit(solution)/shard_map/ppermute | solution.py:290
  34.6 7.9 %collective-permute-start.17 = (f32[256,256]{1,0:T(8,128)S(1)}, f32[256,256]{1,0:T(8,128)S(1)}, u32[]{:S(2)}, u32[]{:S(2)}) collective-permute-start(f32[256,256]{1,0:T(8,128)S(1)} %shard_map.52), channel_id=1, source_target_pairs={{2,4},{11,13},{18,20},{27,29}} | collective-permute-start | bytes 786440 | tf_op jit(solution)/shard_map/ppermute | solution.py:290
  35.3 7.2 %collective-permute-start.18 = (f32[256,256]{1,0:T(8,128)S(1)}, f32[256,256]{1,0:T(8,128)S(1)}, u32[]{:S(2)}, u32[]{:S(2)}) collective-permute-start(f32[256,256]{1,0:T(8,128)S(1)} %shard_map.52), channel_id=1, source_target_pairs={{2,6},{11,15},{18,22},{27,31}} | collective-permute-start | bytes 786440 | tf_op jit(solution)/shard_map/ppermute | solution.py:290
  37.7 6.6 %collective-permute-start = (f32[256,256]{1,0:T(8,128)S(1)}, f32[256,256]{1,0:T(8,128)S(1)}, u32[]{:S(2)}, u32[]{:S(2)}) collective-permute-start(f32[256,256]{1,0:T(8,128)S(1)} %bitcast.4), channel_id=1, source_target_pairs={{0,8},{1,9},{2,10},{3,11},{4,12},{5,13},{6,14},{7,15},{8,0},{9,1},... | collective-permute-start | bytes 786440 | tf_op jit(solution)/shard_map/ppermute | solution.py:290
  40.1 7.1 %collective-permute-start.14 = (f32[256,256]{1,0:T(8,128)S(1)}, f32[256,256]{1,0:T(8,128)S(1)}, u32[]{:S(2)}, u32[]{:S(2)}) collective-permute-start(f32[256,256]{1,0:T(8,128)S(1)} %select_select_fusion.1.trans), channel_id=1, source_target_pairs={{0,9},{2,11},{4,13},{6,15},{9,8},{11,10},{13,12},{15,14},{16,25},{... | collective-permute-start | bytes 786440 | tf_op jit(solution)/shard_map/ppermute | solution.py:290
  41.4 5.8 %collective-permute-start.15 = (f32[256,256]{1,0:T(8,128)S(1)}, f32[256,256]{1,0:T(8,128)S(1)}, u32[]{:S(2)}, u32[]{:S(2)}) collective-permute-start(f32[256,256]{1,0:T(8,128)S(1)} %select_select_fusion.1.trans), channel_id=1, source_target_pairs={{0,8},{1,9},{2,10},{3,11},{4,12},{5,13},{6,14},{7,15},{8,0},{9,1},... | collective-permute-start | bytes 786440 | tf_op jit(solution)/shard_map/ppermute | solution.py:290
  42.5 7.8 %collective-permute-start.20 = (f32[256,256]{1,0:T(8,128)S(1)}, f32[256,256]{1,0:T(8,128)S(1)}, u32[]{:S(2)}, u32[]{:S(2)}) collective-permute-start(f32[256,256]{1,0:T(8,128)S(1)} %select_select_fusion), channel_id=1, source_target_pairs={{0,1},{1,9},{2,3},{3,11},{4,5},{5,13},{6,7},{7,15},{8,0},{9,8},{10... | collective-permute-start | bytes 786440 | tf_op jit(solution)/shard_map/ppermute | solution.py:290
  47.9 3.3 %collective-permute-start.19 = (f32[256,256]{1,0:T(8,128)S(1)}, f32[256,256]{1,0:T(8,128)S(1)}, u32[]{:S(2)}, u32[]{:S(2)}) collective-permute-start(f32[256,256]{1,0:T(8,128)S(1)} %shard_map.53), channel_id=1, source_target_pairs={{0,8},{1,9},{2,10},{3,11},{4,12},{5,13},{6,14},{7,15},{8,24},{9,25... | collective-permute-start | bytes 786440 | tf_op jit(solution)/shard_map/ppermute | solution.py:290
  51.3 3.3 %collective-permute-start.21 = (f32[256,256]{1,0:T(8,128)S(1)}, f32[256,256]{1,0:T(8,128)S(1)}, u32[]{:S(2)}, u32[]{:S(2)}) collective-permute-start(f32[256,256]{1,0:T(8,128)S(1)} %select_add_fusion.even), channel_id=1, source_target_pairs={{0,8},{1,9},{2,10},{3,11},{4,12},{5,13},{6,14},{7,15},{8,0},{9,1},... | collective-permute-start | bytes 786440 | tf_op jit(solution)/shard_map/ppermute | solution.py:290

commit v8 on v6

--- a/solution.py
+++ b/solution.py
@@ -380,10 +380,10 @@
         for k in range(pairs):
             across[line(g, k)] = (g | 1, 2 * k + 1 - g % 2)
     swap = {(g, s): (g ^ 1, s) for g in range(groups) for s in range(count)}
+    even = send(injected, swap)
     crossed = send(trans, across, False)
     trans_even = jnp.where(side == 1, crossed, send(trans, swap))
     trans_odd = jnp.where(side == 1, trans, crossed)
-    even = send(injected, swap)
     opposite = {line(g, k): (g, line(g, k)[1] ^ 1) for g in range(groups) for k in range(pairs)}
     spread_refl = jnp.where(side == parity, refl, send(refl, opposite))
     handed = jnp.zeros_like(injected)

time: 56 us -> 56 us (level)
  no operation moved by 1% of the time
where the time goes in v8:
time: 56 us; the launch traced here: 55.5 us
  starting transfers between devices  27.8 us (50%)
  Pallas kernels  14.9 us (27%)
  waiting for transfers between devices  10.6 us (19%)
  matrix products  1.01 us (2%)
  between operations  0.91 us (2%)
    ppermute x22, starting transfers between devices, send(): return lax.ppermute(block, AXES, route)  27.8 us
    pallas_call x10, Pallas kernels, call(): pl.pallas_call(body, out_shape=[square] * outs, in_specs=[vmem] * len(blo...  11.7 us
    ppermute x22, waiting for transfers between devices, send(): return lax.ppermute(block, AXES, route)  10.6 us
    pallas_call x2, Pallas kernels, picked(): pl.pallas_call(functools.partial(pick, marks, which), out_shape=[block] *...  2.11 us
  transfers between devices with their start and end apart: 22, of which 5 were waited for; matrix products, arithmetic and copies ran while one was open for 2% of the time, Pallas kernels for 23%

profile of v8, /device:TPU:25, one launch (start us, length us, event | category | flops | bytes accessed | tf_op | source)
XLA Modules:
  0.0 55.5 jit_solution(2663553613141744782)
XLA Ops:
  0.6 1.0 %shard_map.41.refl = f32[256,256]{1,0:T(8,128)S(1)} custom-call(f32[4,256,256]{2,1,0:T(8,128)} %bitcast.13), custom_call_target="tpu_custom_call" | custom-call | tf_op jit(solution)/shard_map/pallas_call | solution.py:107
  1.6 1.3 %collective-permute-start.1 = (f32[256,256]{1,0:T(8,128)S(1)}, f32[256,256]{1,0:T(8,128)S(1)}, u32[]{:S(2)}, u32[]{:S(2)}) collective-permute-start(f32[256,256]{1,0:T(8,128)S(1)} %shard_map.41.refl), channel_id=1, source_target_pairs={{0,8},{1,0},{2,10},{3,2},{4,12},{5,4},{6,7},{7,6},{8,9},{9,1},{10,... | collective-permute-start | bytes 786440 | tf_op jit(solution)/shard_map/ppermute | solution.py:270
  2.9 1.1 %shard_map.42 = (f32[256,256]{1,0:T(8,128)S(1)}, f32[256,256]{1,0:T(8,128)S(1)}, f32[256,256]{1,0:T(8,128)S(1)}) custom-call(f32[4,256,256]{2,1,0:T(8,128)} %bitcast.14), custom_call_target="tpu_custom_call" | custom-call | tf_op jit(solution)/shard_map/pallas_call | solution.py:107
  4.0 0.3 collective-permute-start.2
  4.3 1.2 %collective-permute-start.4 = (f32[256,256]{1,0:T(8,128)S(1)}, f32[256,256]{1,0:T(8,128)S(1)}, u32[]{:S(2)}, u32[]{:S(2)}) collective-permute-start(f32[256,256]{1,0:T(8,128)S(1)} %get-tuple-element.29.up), channel_id=1, source_target_pairs={{0,8},{1,0},{2,10},{3,2},{4,12},{5,4},{6,14},{7,15},{8,9},{9,1},{1... | collective-permute-start | bytes 786440 | tf_op jit(solution)/shard_map/ppermute | solution.py:270
  5.6 0.0 collective-permute-start.5
  5.6 3.3 %collective-permute-done.1.c0 = f32[256,256]{1,0:T(8,128)S(1)} collective-permute-done((f32[256,256]{1,0:T(8,128)S(1)}, f32[256,256]{1,0:T(8,128)S(1)}, u32[]{:S(2)}, u32[]{:S(2)}) %collective-permute-start.1) | collective-permute-done | bytes 262176 | tf_op jit(solution)/shard_map/ppermute | solution.py:270
  8.8 1.7 %shard_map.43 = (f32[256,256]{1,0:T(8,128)S(1)}, f32[256,256]{1,0:T(8,128)S(1)}, f32[256,256]{1,0:T(8,128)S(1)}, f32[256,256]{1,0:T(8,128)S(1)}) custom-call(f32[256,256]{1,0:T(8,128)S(1)} %shard_map.41.refl, f32[256,256]{1,0:T(8,128)S(1)} %get-tuple-element.28.trans, f32[256,256]{1,0:T(8,128)S(1)} %get-tuple-element.29.up, ...), custom_call_target="tpu_custom_call" | custom-call | tf_op jit(solution)/shard_map/pallas_call | solution.py:64
  10.5 0.1 collective-permute-start.6
  10.6 0.7 %shard_map.44 = (f32[256,256]{1,0:T(8,128)S(1)}, f32[256,256]{1,0:T(8,128)S(1)}) custom-call(f32[256,256]{1,0:T(8,128)S(1)} %get-tuple-element.28.trans, f32[256,256]{1,0:T(8,128)S(1)} %get-tuple-element.29.up, f32[256,256]{1,0:T(8,128)S(1)} %get-tuple-element.30.behind, f32[256,256]{1,0:T(8,128)S(1)} %get-tuple-element.32.solver, ...), custom_call_target="tpu_custom_call" | custom-call | tf_op jit(solution)/shard_map/pallas_call | solution.py:64
  11.3 3.2 %collective-permute-done.2.c1 = f32[256,256]{1,0:T(8,128)S(1)} collective-permute-done((f32[256,256]{1,0:T(8,128)S(1)}, f32[256,256]{1,0:T(8,128)S(1)}, u32[]{:S(2)}, u32[]{:S(2)}) %collective-permute-start.2) | collective-permute-done | bytes 262176 | tf_op jit(solution)/shard_map/ppermute | solution.py:270
  14.5 0.4 shard_map.45
  14.9 0.1 collective-permute-start.3
  15.0 0.0 collective-permute-done.4.c2
  15.0 0.4 shard_map.46
  15.4 0.0 collective-permute-done.5
  15.5 1.6 %collective-permute-start.8 = (f32[256,256]{1,0:T(8,128)S(1)}, f32[256,256]{1,0:T(8,128)S(1)}, u32[]{:S(2)}, u32[]{:S(2)}) collective-permute-start(f32[256,256]{1,0:T(8,128)S(1)} %add.22.o3), channel_id=1, source_target_pairs={{0,2},{1,9},{2,10},{3,1},{4,12},{5,13},{6,14},{7,15},{8,0},{9,11},... | collective-permute-start | bytes 786440 | tf_op jit(solution)/shard_map/ppermute | solution.py:270
  17.1 0.1 collective-permute-start.9
  17.1 0.0 collective-permute-done.6.refl_b.c0
  17.1 1.7 %shard_map.47 = (f32[256,256]{1,0:T(8,128)S(1)}, f32[256,256]{1,0:T(8,128)S(1)}) custom-call(f32[256,256]{1,0:T(8,128)S(1)} %get-tuple-element.37.o0, f32[256,256]{1,0:T(8,128)S(1)} %get-tuple-element.36.o1, f32[256,256]{1,0:T(8,128)S(1)} %get-tuple-element.39.o2, f32[256,256]{1,0:T(8,128)S(1)} %add.22.o3, f32[256,256]{1,0:T(8,128)S(1)} %collective-permute-done.6.refl_b.c0), custom_call_target="tpu_custom_call" | custom-call | tf_op jit(solution)/shard_map/pallas_call | solution.py:64
  18.8 3.5 %collective-permute-start.10 = (f32[256,256]{1,0:T(8,128)S(1)}, f32[256,256]{1,0:T(8,128)S(1)}, u32[]{:S(2)}, u32[]{:S(2)}) collective-permute-start(f32[256,256]{1,0:T(8,128)S(1)} %get-tuple-element.45), channel_id=1, source_target_pairs={{0,8},{1,9},{2,10},{3,5},{4,2},{5,13},{6,14},{7,15},{8,0},{9,1},{1... | collective-permute-start | bytes 786440 | tf_op jit(solution)/shard_map/ppermute | solution.py:270
  22.3 0.0 collective-permute-done.3.left.c1
  22.3 0.3 shard_map.48
  22.5 1.6 %collective-permute-start.7 = (f32[256,256]{1,0:T(8,128)S(1)}, f32[256,256]{1,0:T(8,128)S(1)}, u32[]{:S(2)}, u32[]{:S(2)}) collective-permute-start(f32[256,256]{1,0:T(8,128)S(1)} %shard_map.48), channel_id=1, source_target_pairs={{0,8},{1,9},{2,10},{3,5},{4,2},{5,13},{6,14},{7,15},{8,0},{9,1},{1... | collective-permute-start | bytes 786440 | tf_op jit(solution)/shard_map/ppermute | solution.py:270
  24.1 0.0 collective-permute-done.8.c3
  24.1 1.8 %shard_map.49 = (f32[256,256]{1,0:T(8,128)S(1)}, f32[256,256]{1,0:T(8,128)S(1)}, f32[256,256]{1,0:T(8,128)S(1)}) custom-call(f32[256,256]{1,0:T(8,128)S(1)} %get-tuple-element.37.o0, f32[256,256]{1,0:T(8,128)S(1)} %get-tuple-element.36.o1, f32[256,256]{1,0:T(8,128)S(1)} %get-tuple-element.39.o2, f32[256,256]{1,0:T(8,128)S(1)} %add.22.o3, ...), custom_call_target="tpu_custom_call" | custom-call | tf_op jit(solution)/shard_map/pallas_call | solution.py:64
  25.9 0.0 collective-permute-done.9.c2
  25.9 0.0 collective-permute-done.10.refl_b.low_refl
  25.9 2.5 %shard_map.50.right.down = f32[256,256]{1,0:T(8,128)S(1)} custom-call(f32[256,256]{1,0:T(8,128)S(1)} %get-tuple-element.43.back_a, f32[256,256]{1,0:T(8,128)S(1)} %get-tuple-element.44.trans_a, f32[256,256]{1,0:T(8,128)S(1)} %collective-permute-done.10.refl_b.low_refl), custom_call_target="tpu_custom_call" | custom-call | tf_op jit(solution)/shard_map/pallas_call | solution.py:64
  28.4 0.0 collective-permute-done.7.left
  28.5 0.3 shard_map.51
  28.7 0.1 collective-permute-start.11
  28.8 2.7 %collective-permute-start.12 = (f32[256,256]{1,0:T(8,128)S(1)}, f32[256,256]{1,0:T(8,128)S(1)}, u32[]{:S(2)}, u32[]{:S(2)}) collective-permute-start(f32[256,256]{1,0:T(8,128)S(1)} %shard_map.51), channel_id=1, source_target_pairs={{0,8},{1,9},{2,6},{3,11},{4,12},{5,13},{6,14},{7,3},{8,0},{9,1},{1... | collective-permute-start | bytes 786440 | tf_op jit(solution)/shard_map/ppermute | solution.py:270
  31.5 0.0 collective-permute-start.13
  31.5 0.0 copy-start
  31.5 2.0 %shard_map.52 = f32[256,256]{1,0:T(8,128)S(1)} custom-call(f32[256,256]{1,0:T(8,128)S(1)} %get-tuple-element.37.o0, f32[256,256]{1,0:T(8,128)S(1)} %get-tuple-element.39.o2, f32[256,256]{1,0:T(8,128)S(1)} %add.22.o3, f32[256,256]{1,0:T(8,128)S(1)} %collective-permute-done.6.refl_b.c0, f32[256,256]{1,0:T(8,128)S(1)} %collective-permute-done.3.left.c1, ...), custom_call_target="tpu_custom_call" | custom-call | tf_op jit(solution)/shard_map/pallas_call | solution.py:64
  33.5 0.7 %collective-permute-start.16 = (f32[256,256]{1,0:T(8,128)S(1)}, f32[256,256]{1,0:T(8,128)S(1)}, u32[]{:S(2)}, u32[]{:S(2)}) collective-permute-start(f32[256,256]{1,0:T(8,128)S(1)} %shard_map.52), channel_id=1, source_target_pairs={{2,0},{11,9},{18,16},{27,25}} | collective-permute-start | bytes 786440 | tf_op jit(solution)/shard_map/ppermute | solution.py:270
  34.2 0.0 copy-done
  34.2 0.6 %collective-permute-start = (f32[256,256]{1,0:T(8,128)S(1)}, f32[256,256]{1,0:T(8,128)S(1)}, u32[]{:S(2)}, u32[]{:S(2)}) collective-permute-start(f32[256,256]{1,0:T(8,128)S(1)} %bitcast.15), channel_id=1, source_target_pairs={{0,8},{1,9},{2,10},{3,11},{4,12},{5,13},{6,14},{7,15},{8,0},{9,1},... | collective-permute-start | bytes 786440 | tf_op jit(solution)/shard_map/ppermute | solution.py:270
  34.8 0.0 collective-permute-done.11
  34.8 0.7 %collective-permute-start.17 = (f32[256,256]{1,0:T(8,128)S(1)}, f32[256,256]{1,0:T(8,128)S(1)}, u32[]{:S(2)}, u32[]{:S(2)}) collective-permute-start(f32[256,256]{1,0:T(8,128)S(1)} %shard_map.52), channel_id=1, source_target_pairs={{2,4},{11,13},{18,20},{27,29}} | collective-permute-start | bytes 786440 | tf_op jit(solution)/shard_map/ppermute | solution.py:270
  35.5 0.0 collective-permute-done.12
  35.5 0.7 %collective-permute-start.18 = (f32[256,256]{1,0:T(8,128)S(1)}, f32[256,256]{1,0:T(8,128)S(1)}, u32[]{:S(2)}, u32[]{:S(2)}) collective-permute-start(f32[256,256]{1,0:T(8,128)S(1)} %shard_map.52), channel_id=1, source_target_pairs={{2,6},{11,15},{18,22},{27,31}} | collective-permute-start | bytes 786440 | tf_op jit(solution)/shard_map/ppermute | solution.py:270
  36.2 0.0 collective-permute-done.13
  36.2 0.1 select_select_fusion.1
  36.3 1.3 %collective-permute-start.14 = (f32[256,256]{1,0:T(8,128)S(1)}, f32[256,256]{1,0:T(8,128)S(1)}, u32[]{:S(2)}, u32[]{:S(2)}) collective-permute-start(f32[256,256]{1,0:T(8,128)S(1)} %select_select_fusion.1), channel_id=1, source_target_pairs={{0,9},{2,11},{4,13},{6,15},{9,8},{11,10},{13,12},{15,14},{16,25},{... | collective-permute-start | bytes 786440 | tf_op jit(solution)/shard_map/ppermute | solution.py:270
  37.6 0.0 collective-permute-done.16
  37.6 1.8 %collective-permute-start.15 = (f32[256,256]{1,0:T(8,128)S(1)}, f32[256,256]{1,0:T(8,128)S(1)}, u32[]{:S(2)}, u32[]{:S(2)}) collective-permute-start(f32[256,256]{1,0:T(8,128)S(1)} %select_select_fusion.1), channel_id=1, source_target_pairs={{0,8},{1,9},{2,10},{3,11},{4,12},{5,13},{6,14},{7,15},{8,0},{9,1},... | collective-permute-start | bytes 786440 | tf_op jit(solution)/shard_map/ppermute | solution.py:270
  39.3 0.0 collective-permute-done.17
  39.3 0.0 collective-permute-done.18
  39.3 0.1 select_select_fusion
  39.4 6.6 %collective-permute-start.20 = (f32[256,256]{1,0:T(8,128)S(1)}, f32[256,256]{1,0:T(8,128)S(1)}, u32[]{:S(2)}, u32[]{:S(2)}) collective-permute-start(f32[256,256]{1,0:T(8,128)S(1)} %select_select_fusion), channel_id=1, source_target_pairs={{0,1},{1,9},{2,3},{3,11},{4,5},{5,13},{6,7},{7,15},{8,0},{9,8},{10... | collective-permute-start | bytes 786440 | tf_op jit(solution)/shard_map/ppermute | solution.py:270
  46.0 0.0 collective-permute-done
  46.0 0.0 collective-permute-done.14
  46.0 0.0 collective-permute-done.15
  46.0 0.3 fusion
  46.4 0.3 fusion.1
  46.7 1.3 %collective-permute-start.19 = (f32[256,256]{1,0:T(8,128)S(1)}, f32[256,256]{1,0:T(8,128)S(1)}, u32[]{:S(2)}, u32[]{:S(2)}) collective-permute-start(f32[256,256]{1,0:T(8,128)S(1)} %fusion.1), channel_id=1, source_target_pairs={{0,8},{1,9},{2,10},{3,11},{4,12},{5,13},{6,14},{7,15},{8,24},{9,25... | collective-permute-start | bytes 786440 | tf_op jit(solution)/shard_map/ppermute | solution.py:270
  48.0 1.1 %collective-permute-done.20 = f32[256,256]{1,0:T(8,128)S(1)} collective-permute-done((f32[256,256]{1,0:T(8,128)S(1)}, f32[256,256]{1,0:T(8,128)S(1)}, u32[]{:S(2)}, u32[]{:S(2)}) %collective-permute-start.20) | collective-permute-done | bytes 262176 | tf_op jit(solution)/shard_map/ppermute | solution.py:270
  49.1 2.1 %collective-permute-done.19 = f32[256,256]{1,0:T(8,128)S(1)} collective-permute-done((f32[256,256]{1,0:T(8,128)S(1)}, f32[256,256]{1,0:T(8,128)S(1)}, u32[]{:S(2)}, u32[]{:S(2)}) %collective-permute-start.19) | collective-permute-done | bytes 262176 | tf_op jit(solution)/shard_map/ppermute | solution.py:270
  51.3 1.9 %collective-permute-start.21 = (f32[256,256]{1,0:T(8,128)S(1)}, f32[256,256]{1,0:T(8,128)S(1)}, u32[]{:S(2)}, u32[]{:S(2)}) collective-permute-start(f32[256,256]{1,0:T(8,128)S(1)} %select_add_fusion), channel_id=1, source_target_pairs={{0,8},{1,9},{2,10},{3,11},{4,12},{5,13},{6,14},{7,15},{8,0},{9,1},... | collective-permute-start | bytes 786440 | tf_op jit(solution)/shard_map/ppermute | solution.py:270
  53.2 0.3 convolution_add_fusion.odd
  53.6 0.8 %collective-permute-done.21.even = f32[256,256]{1,0:T(8,128)S(1)} collective-permute-done((f32[256,256]{1,0:T(8,128)S(1)}, f32[256,256]{1,0:T(8,128)S(1)}, u32[]{:S(2)}, u32[]{:S(2)}) %collective-permute-start.21) | collective-permute-done | bytes 262176 | tf_op jit(solution)/shard_map/ppermute | solution.py:270
  54.4 1.1 %shard_map.53 = (f32[256,256]{1,0:T(8,128)}, f32[256,256]{1,0:T(8,128)}) custom-call(f32[256,256]{1,0:T(8,128)S(1)} %convolution_add_fusion.odd, f32[256,256]{1,0:T(8,128)S(1)} %collective-permute-done.21.even, f32[256,256]{1,0:T(8,128)S(1)} %broadcast_select_fusion.refl), custom_call_target="tpu_custom_call" | custom-call | tf_op jit(solution)/shard_map/pallas_call | solution.py:231
  (3 shorter events, 0.1 us)
Async XLA Ops:
  1.6 7.2 %collective-permute-start.1 = (f32[256,256]{1,0:T(8,128)S(1)}, f32[256,256]{1,0:T(8,128)S(1)}, u32[]{:S(2)}, u32[]{:S(2)}) collective-permute-start(f32[256,256]{1,0:T(8,128)S(1)} %shard_map.41.refl), channel_id=1, source_target_pairs={{0,8},{1,0},{2,10},{3,2},{4,12},{5,4},{6,7},{7,6},{8,9},{9,1},{10,... | collective-permute-start | bytes 786440 | tf_op jit(solution)/shard_map/ppermute | solution.py:270
  4.0 10.4 %collective-permute-start.2 = (f32[256,256]{1,0:T(8,128)S(1)}, f32[256,256]{1,0:T(8,128)S(1)}, u32[]{:S(2)}, u32[]{:S(2)}) collective-permute-start(f32[256,256]{1,0:T(8,128)S(1)} %get-tuple-element.28.trans), channel_id=1, source_target_pairs={{0,8},{1,0},{2,10},{3,2},{4,12},{5,4},{6,7},{7,6},{8,9},{9,1},{10,... | collective-permute-start | bytes 786440 | tf_op jit(solution)/shard_map/ppermute | solution.py:270
  4.3 10.6 %collective-permute-start.4 = (f32[256,256]{1,0:T(8,128)S(1)}, f32[256,256]{1,0:T(8,128)S(1)}, u32[]{:S(2)}, u32[]{:S(2)}) collective-permute-start(f32[256,256]{1,0:T(8,128)S(1)} %get-tuple-element.29.up), channel_id=1, source_target_pairs={{0,8},{1,0},{2,10},{3,2},{4,12},{5,4},{6,14},{7,15},{8,9},{9,1},{1... | collective-permute-start | bytes 786440 | tf_op jit(solution)/shard_map/ppermute | solution.py:270
  5.6 9.9 %collective-permute-start.5 = (f32[256,256]{1,0:T(8,128)S(1)}, f32[256,256]{1,0:T(8,128)S(1)}, u32[]{:S(2)}, u32[]{:S(2)}) collective-permute-start(f32[256,256]{1,0:T(8,128)S(1)} %get-tuple-element.30.behind), channel_id=1, source_target_pairs={{0,8},{1,0},{2,10},{3,2},{4,12},{5,4},{6,14},{7,15},{8,9},{9,1},{1... | collective-permute-start | bytes 786440 | tf_op jit(solution)/shard_map/ppermute | solution.py:270
  10.5 6.6 %collective-permute-start.6 = (f32[256,256]{1,0:T(8,128)S(1)}, f32[256,256]{1,0:T(8,128)S(1)}, u32[]{:S(2)}, u32[]{:S(2)}) collective-permute-start(f32[256,256]{1,0:T(8,128)S(1)} %get-tuple-element.37.o0), channel_id=1, source_target_pairs={{0,2},{1,9},{2,10},{3,1},{4,12},{5,6},{6,4},{7,15},{8,0},{9,11},{1... | collective-permute-start | bytes 786440 | tf_op jit(solution)/shard_map/ppermute | solution.py:270
  14.9 7.4 %collective-permute-start.3 = (f32[256,256]{1,0:T(8,128)S(1)}, f32[256,256]{1,0:T(8,128)S(1)}, u32[]{:S(2)}, u32[]{:S(2)}) collective-permute-start(f32[256,256]{1,0:T(8,128)S(1)} %get-tuple-element.36.o1), channel_id=1, source_target_pairs={{0,2},{1,9},{2,10},{3,1},{4,12},{5,6},{6,4},{7,15},{8,0},{9,11},{1... | collective-permute-start | bytes 786440 | tf_op jit(solution)/shard_map/ppermute | solution.py:270
  15.5 8.6 %collective-permute-start.8 = (f32[256,256]{1,0:T(8,128)S(1)}, f32[256,256]{1,0:T(8,128)S(1)}, u32[]{:S(2)}, u32[]{:S(2)}) collective-permute-start(f32[256,256]{1,0:T(8,128)S(1)} %add.22.o3), channel_id=1, source_target_pairs={{0,2},{1,9},{2,10},{3,1},{4,12},{5,13},{6,14},{7,15},{8,0},{9,11},... | collective-permute-start | bytes 786440 | tf_op jit(solution)/shard_map/ppermute | solution.py:270
  17.1 8.8 %collective-permute-start.9 = (f32[256,256]{1,0:T(8,128)S(1)}, f32[256,256]{1,0:T(8,128)S(1)}, u32[]{:S(2)}, u32[]{:S(2)}) collective-permute-start(f32[256,256]{1,0:T(8,128)S(1)} %get-tuple-element.39.o2), channel_id=1, source_target_pairs={{0,2},{1,9},{2,10},{3,1},{4,12},{5,13},{6,14},{7,15},{8,0},{9,11},... | collective-permute-start | bytes 786440 | tf_op jit(solution)/shard_map/ppermute | solution.py:270
  18.8 7.1 %collective-permute-start.10 = (f32[256,256]{1,0:T(8,128)S(1)}, f32[256,256]{1,0:T(8,128)S(1)}, u32[]{:S(2)}, u32[]{:S(2)}) collective-permute-start(f32[256,256]{1,0:T(8,128)S(1)} %get-tuple-element.45), channel_id=1, source_target_pairs={{0,8},{1,9},{2,10},{3,5},{4,2},{5,13},{6,14},{7,15},{8,0},{9,1},{1... | collective-permute-start | bytes 786440 | tf_op jit(solution)/shard_map/ppermute | solution.py:270
  22.5 5.9 %collective-permute-start.7 = (f32[256,256]{1,0:T(8,128)S(1)}, f32[256,256]{1,0:T(8,128)S(1)}, u32[]{:S(2)}, u32[]{:S(2)}) collective-permute-start(f32[256,256]{1,0:T(8,128)S(1)} %shard_map.48), channel_id=1, source_target_pairs={{0,8},{1,9},{2,10},{3,5},{4,2},{5,13},{6,14},{7,15},{8,0},{9,1},{1... | collective-permute-start | bytes 786440 | tf_op jit(solution)/shard_map/ppermute | solution.py:270
  28.7 6.1 %collective-permute-start.11 = (f32[256,256]{1,0:T(8,128)S(1)}, f32[256,256]{1,0:T(8,128)S(1)}, u32[]{:S(2)}, u32[]{:S(2)}) collective-permute-start(f32[256,256]{1,0:T(8,128)S(1)} %shard_map.51), channel_id=1, source_target_pairs={{0,8},{1,3},{2,0},{3,11},{4,12},{5,13},{6,14},{7,15},{8,10},{9,1},... | collective-permute-start | bytes 786440 | tf_op jit(solution)/shard_map/ppermute | solution.py:270
  28.8 6.7 %collective-permute-start.12 = (f32[256,256]{1,0:T(8,128)S(1)}, f32[256,256]{1,0:T(8,128)S(1)}, u32[]{:S(2)}, u32[]{:S(2)}) collective-permute-start(f32[256,256]{1,0:T(8,128)S(1)} %shard_map.51), channel_id=1, source_target_pairs={{0,8},{1,9},{2,6},{3,11},{4,12},{5,13},{6,14},{7,3},{8,0},{9,1},{1... | collective-permute-start | bytes 786440 | tf_op jit(solution)/shard_map/ppermute | solution.py:270
  31.5 4.7 %collective-permute-start.13 = (f32[256,256]{1,0:T(8,128)S(1)}, f32[256,256]{1,0:T(8,128)S(1)}, u32[]{:S(2)}, u32[]{:S(2)}) collective-permute-start(f32[256,256]{1,0:T(8,128)S(1)} %shard_map.51), channel_id=1, source_target_pairs={{0,8},{1,9},{2,4},{3,11},{4,12},{5,3},{6,14},{7,15},{8,0},{9,1},{1... | collective-permute-start | bytes 786440 | tf_op jit(solution)/shard_map/ppermute | solution.py:270
  31.5 2.7 %copy-start = (f32[1,256,256]{2,1,0:T(8,128)S(1)}, f32[1,256,256]{2,1,0:T(8,128)}, u32[]{:S(2)}) copy-start(f32[1,256,256]{2,1,0:T(8,128)} %param.3) | copy-start | bytes 786436
  33.5 4.0 %collective-permute-start.16 = (f32[256,256]{1,0:T(8,128)S(1)}, f32[256,256]{1,0:T(8,128)S(1)}, u32[]{:S(2)}, u32[]{:S(2)}) collective-permute-start(f32[256,256]{1,0:T(8,128)S(1)} %shard_map.52), channel_id=1, source_target_pairs={{2,0},{11,9},{18,16},{27,25}} | collective-permute-start | bytes 786440 | tf_op jit(solution)/shard_map/ppermute | solution.py:270
  34.2 11.8 %collective-permute-start = (f32[256,256]{1,0:T(8,128)S(1)}, f32[256,256]{1,0:T(8,128)S(1)}, u32[]{:S(2)}, u32[]{:S(2)}) collective-permute-start(f32[256,256]{1,0:T(8,128)S(1)} %bitcast.15), channel_id=1, source_target_pairs={{0,8},{1,9},{2,10},{3,11},{4,12},{5,13},{6,14},{7,15},{8,0},{9,1},... | collective-permute-start | bytes 786440 | tf_op jit(solution)/shard_map/ppermute | solution.py:270
  34.8 4.5 %collective-permute-start.17 = (f32[256,256]{1,0:T(8,128)S(1)}, f32[256,256]{1,0:T(8,128)S(1)}, u32[]{:S(2)}, u32[]{:S(2)}) collective-permute-start(f32[256,256]{1,0:T(8,128)S(1)} %shard_map.52), channel_id=1, source_target_pairs={{2,4},{11,13},{18,20},{27,29}} | collective-permute-start | bytes 786440 | tf_op jit(solution)/shard_map/ppermute | solution.py:270
  35.5 3.9 %collective-permute-start.18 = (f32[256,256]{1,0:T(8,128)S(1)}, f32[256,256]{1,0:T(8,128)S(1)}, u32[]{:S(2)}, u32[]{:S(2)}) collective-permute-start(f32[256,256]{1,0:T(8,128)S(1)} %shard_map.52), channel_id=1, source_target_pairs={{2,6},{11,15},{18,22},{27,31}} | collective-permute-start | bytes 786440 | tf_op jit(solution)/shard_map/ppermute | solution.py:270
  36.3 9.8 %collective-permute-start.14 = (f32[256,256]{1,0:T(8,128)S(1)}, f32[256,256]{1,0:T(8,128)S(1)}, u32[]{:S(2)}, u32[]{:S(2)}) collective-permute-start(f32[256,256]{1,0:T(8,128)S(1)} %select_select_fusion.1), channel_id=1, source_target_pairs={{0,9},{2,11},{4,13},{6,15},{9,8},{11,10},{13,12},{15,14},{16,25},{... | collective-permute-start | bytes 786440 | tf_op jit(solution)/shard_map/ppermute | solution.py:270
  37.6 8.5 %collective-permute-start.15 = (f32[256,256]{1,0:T(8,128)S(1)}, f32[256,256]{1,0:T(8,128)S(1)}, u32[]{:S(2)}, u32[]{:S(2)}) collective-permute-start(f32[256,256]{1,0:T(8,128)S(1)} %select_select_fusion.1), channel_id=1, source_target_pairs={{0,8},{1,9},{2,10},{3,11},{4,12},{5,13},{6,14},{7,15},{8,0},{9,1},... | collective-permute-start | bytes 786440 | tf_op jit(solution)/shard_map/ppermute | solution.py:270
  39.4 9.7 %collective-permute-start.20 = (f32[256,256]{1,0:T(8,128)S(1)}, f32[256,256]{1,0:T(8,128)S(1)}, u32[]{:S(2)}, u32[]{:S(2)}) collective-permute-start(f32[256,256]{1,0:T(8,128)S(1)} %select_select_fusion), channel_id=1, source_target_pairs={{0,1},{1,9},{2,3},{3,11},{4,5},{5,13},{6,7},{7,15},{8,0},{9,8},{10... | collective-permute-start | bytes 786440 | tf_op jit(solution)/shard_map/ppermute | solution.py:270
  46.7 4.6 %collective-permute-start.19 = (f32[256,256]{1,0:T(8,128)S(1)}, f32[256,256]{1,0:T(8,128)S(1)}, u32[]{:S(2)}, u32[]{:S(2)}) collective-permute-start(f32[256,256]{1,0:T(8,128)S(1)} %fusion.1), channel_id=1, source_target_pairs={{0,8},{1,9},{2,10},{3,11},{4,12},{5,13},{6,14},{7,15},{8,24},{9,25... | collective-permute-start | bytes 786440 | tf_op jit(solution)/shard_map/ppermute | solution.py:270
  51.3 3.1 %collective-permute-start.21 = (f32[256,256]{1,0:T(8,128)S(1)}, f32[256,256]{1,0:T(8,128)S(1)}, u32[]{:S(2)}, u32[]{:S(2)}) collective-permute-start(f32[256,256]{1,0:T(8,128)S(1)} %select_add_fusion), channel_id=1, source_target_pairs={{0,8},{1,9},{2,10},{3,11},{4,12},{5,13},{6,14},{7,15},{8,0},{9,1},... | collective-permute-start | bytes 786440 | tf_op jit(solution)/shard_map/ppermute | solution.py:270
